TPU v7x, 32 devices: a whole 2x2x4 slice. The times are simulated.
32 devices in a mesh: dp: 16 (over z, y, core), mp: 2 (over x).
Axes of the slice: x: 2, y: 2, z: 4, core: 2. Of those that a mesh axis runs over, the one named last changes fastest.
Arguments:
- tokens: bfloat16 [40960, 1024], P(('dp', 'mp')), may hold values from -6 to 6
- cotangent: bfloat16 [40960, 1024], P(('dp', 'mp')), may hold values from -6 to 6
- group_start: int32 [16], P('dp'), may hold values from 0 to 1, as said below
- band_index: int32 [16], P('dp'), may hold values from 0 to 15, as said below
- class_label: int32 [16], P('dp'), may hold values from 0 to 100
- time_table: float32 [16, 1024], replicated, may hold values from -1.5 to 1.5
- class_table: float32 [101, 1024], replicated, may hold values from -1.5 to 1.5
- modulation_weight: bfloat16 [2, 1024, 6, 1024], P(None, None, None, 'mp'), may hold values from -0.1875 to 0.1875
- modulation_bias: float32 [2, 6, 1024], P(None, None, 'mp'), may hold values from -0.8 to 0.8
- input_weight: bfloat16 [2, 1024, 3, 1024], P(None, None, None, 'mp'), may hold values from -0.1875 to 0.1875
- output_weight: bfloat16 [2, 1024, 1024], P(None, 'mp'), may hold values from -0.5 to 0.5
- space_offsets: float32 [16, 62], P('mp'), may hold values from -0.8 to 0.8
- time_offsets: float32 [16, 39], P('mp'), may hold values from -0.8 to 0.8
- up_weight: bfloat16 [2, 1024, 4096], P(None, None, 'mp'), may hold values from -0.1875 to 0.1875
- up_bias: float32 [2, 4096], P(None, 'mp'), may hold values from -0.8 to 0.8
- down_weight: bfloat16 [2, 4096, 1024], P(None, 'mp'), may hold values from -0.09375 to 0.09375
Outputs:
- result: float32 [40960, 1024], P(('dp', 'mp'))
- grad_tokens: float32 [40960, 1024], P(('dp', 'mp'))
- grad_modulation_weight: float32 [2, 1024, 6, 1024], P(None, None, None, 'mp')
- grad_modulation_bias: float32 [2, 6, 1024], P(None, None, 'mp')
- grad_input_weight: float32 [2, 1024, 3, 1024], P(None, None, None, 'mp')
- grad_output_weight: float32 [2, 1024, 1024], P(None, 'mp')
- grad_space_offsets: float32 [16, 62], P('mp')
- grad_time_offsets: float32 [16, 39], P('mp')
- grad_up_weight: float32 [2, 1024, 4096], P(None, None, 'mp')
- grad_up_bias: float32 [2, 4096], P(None, 'mp')
- grad_down_weight: float32 [2, 4096, 1024], P(None, 'mp')
Inputs may be any that keep to these rules, and one draw needn't show every extreme that they name: `group_start`: 1 marks the first video of a group, 0 the others; a group runs up to the next 1. `band_index`: read only where group_start is 1.
All inputs are finite; a program needn't handle non-finite values.
Results may differ from a plain program's by a relative error of at most 0.04.
The roundings to bfloat16 on the way count: a program that leaves them out, or rounds other values in their place, can miss the bound.
Values may be sent and summed in bfloat16 or wider, within the bound.
A program may use at most 512 MiB of HBM per device.

v0:
```python
import jax
import jax.numpy as jnp
from jax import lax
from jax.sharding import PartitionSpec as P

FRAMES = 5
HEIGHT = 16
WIDTH = 32


HIGH = lax.Precision.HIGHEST
EPSILON = 1e-06
CONTRACT_LAST = (((1,), (1,)), ((), ()))
CONTRACT_FIRST = (((0,), (0,)), ((), ()))


def carried_in(value, axis, join, neutral):
    count, mine = (lax.axis_size(axis), lax.axis_index(axis))
    pieces = lax.all_gather(value, axis)
    total = jnp.full_like(value, 0) + jnp.asarray(neutral, value.dtype)

    def lap(position, total):
        longer = join(total, pieces[position])
        return jnp.where(position < mine, longer, total)

    return lax.fori_loop(0, count - 1, lap, total)


def as_sent(shard):
    return jax.tree.map(lambda a: a.astype(jnp.bfloat16) if a.dtype == jnp.float32 else a, shard)


def normalize(values):
    centred = values - jnp.mean(values, axis=-1, keepdims=True)
    spread = jnp.mean(centred * centred, axis=-1, keepdims=True)
    return centred * lax.rsqrt(spread + EPSILON)


def modulate(values, shift, scale):
    return normalize(values) * (1.0 + scale) + shift


def window_shape(layer):
    if layer == 0:
        return (1, 16, 16)
    return (FRAMES, 8, 8)


def to_windows(values, layer):
    chans = values.shape[-1]
    if layer == 0:
        grid = values.reshape(FRAMES, HEIGHT // 16, 16, WIDTH // 16, 16, chans)
        return grid.transpose(0, 1, 3, 2, 4, 5).reshape(-1, 256, chans)
    grid = values.reshape(FRAMES, HEIGHT // 8, 8, WIDTH // 8, 8, chans)
    return grid.transpose(1, 3, 0, 2, 4, 5).reshape(-1, FRAMES * 64, chans)


def from_windows(values, layer):
    chans = values.shape[-1]
    if layer == 0:
        grid = values.reshape(FRAMES, HEIGHT // 16, WIDTH // 16, 16, 16, chans)
        return grid.transpose(0, 1, 3, 2, 4, 5).reshape(-1, chans)
    grid = values.reshape(HEIGHT // 8, WIDTH // 8, FRAMES, 8, 8, chans)
    return grid.transpose(2, 0, 3, 1, 4, 5).reshape(-1, chans)


def offset_map(layer):
    extents = window_shape(layer)
    count = extents[0] * extents[1] * extents[2]
    place = jnp.arange(count, dtype=jnp.int32)
    positions = (
        place // (extents[1] * extents[2]),
        place // extents[2] % extents[1],
        place % extents[2],
    )
    columns = []
    for position, extent in zip(positions, extents):
        if extent > 1:
            offset = (position[:, None] - position[None, :] + extent - 1).reshape(-1)
            levels = jnp.arange(2 * extent - 1, dtype=jnp.int32)
            columns.append((offset[:, None] == levels[None, :]).astype(jnp.float32))
    return jnp.concatenate(columns, axis=1)


def window_scores(projected, offsets, onehot, layer):
    windows = to_windows(projected, layer)
    count = windows.shape[1]
    heads = offsets.shape[0]
    split = windows.reshape(windows.shape[0], count, 3, heads, -1)
    queries = split[:, :, 0]
    keys = split[:, :, 1]
    values = split[:, :, 2]
    factor = split.shape[-1] ** (-0.5)
    bias = jnp.dot(offsets, onehot.T, precision=HIGH).reshape(heads, count, count)
    scores = (
        jnp.einsum("nqhe,nkhe->nhqk", queries, keys, preferred_element_type=jnp.float32) * factor
        + bias
    )
    return (queries, keys, values, scores, factor)


def gather_rows(values):
    return lax.all_gather(values, "mp", axis=0, tiled=True)


def gather_grads(values):
    return lax.all_gather(values, "mp", axis=0, tiled=True)


def scatter_rows(source, weight, count):

    def term(start, size):
        return jnp.dot(source, weight, preferred_element_type=jnp.float32)

    return lax.psum_scatter(
        term(jnp.int32(0), count * lax.axis_size("mp")), "mp", scatter_dimension=0, tiled=True
    )


def scatter_back(source, weight, count):

    def term(start, size):
        return lax.dot_general(source, weight, CONTRACT_LAST, preferred_element_type=jnp.float32)

    return lax.psum_scatter(
        term(jnp.int32(0), count * lax.axis_size("mp")).astype(jnp.bfloat16),
        "mp",
        scatter_dimension=0,
        tiled=True,
    ).astype(jnp.float32)


def per_device(
    tokens,
    cotangent,
    group_start,
    band_index,
    class_label,
    time_table,
    class_table,
    modulation_weight,
    modulation_bias,
    input_weight,
    output_weight,
    space_offsets,
    time_offsets,
    up_weight,
    up_bias,
    down_weight,
):
    local_rows = tokens.shape[0]
    marked = jnp.where(group_start > 0, band_index, -1)

    def latest(earlier, later):
        return jnp.where(later >= 0, later, earlier)

    before = carried_in(marked, "dp", latest, jnp.full_like(marked, -1))
    current = jnp.where(group_start > 0, band_index, before)
    band_hot = (
        current[:, None] == jnp.arange(time_table.shape[0], dtype=jnp.int32)[None, :]
    ).astype(jnp.float32)
    class_hot = (
        class_label[:, None] == jnp.arange(class_table.shape[0], dtype=jnp.int32)[None, :]
    ).astype(jnp.float32)
    condition = jnp.dot(band_hot, time_table, precision=HIGH) + jnp.dot(
        class_hot, class_table, precision=HIGH
    )
    activated = jax.nn.silu(condition[0]).astype(jnp.bfloat16)
    local_modulation = (
        jnp.einsum("d,ldcf->lcf", activated, modulation_weight, preferred_element_type=jnp.float32)
        + modulation_bias
    )
    modulation = lax.all_gather(local_modulation, "mp", axis=2, tiled=True)
    tables = (space_offsets, time_offsets)
    width = input_weight.shape[1]
    residual = tokens.astype(jnp.float32)
    saved = []
    for layer in range(2):
        shift_one, scale_one, gate_one, shift_two, scale_two, gate_two = [
            modulation[layer, number] for number in range(6)
        ]
        onehot = offset_map(layer)
        entry = residual
        normed = modulate(entry, shift_one, scale_one).astype(jnp.bfloat16)
        gathered = gather_rows(normed)
        projected = jnp.dot(
            gathered, input_weight[layer].reshape(width, -1), preferred_element_type=jnp.float32
        ).astype(jnp.bfloat16)
        queries, keys, values, scores, factor = window_scores(
            projected, tables[layer], onehot, layer
        )
        top = jnp.max(scores, axis=-1, keepdims=True)
        expo = jnp.exp(scores - top)
        total = jnp.sum(expo, axis=-1, keepdims=True)
        probs = (expo / total).astype(jnp.bfloat16)
        mixed = jnp.einsum("nhqk,nkhe->nqhe", probs, values, preferred_element_type=jnp.float32)
        attended = from_windows(
            mixed.reshape(mixed.shape[0], mixed.shape[1], -1).astype(jnp.bfloat16), layer
        )
        branch = scatter_rows(attended, output_weight[layer], local_rows)
        middle = entry + gate_one * branch
        normed_two = modulate(middle, shift_two, scale_two).astype(jnp.bfloat16)
        gathered_two = gather_rows(normed_two)
        hidden_pre = (
            jnp.dot(gathered_two, up_weight[layer], preferred_element_type=jnp.float32)
            + up_bias[layer]
        )
        hidden = jax.nn.gelu(hidden_pre).astype(jnp.bfloat16)
        branch_two = scatter_rows(hidden, down_weight[layer], local_rows)
        residual = middle + gate_two * branch_two
        saved.append(
            (
                entry,
                normed,
                gathered,
                projected,
                top,
                total,
                attended,
                branch,
                middle,
                normed_two,
                gathered_two,
                hidden_pre,
                hidden,
                branch_two,
            )
        )
    grad = cotangent.astype(jnp.float32)
    collected = [None, None]
    for layer in (1, 0):
        (
            entry,
            normed,
            gathered,
            projected,
            top,
            total,
            attended,
            branch,
            middle,
            normed_two,
            gathered_two,
            hidden_pre,
            hidden,
            branch_two,
        ) = saved[layer]
        shift_one, scale_one, gate_one, shift_two, scale_two, gate_two = [
            modulation[layer, number] for number in range(6)
        ]
        onehot = offset_map(layer)
        grad_down_branch = (gate_two * grad).astype(jnp.bfloat16)
        gate_two_grad = jnp.sum(grad * branch_two, axis=0)
        full_down = gather_grads(grad_down_branch)
        grad_hidden = lax.dot_general(
            full_down, down_weight[layer], CONTRACT_LAST, preferred_element_type=jnp.float32
        )
        down_grad = lax.dot_general(
            hidden, full_down, CONTRACT_FIRST, preferred_element_type=jnp.float32
        )
        gelu_pull = jax.vjp(jax.nn.gelu, hidden_pre)[1]
        grad_pre = gelu_pull(grad_hidden)[0].astype(jnp.bfloat16)
        up_bias_grad = jnp.sum(grad_pre, axis=0, dtype=jnp.float32)
        up_grad = lax.dot_general(
            gathered_two, grad_pre, CONTRACT_FIRST, preferred_element_type=jnp.float32
        )
        grad_normed_two = scatter_back(grad_pre, up_weight[layer], local_rows)
        middle_pull = jax.vjp(modulate, middle, shift_two, scale_two)[1]
        grad_middle, shift_two_grad, scale_two_grad = middle_pull(grad_normed_two)
        grad_middle = grad + grad_middle
        grad_out_branch = (gate_one * grad_middle).astype(jnp.bfloat16)
        gate_one_grad = jnp.sum(grad_middle * branch, axis=0)
        full_out = gather_grads(grad_out_branch)
        grad_attended = lax.dot_general(
            full_out, output_weight[layer], CONTRACT_LAST, preferred_element_type=jnp.float32
        ).astype(jnp.bfloat16)
        out_grad = lax.dot_general(
            attended, full_out, CONTRACT_FIRST, preferred_element_type=jnp.float32
        )
        queries, keys, values, scores, factor = window_scores(
            projected, tables[layer], onehot, layer
        )
        probs = jnp.exp(scores - top) / total
        heads = tables[layer].shape[0]
        upstream = to_windows(grad_attended, layer).reshape(queries.shape)
        grad_probs = jnp.einsum(
            "nqhe,nkhe->nhqk", upstream, values, preferred_element_type=jnp.float32
        )
        inner = jnp.sum(probs * grad_probs, axis=-1, keepdims=True)
        grad_scores = (probs * (grad_probs - inner)).astype(jnp.bfloat16)
        offset_grad = jnp.dot(
            jnp.sum(grad_scores, axis=0, dtype=jnp.float32).reshape(heads, -1),
            onehot,
            precision=HIGH,
        )
        grad_queries = (
            jnp.einsum("nhqk,nkhe->nqhe", grad_scores, keys, preferred_element_type=jnp.float32)
            * factor
        ).astype(jnp.bfloat16)
        grad_keys = (
            jnp.einsum("nhqk,nqhe->nkhe", grad_scores, queries, preferred_element_type=jnp.float32)
            * factor
        ).astype(jnp.bfloat16)
        grad_values = jnp.einsum(
            "nhqk,nqhe->nkhe",
            probs.astype(jnp.bfloat16),
            upstream,
            preferred_element_type=jnp.float32,
        ).astype(jnp.bfloat16)
        stacked = jnp.stack([grad_queries, grad_keys, grad_values], axis=2)
        grad_projected = from_windows(
            stacked.reshape(stacked.shape[0], stacked.shape[1], -1), layer
        )
        in_grad = lax.dot_general(
            gathered, grad_projected, CONTRACT_FIRST, preferred_element_type=jnp.float32
        ).reshape(input_weight.shape[1:])
        grad_normed = scatter_back(
            grad_projected, input_weight[layer].reshape(width, -1), local_rows
        )
        entry_pull = jax.vjp(modulate, entry, shift_one, scale_one)[1]
        grad_entry, shift_one_grad, scale_one_grad = entry_pull(grad_normed)
        grad = grad_middle + grad_entry
        partial_rows = jnp.stack(
            [
                shift_one_grad,
                scale_one_grad,
                gate_one_grad,
                shift_two_grad,
                scale_two_grad,
                gate_two_grad,
            ]
        )
        modulation_grad = lax.psum_scatter(partial_rows, "mp", scatter_dimension=1, tiled=True)
        projection_grad = activated.astype(jnp.float32)[:, None, None] * modulation_grad[None]
        grads_here = (
            projection_grad,
            modulation_grad,
            in_grad,
            out_grad,
            offset_grad,
            up_grad,
            up_bias_grad,
            down_grad,
        )
        collected[layer] = grads_here
    summed = jax.tree.map(
        lambda part: part.astype(jnp.float32), lax.psum(as_sent(collected[0] + collected[1]), "dp")
    )
    collected = [summed[:8], summed[8:]]

    def stacked_pair(number):
        return jnp.stack([collected[0][number], collected[1][number]])

    return (
        residual,
        grad,
        stacked_pair(0),
        stacked_pair(1),
        stacked_pair(2),
        stacked_pair(3),
        collected[0][4],
        collected[1][4],
        stacked_pair(5),
        stacked_pair(6),
        stacked_pair(7),
    )


def solution(mesh):
    return jax.shard_map(
        per_device,
        mesh=mesh,
        in_specs=(
            P(("dp", "mp"), None),
            P(("dp", "mp"), None),
            P("dp"),
            P("dp"),
            P("dp"),
            P(),
            P(),
            P(None, None, None, "mp"),
            P(None, None, "mp"),
            P(None, None, None, "mp"),
            P(None, "mp", None),
            P("mp", None),
            P("mp", None),
            P(None, None, "mp"),
            P(None, "mp"),
            P(None, "mp", None),
        ),
        out_specs=(
            P(("dp", "mp"), None),
            P(("dp", "mp"), None),
            P(None, None, None, "mp"),
            P(None, None, "mp"),
            P(None, None, None, "mp"),
            P(None, "mp", None),
            P("mp", None),
            P("mp", None),
            P(None, None, "mp"),
            P(None, "mp"),
            P(None, "mp", None),
        ),
        check_vma=False,
    )
```

profile of v0, /device:TPU:0, one launch (start us, length us, event | category | flops | bytes accessed | tf_op | source)
XLA Modules:
  0.0 3004.8 jit_solution(1778004621914010906)
XLA Ops:
  24.9 28.6 while.13
  99.6 41.6 %all-gather.10.cloned.1.call-done = bf16[2560,1024]{1,0:T(8,128)(2,1)} async-done(((bf16[1280,1024]{1,0:T(8,128)(2,1)}), bf16[2560,1024]{1,0:T(8,128)(2,1)}) %all-gather.10.cloned.1.call-update) | async-done | bytes 5242896 | tf_op jit(solution)/shard_map/all_gather | solution.py:103
  162.4 19.8 reshape_reshape.20
  261.6 122.0 %reduce-scatter.11.cloned.1.call-done = f32[1280,1024]{1,0:T(8,128)} async-done(((f32[2560,1024]{1,0:T(8,128)}), f32[1280,1024]{1,0:T(8,128)}) %reduce-scatter.11.cloned.1.call-update) | async-done | bytes 5242896 | tf_op jit(solution)/shard_map/reduce_scatter | solution.py:115
  393.3 66.8 %all-gather.12.cloned.1.call-done = bf16[2560,1024]{1,0:T(8,128)(2,1)} async-done(((bf16[1280,1024]{1,0:T(8,128)(2,1)}), bf16[2560,1024]{1,0:T(8,128)(2,1)}) %all-gather.12.cloned.1.call-update) | async-done | bytes 5242896 | tf_op jit(solution)/shard_map/all_gather | solution.py:103
  478.4 21.2 fusion.72
  502.4 119.3 %reduce-scatter.13.cloned.1.call-done = f32[1280,1024]{1,0:T(8,128)} async-done(((f32[2560,1024]{1,0:T(8,128)}), f32[1280,1024]{1,0:T(8,128)}) %reduce-scatter.13.cloned.1.call-update) | async-done | bytes 5242896 | tf_op jit(solution)/shard_map/reduce_scatter | solution.py:115
  658.4 41.3 %all-gather.14.cloned.1.call-done = bf16[2560,1024]{1,0:T(8,128)(2,1)} async-done(((bf16[1280,1024]{1,0:T(8,128)(2,1)}), bf16[2560,1024]{1,0:T(8,128)(2,1)}) %all-gather.14.cloned.1.call-update) | async-done | bytes 5242896 | tf_op jit(solution)/shard_map/all_gather | solution.py:103
  785.7 38.4 %fusion.206 = (f32[8,8,320]{2,1,0:T(8,128)S(1)}, f32[8,8,320,320]{2,3,1,0:T(8,128)}) fusion(f32[8,8,320,320]{2,3,1,0:T(8,128)} %fusion.90, f32[8,320,320]{1,2,0:T(8,128)} %copy.174), kind=kOutput, calls=%fused_computation.323 | output fusion | flops 39321920 | bytes 55787520 | tf_op jit(solution)/shard_map/sub | solution.py:193
  824.0 32.6 %convert_bitcast_fusion.7 = bf16[8,320,8,64]{1,3,2,0:T(8,128)(2,1)} fusion(bf16[8,320,1,8,64]{1,4,3,0,2:T(8,128)(2,1)} %copy.220, f32[8,8,320]{2,1,0:T(8,128)S(1)} %get-tuple-element.220, f32[8,8,320,320]{2,3,1,0:T(8,128)} %fusion.90, f32[8,320,320]{1,2,0:T(8,128)} %copy.174), kind=kOutput, calls=%fused_computation.193 | convolution fusion | flops 886067520 | bytes 34816000 | tf_op jit(solution)/shard_map/nhqk,nkhe->nqhe/dot_general | solution.py:196
  878.6 122.0 %reduce-scatter.15.cloned.1.call-done = f32[1280,1024]{1,0:T(8,128)} async-done(((f32[2560,1024]{1,0:T(8,128)}), f32[1280,1024]{1,0:T(8,128)}) %reduce-scatter.15.cloned.1.call-update) | async-done | bytes 5242896 | tf_op jit(solution)/shard_map/reduce_scatter | solution.py:115
  1012.2 66.3 %all-gather.16.cloned.1.call-done = bf16[2560,1024]{1,0:T(8,128)(2,1)} async-done(((bf16[1280,1024]{1,0:T(8,128)(2,1)}), bf16[2560,1024]{1,0:T(8,128)(2,1)}) %all-gather.16.cloned.1.call-update) | async-done | bytes 5242896 | tf_op jit(solution)/shard_map/all_gather | solution.py:103
  1096.7 52.5 %all-gather.18.cloned.1.call-done = bf16[2560,1024]{1,0:T(8,128)(2,1)} async-done(((bf16[1280,1024]{1,0:T(8,128)(2,1)}), bf16[2560,1024]{1,0:T(8,128)(2,1)}) %all-gather.18.cloned.1.call-update) | async-done | bytes 5242896 | tf_op jit(solution)/shard_map/all_gather | solution.py:107
  1149.2 30.7 %fusion.207 = (bf16[2048]{0:T(1024)(128)(2,1)}, bf16[2560,2048]{1,0:T(8,128)(2,1)}) fusion(f32[2560,2048]{1,0:T(8,128)} %fusion.69, f32[2048]{0:T(1024)S(1)} %bitcast.397, bf16[2560,1024]{1,0:T(8,128)(2,1)} %all-gather.18.cloned.1.call-done, bf16[2,2048,1024]{2,1,0:T(8,128)(2,1)} %param.33), kind=kOutput, calls=%fused_computation.324 | convolution fusion | flops 10852759552 | bytes 40906752 | tf_op jit(solution)/shard_map/dot_general | solution.py:255
  1196.8 65.8 %reduce-scatter.19.cloned.1.call-done = bf16[1280,1024]{1,0:T(8,128)(2,1)} async-done(((bf16[2560,1024]{1,0:T(8,128)(2,1)}), bf16[1280,1024]{1,0:T(8,128)(2,1)}) %reduce-scatter.19.cloned.1.call-update) | async-done | bytes 2621456 | tf_op jit(solution)/shard_map/reduce_scatter | solution.py:125
  1276.5 68.7 %all-gather.20.cloned.1.call-done = bf16[2560,1024]{1,0:T(8,128)(2,1)} async-done(((bf16[1280,1024]{1,0:T(8,128)(2,1)}), bf16[2560,1024]{1,0:T(8,128)(2,1)}) %all-gather.20.cloned.1.call-update) | async-done | bytes 5242896 | tf_op jit(solution)/shard_map/all_gather | solution.py:107
  1362.9 32.5 %convert_bitcast_fusion.6 = bf16[8,320,1,8,64]{1,4,3,0,2:T(8,128)(2,1)} fusion(bf16[8,320,8,64]{1,3,2,0:T(8,128)(2,1)} %copy.179, f32[8,8,320]{2,1,0:T(8,128)S(1)} %get-tuple-element.220, f32[8,8,320,320]{2,3,1,0:T(8,128)} %fusion.90, f32[8,320,320]{1,2,0:T(8,128)} %copy.174), kind=kOutput, calls=%fused_computation.192 | convolution fusion | flops 886067520 | bytes 34816000 | tf_op jit(solution)/shard_map/nhqk,nqhe->nkhe/dot_general | solution.py:304
  1395.4 26.1 multiply_reduce_fusion
  1421.5 28.4 convert_reduce_fusion
  1497.6 20.7 reshape_reshape.23
  1538.1 21.4 fusion.66
  1559.6 43.7 %reduce-scatter.21.cloned.1.call-done = bf16[1280,1024]{1,0:T(8,128)(2,1)} async-done(((bf16[2560,1024]{1,0:T(8,128)(2,1)}), bf16[1280,1024]{1,0:T(8,128)(2,1)}) %reduce-scatter.21.cloned.1.call-update) | async-done | bytes 2621456 | tf_op jit(solution)/shard_map/reduce_scatter | solution.py:125
  1613.1 114.8 %reduce-scatter.17.cloned.1.call-done = f32[1280,1024]{1,0:T(8,128)} async-done(((f32[2560,1024]{1,0:T(8,128)}), f32[1280,1024]{1,0:T(8,128)}) %reduce-scatter.17.cloned.1.call-update) | async-done | bytes 5242896 | tf_op jit(solution)/shard_map/reduce_scatter | solution.py:115
  1748.1 68.7 %all-gather.22.cloned.1.call-done = bf16[2560,1024]{1,0:T(8,128)(2,1)} async-done(((bf16[1280,1024]{1,0:T(8,128)(2,1)}), bf16[2560,1024]{1,0:T(8,128)(2,1)}) %all-gather.22.cloned.1.call-update) | async-done | bytes 5242896 | tf_op jit(solution)/shard_map/all_gather | solution.py:107
  1816.8 30.8 %fusion.208 = (bf16[2048]{0:T(1024)(128)(2,1)}, bf16[2560,2048]{1,0:T(8,128)(2,1)S(1)}) fusion(f32[2560,2048]{1,0:T(8,128)} %fusion.75, f32[2048]{0:T(1024)S(1)} %bitcast.395, bf16[2560,1024]{1,0:T(8,128)(2,1)} %all-gather.22.cloned.1.call-done, bf16[2,2048,1024]{2,1,0:T(8,128)(2,1)} %param.33), kind=kOutput, calls=%fused_computation.325 | convolution fusion | flops 10852759552 | bytes 40906752 | tf_op jit(solution)/shard_map/dot_general | solution.py:255
  1867.1 65.8 %reduce-scatter.23.cloned.1.call-done = bf16[1280,1024]{1,0:T(8,128)(2,1)} async-done(((bf16[2560,1024]{1,0:T(8,128)(2,1)}), bf16[1280,1024]{1,0:T(8,128)(2,1)}) %reduce-scatter.23.cloned.1.call-update) | async-done | bytes 2621456 | tf_op jit(solution)/shard_map/reduce_scatter | solution.py:125
  1953.6 68.7 %all-gather.24.cloned.1.call-done = bf16[2560,1024]{1,0:T(8,128)(2,1)} async-done(((bf16[1280,1024]{1,0:T(8,128)(2,1)}), bf16[2560,1024]{1,0:T(8,128)(2,1)}) %all-gather.24.cloned.1.call-update) | async-done | bytes 5242896 | tf_op jit(solution)/shard_map/all_gather | solution.py:107
  2111.9 20.7 reshape_reshape.25
  2168.8 21.9 convert_bitcast_fusion
  2220.9 22.1 convert_bitcast_fusion.1
  2354.2 65.4 %all-reduce.1 = (bf16[1,6,512]{2,1,0:T(8,128)(2,1)S(1)}, bf16[1,6,512]{2,1,0:T(8,128)(2,1)S(1)}, bf16[8,62]{1,0:T(8,128)(2,1)S(1)}, bf16[8,39]{1,0:T(8,128)(2,1)...) all-reduce(bf16[1,6,512]{2,1,0:T(8,128)(2,1)S(1)} %convert_bitcast_, ...), channel_id=1, replica_groups=mesh['dp'=16,'mp'=2] {'dp'}, use_global_device_ids=true, to_apply=%region_49.50 | all-reduce | flops 11048 | bytes 44192 | tf_op jit(solution)/shard_map/psum | solution.py:347
  2422.1 532.7 %all-reduce.5.cloned.1.call-done = (bf16[1,1024,6,512]{3,1,2,0:T(8,128)(2,1)}, bf16[1,1024,6,512]{3,1,2,0:T(8,128)(2,1)}, bf16[1,1024,3,512]{3,1,2,0:T(8,128)(2,...) async-done(((bf16[1,1024,6,512]{3,1,2,0:T(8,128)(2,1)}, ...) | async-done | bytes 37748752 | tf_op jit(solution)/shard_map/psum | solution.py:347
  (429 shorter events, 874.3 us)
Async XLA Ops:
  7.2 134.0 %all-gather.10.cloned.1.call-start = ((), (), s32[]{:S(2)}) async-start(), calls=%async_computation.10 | async-start | bytes 7864320 | tf_op jit(solution)/shard_map/all_gather | solution.py:103
  72.5 311.1 %copy-start.66 = (f32[1,1,1024]{2,0,1:T(1,128)}, f32[1,1,1024]{2,0,1:T(1,128)S(1)}, u32[]{:S(2)}) copy-start(f32[1,1,1024]{2,0,1:T(1,128)S(1)} %get-tuple-element.213) | copy-start | bytes 12292
  72.5 315.1 %copy-start.51 = (f32[1,1,1024]{2,0,1:T(1,128)}, f32[1,1,1024]{2,0,1:T(1,128)S(1)}, u32[]{:S(2)}) copy-start(f32[1,1,1024]{2,0,1:T(1,128)S(1)} %get-tuple-element.209) | copy-start | bytes 12292
  74.9 308.7 %reduce-scatter.11.cloned.1.call-start = ((), (), s32[]{:S(2)}) async-start(), calls=%async_computation.11 | async-start | bytes 15728640 | tf_op jit(solution)/shard_map/reduce_scatter | solution.py:115
  261.5 198.6 %all-gather.12.cloned.1.call-start = ((), (), s32[]{:S(2)}) async-start(), calls=%async_computation.12 | async-start | bytes 7864320 | tf_op jit(solution)/shard_map/all_gather | solution.py:103
  391.4 230.3 %reduce-scatter.13.cloned.1.call-start = ((), (), s32[]{:S(2)}) async-start(), calls=%async_computation.13 | async-start | bytes 15728640 | tf_op jit(solution)/shard_map/reduce_scatter | solution.py:115
  393.3 85.2 %copy-start.88 = (f32[1,2048]{1,0:T(1,128)}, f32[1,2048]{1,0:T(1,128)S(1)}, u32[]{:S(2)}) copy-start(f32[1,2048]{1,0:T(1,128)S(1)} %get-tuple-element.215) | copy-start | bytes 24580
  499.7 122.0 %copy-start.70 = (f32[1,1,1024]{2,0,1:T(1,128)S(1)}, f32[1,1,1024]{2,0,1:T(1,128)}, u32[]{:S(2)}) copy-start(f32[1,1,1024]{2,0,1:T(1,128)} %get-tuple-element.210) | copy-start | bytes 12292
  499.7 200.0 %all-gather.14.cloned.1.call-start = ((), (), s32[]{:S(2)}) async-start(), calls=%async_computation.14 | async-start | bytes 7864320 | tf_op jit(solution)/shard_map/all_gather | solution.py:103
  502.4 129.6 %copy-start.33 = (pred[102400,15]{0,1:T(8,128)(4,1)}, pred[102400,15]{0,1:T(8,128)(4,1)S(1)}, u32[]{:S(2)}) copy-start(pred[102400,15]{0,1:T(8,128)(4,1)S(1)} %get-tuple-element.232) | copy-start | bytes 4608004
  631.0 369.5 %reduce-scatter.15.cloned.1.call-start = ((), (), s32[]{:S(2)}) async-start(), calls=%async_computation.15 | async-start | bytes 15728640 | tf_op jit(solution)/shard_map/reduce_scatter | solution.py:115
  878.5 122.0 %copy-start.72 = (f32[1,1,1024]{2,0,1:T(1,128)S(1)}, f32[1,1,1024]{2,0,1:T(1,128)}, u32[]{:S(2)}) copy-start(f32[1,1,1024]{2,0,1:T(1,128)} %get-tuple-element.207) | copy-start | bytes 12292
  878.5 200.0 %all-gather.16.cloned.1.call-start = ((), (), s32[]{:S(2)}) async-start(), calls=%async_computation.16 | async-start | bytes 7864320 | tf_op jit(solution)/shard_map/all_gather | solution.py:103
  1009.8 139.4 %all-gather.18.cloned.1.call-start = ((), (), s32[]{:S(2)}) async-start(), calls=%async_computation.18 | async-start | bytes 7864320 | tf_op jit(solution)/shard_map/all_gather | solution.py:107
  1012.1 137.1 %copy-start.91 = (f32[1,2048]{1,0:T(1,128)S(1)}, f32[1,2048]{1,0:T(1,128)}, u32[]{:S(2)}) copy-start(f32[1,2048]{1,0:T(1,128)} %get-tuple-element.214) | copy-start | bytes 24580
  1012.1 250.4 %reduce-scatter.19.cloned.1.call-start = ((), (), s32[]{:S(2)}) async-start(), calls=%async_computation.19 | async-start | bytes 7864320 | tf_op jit(solution)/shard_map/reduce_scatter | solution.py:125
  1196.7 148.5 %all-gather.20.cloned.1.call-start = ((), (), s32[]{:S(2)}) async-start(), calls=%async_computation.20 | async-start | bytes 7864320 | tf_op jit(solution)/shard_map/all_gather | solution.py:107
  1276.4 326.8 %reduce-scatter.21.cloned.1.call-start = ((), (), s32[]{:S(2)}) async-start(), calls=%async_computation.21 | async-start | bytes 7864320 | tf_op jit(solution)/shard_map/reduce_scatter | solution.py:125
  1537.4 190.5 %reduce-scatter.17.cloned.1.call-start = ((), (), s32[]{:S(2)}) async-start(), calls=%async_computation.17 | async-start | bytes 15728640 | tf_op jit(solution)/shard_map/reduce_scatter | solution.py:115
  1559.6 257.2 %all-gather.22.cloned.1.call-start = ((), (), s32[]{:S(2)}) async-start(), calls=%async_computation.22 | async-start | bytes 7864320 | tf_op jit(solution)/shard_map/all_gather | solution.py:107
  1607.7 120.2 %copy-start.62 = (f32[1280]{0:T(1024)S(1)}, f32[1280]{0:T(1024)}, u32[]{:S(2)}) copy-start(f32[1280]{0:T(1024)} %copy-done.61) | copy-start | bytes 15364
  1607.7 120.2 %copy-start.69 = (f32[1,1,1024]{2,0,1:T(1,128)S(1)}, f32[1,1,1024]{2,0,1:T(1,128)}, u32[]{:S(2)}) copy-start(f32[1,1,1024]{2,0,1:T(1,128)} %get-tuple-element.202) | copy-start | bytes 12292
  1613.0 132.7 %copy-start.71 = (f32[1,1,1024]{2,0,1:T(1,128)S(1)}, f32[1,1,1024]{2,0,1:T(1,128)}, u32[]{:S(2)}) copy-start(f32[1,1,1024]{2,0,1:T(1,128)} %get-tuple-element.210) | copy-start | bytes 12292
  1745.7 71.0 %copy-start.89 = (f32[1,2048]{1,0:T(1,128)S(1)}, f32[1,2048]{1,0:T(1,128)}, u32[]{:S(2)}) copy-start(f32[1,2048]{1,0:T(1,128)} %copy-done.88) | copy-start | bytes 24580
  1748.0 184.8 %reduce-scatter.23.cloned.1.call-start = ((), (), s32[]{:S(2)}) async-start(), calls=%async_computation.23 | async-start | bytes 7864320 | tf_op jit(solution)/shard_map/reduce_scatter | solution.py:125
  1867.0 70.3 %copy-start.44 = (f32[1280]{0:T(1024)S(1)}, f32[1280]{0:T(1024)}, u32[]{:S(2)}) copy-start(f32[1280]{0:T(1024)} %copy-done.43) | copy-start | bytes 15364
  1867.1 155.2 %all-gather.24.cloned.1.call-start = ((), (), s32[]{:S(2)}) async-start(), calls=%async_computation.24 | async-start | bytes 7864320 | tf_op jit(solution)/shard_map/all_gather | solution.py:107
  1951.2 71.0 %copy-start.98 = (bf16[2,512,1024]{2,1,0:T(8,128)(2,1)S(1)}, bf16[2,512,1024]{2,1,0:T(8,128)(2,1)}, u32[]{:S(2)}) copy-start(bf16[2,512,1024]{2,1,0:T(8,128)(2,1)} %param.28) | copy-start | bytes 6291460
  1953.5 330.9 %reduce-scatter.25.cloned.1.call-start = ((), (), s32[]{:S(2)}) async-start(), calls=%async_computation.25 | async-start | bytes 7864320 | tf_op jit(solution)/shard_map/reduce_scatter | solution.py:125
  2151.7 146.9 %reduce-scatter.29.cloned.1.call-start = ((), (), s32[]{:S(2)}) async-start(), calls=%async_computation.27 | async-start | bytes 49152 | tf_op jit(solution)/shard_map/reduce_scatter | solution.py:333
  2220.8 80.6 %reduce-scatter.27.cloned.1.call-start = ((), (), s32[]{:S(2)}) async-start(), calls=%async_computation.26 | async-start | bytes 49152 | tf_op jit(solution)/shard_map/reduce_scatter | solution.py:333
  2291.4 663.3 %all-reduce.5.cloned.1.call-start = ((), (), s32[]{:S(2)}) async-start(), calls=%async_computation.28 | async-start | bytes 75497472 | tf_op jit(solution)/shard_map/psum | solution.py:347
  (91 other events, 983.6 us)
Sparse Core Ops, SparseCore 0:
  75.0 66.1 all-gather.9
  261.7 121.8 reduce-scatter.10
  391.5 68.5 all-gather.11
  499.8 121.8 reduce-scatter.12
  631.1 68.5 all-gather.13
  878.6 121.8 reduce-scatter.14
  1009.9 68.5 all-gather.15
  1080.6 68.5 all-gather.17
  1196.8 65.6 reduce-scatter.18
  1276.6 68.5 all-gather.19
  1537.6 65.6 reduce-scatter.20
  1606.0 121.8 reduce-scatter.16
  1748.1 68.5 all-gather.21
  1867.2 65.6 reduce-scatter.22
  1953.6 68.5 all-gather.23
  2151.8 65.6 reduce-scatter.24
  2220.9 9.8 reduce-scatter.28
  2291.5 9.8 reduce-scatter.26
  2311.1 643.6 all-reduce.4
where the time goes:
time: 3010 us; the launch traced here: 3000 us
  waiting for transfers between devices  1660 us (55%)
  matrix products  597 us (20%)
  local copies, waits for them, and re-layouts  365 us (12%)
  other arithmetic  258 us (9%)
  blocking collectives  83.6 us (3%)
    psum x1, waiting for transfers between devices, per_device(): lax.psum(as_sent(collected[0] + collected[1]), 'dp')  533 us
    reduce_scatter x4, waiting for transfers between devices, scatter_rows(): lax.psum_scatter(term(jnp.int32(0), count * lax.axis_size('mp')), 'mp', s...  478 us
    all_gather x4, waiting for transfers between devices, gather_grads(): return lax.all_gather(values, 'mp', axis=0, tiled=True)  259 us
    all_gather x4, waiting for transfers between devices, gather_rows(): return lax.all_gather(values, 'mp', axis=0, tiled=True)  216 us
    reduce_scatter x4, waiting for transfers between devices, scatter_back(): lax.psum_scatter(term(jnp.int32(0), count * lax.axis_size('mp')).astype(j...  175 us
    unnamed x222, local copies, waits for them, and re-layouts  83.9 us
    psum x1, blocking collectives, per_device(): lax.psum(as_sent(collected[0] + collected[1]), 'dp')  65.4 us
    dot_general x2, matrix products, per_device(): lax.dot_general(full_down, down_weight[layer], CONTRACT_LAST, preferred_e...  61.5 us
  transfers between devices with their start and end apart: 19, of which 17 were waited for; matrix products, arithmetic and copies ran while one was open for 10% of the time, Pallas kernels for 0%

commit v1 on v0

--- a/solution.py
+++ b/solution.py
@@ -1,6 +1,12 @@
+import functools
+
 import jax
 import jax.numpy as jnp
+import numpy as np
 from jax import lax
+from jax.experimental import pallas as pl
+from jax.experimental.pallas import tpu as pltpu
+from jax.sharding import Mesh
 from jax.sharding import PartitionSpec as P
 
 FRAMES = 5
@@ -366,16 +372,933 @@
     )
 
 
+VMEM = 58 * 2**20
+ROWS = 256
+HEAD = 64
+
+
+def full_block(*shape):
+    return pl.BlockSpec(shape, lambda *_: (0,) * len(shape))
+
+
+def once_block(*shape):
+    return pl.BlockSpec(shape, lambda *_: (0,) * len(shape), pipeline_mode=pl.Buffered(1))
+
+
+def params():
+    return pltpu.CompilerParams(vmem_limit_bytes=VMEM)
+
+
+def cost(flops, moved, exps=0):
+    return pl.CostEstimate(flops=int(flops), bytes_accessed=int(moved), transcendentals=int(exps))
+
+
+def shaped(*arrays):
+    return sum(int(np.prod(a.shape)) * a.dtype.itemsize for a in arrays)
+
+
+def row_norm(values):
+    centred = values - jnp.mean(values, axis=-1, keepdims=True)
+    spread = jnp.mean(centred * centred, axis=-1, keepdims=True)
+    scale = lax.rsqrt(spread + EPSILON)
+    return centred * scale, scale
+
+
+def norm_back(values, grad, shift_scale):
+    unit, inverse = row_norm(values)
+    inner = grad * (1.0 + shift_scale)
+    first = jnp.mean(inner, axis=-1, keepdims=True)
+    second = jnp.mean(inner * unit, axis=-1, keepdims=True)
+    pulled = inverse * (inner - first - unit * second)
+    return (
+        pulled,
+        jnp.sum(grad, axis=0, keepdims=True),
+        jnp.sum(grad * unit, axis=0, keepdims=True),
+    )
+
+
+def project_kernel(x_ref, shift_ref, scale_ref, weight_ref, turned_ref, out_ref, normed_ref):
+    rows = x_ref.shape[0]
+
+    @pl.when(pl.program_id(0) == 0)
+    def _():
+        for start in range(0, rows, ROWS):
+            part = pl.ds(start, ROWS)
+            unit, _ = row_norm(x_ref[part, :])
+            value = (unit * (1.0 + scale_ref[...]) + shift_ref[...]).astype(jnp.bfloat16)
+            normed_ref[part, :] = value
+            turned_ref[:, part] = value.T
+
+    for start in range(0, rows, ROWS):
+        part = pl.ds(start, ROWS)
+        out_ref[0, part, :] = jnp.dot(
+            normed_ref[part, :], weight_ref[0], preferred_element_type=jnp.float32
+        ).astype(jnp.bfloat16)
+
+
+def project(x, shift, scale, weight):
+    rows, width = x.shape
+    count, _, cols = weight.shape
+    outs = (
+        jax.ShapeDtypeStruct((width, rows), jnp.bfloat16),
+        jax.ShapeDtypeStruct((count, rows, cols), jnp.bfloat16),
+    )
+    return pl.pallas_call(
+        project_kernel,
+        out_shape=outs,
+        grid=(count,),
+        in_specs=[
+            once_block(rows, width),
+            full_block(1, width),
+            full_block(1, width),
+            pl.BlockSpec((1, width, cols), lambda q: (q, 0, 0)),
+        ],
+        out_specs=(
+            full_block(width, rows),
+            pl.BlockSpec((1, rows, cols), lambda q: (q, 0, 0)),
+        ),
+        scratch_shapes=[pltpu.VMEM((rows, width), jnp.bfloat16)],
+        compiler_params=params(),
+        cost_estimate=cost(2 * rows * width * cols * count, shaped(x, weight, *outs)),
+        name="project",
+    )(x, shift, scale, weight)
+
+
+def pair_scores(kk, query, ublk):
+    scores = lax.dot_general(
+        kk, jnp.concatenate([query, ublk], axis=1), CONTRACT_LAST, preferred_element_type=jnp.float32
+    )
+    expo = jnp.exp(scores - jnp.max(scores, axis=0, keepdims=True))
+    return expo * (1.0 / jnp.sum(expo, axis=0, keepdims=True))
+
+
+def attend_kernel(proj_ref, ublk_ref, place_ref, out_ref):
+    count = proj_ref.shape[1]
+    heads = ublk_ref.shape[0]
+    wide = heads * HEAD
+    lane = lax.broadcasted_iota(jnp.int32, (count, 128), 1)
+    place = place_ref[...]
+    for pair in range(heads // 2):
+        query = proj_ref[0, :, pair * 128 : pair * 128 + 128]
+        key = proj_ref[0, :, wide + pair * 128 : wide + pair * 128 + 128]
+        value = proj_ref[0, :, 2 * wide + pair * 128 : 2 * wide + pair * 128 + 128]
+        turned = value.T
+        kk = jnp.concatenate([key, place], axis=1)
+        halves = []
+        for half in range(2):
+            mine = (lane < HEAD) if half == 0 else (lane >= HEAD)
+            scaled = jnp.where(mine, query * HEAD**-0.5, 0.0).astype(jnp.bfloat16)
+            probs = pair_scores(kk, scaled, ublk_ref[2 * pair + half]).astype(jnp.bfloat16)
+            mixed = jnp.dot(turned, probs, preferred_element_type=jnp.float32)
+            halves.append(mixed[half * HEAD : half * HEAD + HEAD])
+        out_ref[:, pair * 128 : pair * 128 + 128] = (
+            jnp.concatenate(halves, axis=0).astype(jnp.bfloat16).T
+        )
+
+
+def attend(proj, ublk, place):
+    quarters, rows, cols = proj.shape
+    count = place.shape[0]
+    heads = ublk.shape[0] // quarters
+    out = jax.ShapeDtypeStruct((rows, quarters * heads * HEAD), jnp.bfloat16)
+    pairs = rows * count * heads * quarters
+    return pl.pallas_call(
+        attend_kernel,
+        out_shape=out,
+        grid=(quarters, rows // count),
+        in_specs=[
+            pl.BlockSpec((1, count, cols), lambda q, w: (q, w, 0)),
+            pl.BlockSpec((heads, count, 128), lambda q, w: (q, 0, 0)),
+            full_block(count, 128),
+        ],
+        out_specs=pl.BlockSpec((count, heads * HEAD), lambda q, w: (w, q)),
+        compiler_params=params(),
+        cost_estimate=cost(pairs * 768, shaped(proj, ublk, out), pairs),
+        name="attend",
+    )(proj, ublk, place)
+
+
+def join_kernel(
+    att_ref, weight_ref, x_ref, gate_ref, shift_ref, scale_ref, branch_ref, middle_ref, normed_ref, turned_ref
+):
+    branch = jnp.dot(att_ref[...], weight_ref[...], preferred_element_type=jnp.float32)
+    branch_ref[...] = branch
+    middle = x_ref[...] + gate_ref[...] * branch
+    middle_ref[...] = middle
+    unit, _ = row_norm(middle)
+    normed = (unit * (1.0 + scale_ref[...]) + shift_ref[...]).astype(jnp.bfloat16)
+    normed_ref[...] = normed
+    turned_ref[...] = normed.T
+
+
+def join(att, weight, x, gate, shift, scale):
+    rows, width = x.shape
+    outs = (
+        jax.ShapeDtypeStruct((rows, width), jnp.float32),
+        jax.ShapeDtypeStruct((rows, width), jnp.float32),
+        jax.ShapeDtypeStruct((rows, width), jnp.bfloat16),
+        jax.ShapeDtypeStruct((width, rows), jnp.bfloat16),
+    )
+    tile = pl.BlockSpec((ROWS, width), lambda i: (i, 0))
+    return pl.pallas_call(
+        join_kernel,
+        out_shape=outs,
+        grid=(rows // ROWS,),
+        in_specs=[tile, once_block(width, width), tile] + [full_block(1, width)] * 3,
+        out_specs=(tile, tile, tile, pl.BlockSpec((width, ROWS), lambda i: (0, i))),
+        compiler_params=params(),
+        cost_estimate=cost(2 * rows * width * width, shaped(att, weight, x, *outs)),
+        name="join",
+    )(att, weight, x, gate, shift, scale)
+
+
+SLOPE = float(np.sqrt(2 / np.pi))
+
+
+def up_kernel(normed_ref, weight_ref, bias_ref, pre_ref, hidden_ref):
+    for start in range(0, normed_ref.shape[0], ROWS):
+        part = pl.ds(start, ROWS)
+        pre = (
+            jnp.dot(normed_ref[part, :], weight_ref[0], preferred_element_type=jnp.float32)
+            + bias_ref[0]
+        )
+        pre_ref[0, part, :] = pre
+        bent = jnp.tanh(SLOPE * (pre + 0.044715 * (pre * pre * pre)))
+        hidden_ref[0, part, :] = (pre * (0.5 * (1.0 + bent))).astype(jnp.bfloat16)
+
+
+def up(normed, weight, bias):
+    rows, width = normed.shape
+    count, _, cols = weight.shape
+    outs = (
+        jax.ShapeDtypeStruct((count, rows, cols), jnp.float32),
+        jax.ShapeDtypeStruct((count, rows, cols), jnp.bfloat16),
+    )
+    return pl.pallas_call(
+        up_kernel,
+        out_shape=outs,
+        grid=(count,),
+        in_specs=[
+            once_block(rows, width),
+            pl.BlockSpec((1, width, cols), lambda q: (q, 0, 0)),
+            pl.BlockSpec((1, 1, cols), lambda q: (q, 0, 0)),
+        ],
+        out_specs=(
+            pl.BlockSpec((1, rows, cols), lambda q: (q, 0, 0)),
+            pl.BlockSpec((1, rows, cols), lambda q: (q, 0, 0)),
+        ),
+        compiler_params=params(),
+        cost_estimate=cost(2 * rows * width * cols * count, shaped(normed, weight, *outs)),
+        name="up",
+    )(normed, weight, bias)
+
+
+def down_kernel(hidden_ref, weight_ref, middle_ref, gate_ref, branch_ref, out_ref):
+    total = jnp.dot(hidden_ref[0], weight_ref[0], preferred_element_type=jnp.float32)
+    for quarter in range(1, hidden_ref.shape[0]):
+        total += jnp.dot(hidden_ref[quarter], weight_ref[quarter], preferred_element_type=jnp.float32)
+    branch_ref[...] = total
+    out_ref[...] = middle_ref[...] + gate_ref[...] * total
+
+
+def down(hidden, weight, middle, gate):
+    rows, width = middle.shape
+    count, cols, _ = weight.shape
+    outs = (
+        jax.ShapeDtypeStruct((rows, width), jnp.float32),
+        jax.ShapeDtypeStruct((rows, width), jnp.float32),
+    )
+    tile = pl.BlockSpec((ROWS, width), lambda i: (i, 0))
+    return pl.pallas_call(
+        down_kernel,
+        out_shape=outs,
+        grid=(rows // ROWS,),
+        in_specs=[
+            pl.BlockSpec((count, ROWS, cols), lambda i: (0, i, 0)),
+            once_block(count, cols, width),
+            tile,
+            full_block(1, width),
+        ],
+        out_specs=(tile, tile),
+        compiler_params=params(),
+        cost_estimate=cost(2 * rows * width * cols * count, shaped(hidden, weight, middle, *outs)),
+        name="down",
+    )(hidden, weight, middle, gate)
+
+
+def feed_back_kernel(
+    list_ref, gdb_ref, hidden_ref, pre_ref, turned_ref, down_ref, up_ref,
+    down_grad_ref, up_grad_ref, bias_grad_ref, normed_grad_ref, gpre_ref,
+):
+    rows = gdb_ref.shape[0]
+    first = (pl.program_id(0) == 0) & (pl.program_id(1) == 0)
+    sums = jnp.zeros(bias_grad_ref.shape[1:], jnp.float32)
+    for start in range(0, rows, ROWS):
+        part = pl.ds(start, ROWS)
+        grad_hidden = lax.dot_general(
+            gdb_ref[part, :], down_ref[0], CONTRACT_LAST, preferred_element_type=jnp.float32
+        )
+        pre = pre_ref[0, part, :]
+        square = pre * pre
+        bent = jnp.tanh(SLOPE * (pre + 0.044715 * (pre * square)))
+        slope = 0.5 * (1.0 + bent) + (0.5 * SLOPE) * pre * (1.0 - bent * bent) * (
+            1.0 + (3 * 0.044715) * square
+        )
+        grad_pre = (grad_hidden * slope).astype(jnp.bfloat16)
+        gpre_ref[part, :] = grad_pre
+        sums += jnp.sum(grad_pre.astype(jnp.float32), axis=0, keepdims=True)
+    bias_grad_ref[0] = sums
+    down_grad_ref[0] = lax.dot_general(
+        hidden_ref[0], gdb_ref[...], CONTRACT_FIRST, preferred_element_type=jnp.float32
+    ).astype(jnp.bfloat16)
+    up_grad_ref[0] = jnp.dot(
+        turned_ref[...], gpre_ref[...], preferred_element_type=jnp.float32
+    ).astype(jnp.bfloat16)
+
+    def term(part):
+        return lax.dot_general(
+            gpre_ref[part, :], up_ref[0], CONTRACT_LAST, preferred_element_type=jnp.float32
+        )
+
+    @pl.when(first)
+    def _():
+        for start in range(0, rows, ROWS):
+            part = pl.ds(start, ROWS)
+            normed_grad_ref[part, :] = term(part)
+
+    @pl.when(jnp.logical_not(first))
+    def _():
+        for start in range(0, rows, ROWS):
+            part = pl.ds(start, ROWS)
+            normed_grad_ref[part, :] += term(part)
+
+
+def feed_back(quarters, gdb, hidden, pre, turned, down_weight, up_weight):
+    rows, width = gdb.shape
+    cols = hidden.shape[2]
+    step = min(512, cols)
+    picked = quarters.shape[0]
+    outs = (
+        jax.ShapeDtypeStruct((picked, cols, width), jnp.bfloat16),
+        jax.ShapeDtypeStruct((picked, width, cols), jnp.bfloat16),
+        jax.ShapeDtypeStruct((picked, 1, cols), jnp.float32),
+        jax.ShapeDtypeStruct((rows, width), jnp.float32),
+    )
+    grid_spec = pltpu.PrefetchScalarGridSpec(
+        num_scalar_prefetch=1,
+        grid=(picked, cols // step),
+        in_specs=[
+            once_block(rows, width),
+            pl.BlockSpec((1, rows, step), lambda q, j, s: (s[q], 0, j)),
+            pl.BlockSpec((1, rows, step), lambda q, j, s: (s[q], 0, j)),
+            once_block(width, rows),
+            pl.BlockSpec((1, step, width), lambda q, j, s: (s[q], j, 0)),
+            pl.BlockSpec((1, width, step), lambda q, j, s: (s[q], 0, j)),
+        ],
+        out_specs=(
+            pl.BlockSpec((1, step, width), lambda q, j, s: (q, j, 0)),
+            pl.BlockSpec((1, width, step), lambda q, j, s: (q, 0, j)),
+            pl.BlockSpec((1, 1, step), lambda q, j, s: (q, 0, j)),
+            full_block(rows, width),
+        ),
+        scratch_shapes=[pltpu.VMEM((rows, step), jnp.bfloat16)],
+    )
+    return pl.pallas_call(
+        feed_back_kernel,
+        out_shape=outs,
+        grid_spec=grid_spec,
+        compiler_params=params(),
+        cost_estimate=cost(8 * rows * width * cols * picked, shaped(gdb, turned, *outs) + 12 * rows * cols * picked),
+        name="feed_back",
+    )(quarters, gdb, hidden, pre, turned, down_weight, up_weight)
+
+
+def join_back_kernel(
+    one_ref, two_ref, g_ref, middle_ref, branch_ref, att_ref, weight_ref, gate_ref, scale_ref,
+    grad_middle_ref, grad_att_ref, weight_grad_ref, sums_ref, total_ref,
+):
+    pulled, shift_sum, scale_sum = norm_back(
+        middle_ref[...], one_ref[...] + two_ref[...], scale_ref[...]
+    )
+    grad_middle = g_ref[...] + pulled
+    grad_middle_ref[...] = grad_middle
+    gate_sum = jnp.sum(grad_middle * branch_ref[...], axis=0, keepdims=True)
+    grad_branch = (gate_ref[...] * grad_middle).astype(jnp.bfloat16)
+    grad_att_ref[...] = lax.dot_general(
+        grad_branch, weight_ref[...], CONTRACT_LAST, preferred_element_type=jnp.float32
+    ).astype(jnp.bfloat16)
+    weight_term = lax.dot_general(
+        att_ref[...], grad_branch, CONTRACT_FIRST, preferred_element_type=jnp.float32
+    )
+    sums = jnp.concatenate([shift_sum, scale_sum, gate_sum], axis=0)
+    step = pl.program_id(0)
+
+    @pl.when(step == 0)
+    def _():
+        total_ref[...] = weight_term
+        sums_ref[...] = sums
+
+    @pl.when(step > 0)
+    def _():
+        total_ref[...] += weight_term
+        sums_ref[...] += sums
+
+    @pl.when(step == pl.num_programs(0) - 1)
+    def _():
+        weight_grad_ref[...] = total_ref[...].astype(jnp.bfloat16)
+
+
+def join_back(one, two, g, middle, branch, att, weight, gate, scale):
+    rows, width = g.shape
+    outs = (
+        jax.ShapeDtypeStruct((rows, width), jnp.float32),
+        jax.ShapeDtypeStruct((rows, width), jnp.bfloat16),
+        jax.ShapeDtypeStruct((width, width), jnp.bfloat16),
+        jax.ShapeDtypeStruct((3, width), jnp.float32),
+    )
+    tile = pl.BlockSpec((ROWS, width), lambda i: (i, 0))
+    return pl.pallas_call(
+        join_back_kernel,
+        out_shape=outs,
+        grid=(rows // ROWS,),
+        in_specs=[tile] * 6 + [once_block(width, width)] + [full_block(1, width)] * 2,
+        out_specs=(tile, tile, full_block(width, width), full_block(3, width)),
+        scratch_shapes=[pltpu.VMEM((width, width), jnp.float32)],
+        compiler_params=params(),
+        cost_estimate=cost(4 * rows * width * width, shaped(one, two, g, middle, branch, att, weight, *outs)),
+        name="join_back",
+    )(one, two, g, middle, branch, att, weight, gate, scale)
+
+
+def attend_back_kernel(proj_ref, grad_ref, ublk_ref, place_ref, out_ref, table_ref):
+    count = proj_ref.shape[1]
+    heads = ublk_ref.shape[0]
+    wide = heads * HEAD
+    lane = lax.broadcasted_iota(jnp.int32, (count, 128), 1)
+    place = place_ref[...]
+    fresh = pl.program_id(1) == 0
+
+    @pl.when(fresh)
+    def _():
+        table_ref[...] = jnp.zeros_like(table_ref)
+
+    for pair in range(heads // 2):
+        part = slice(pair * 128, pair * 128 + 128)
+        query = proj_ref[0, :, part]
+        key = proj_ref[0, :, wide + pair * 128 : wide + pair * 128 + 128]
+        value = proj_ref[0, :, 2 * wide + pair * 128 : 2 * wide + pair * 128 + 128]
+        upstream = grad_ref[:, part]
+        turned = (key * HEAD**-0.5).astype(jnp.bfloat16).T
+        kk = jnp.concatenate([key, place], axis=1)
+        halves = []
+        grad_key = jnp.zeros((count, 128), jnp.float32)
+        grad_value = jnp.zeros((count, 128), jnp.float32)
+        for half in range(2):
+            mine = (lane < HEAD) if half == 0 else (lane >= HEAD)
+            scaled = jnp.where(mine, query * HEAD**-0.5, 0.0).astype(jnp.bfloat16)
+            above = jnp.where(mine, upstream, 0.0).astype(jnp.bfloat16)
+            probs = pair_scores(kk, scaled, ublk_ref[2 * pair + half])
+            grad_probs = lax.dot_general(
+                value, above, CONTRACT_LAST, preferred_element_type=jnp.float32
+            )
+            inner = jnp.sum(probs * grad_probs, axis=0, keepdims=True)
+            grad_scores = (probs * (grad_probs - inner)).astype(jnp.bfloat16)
+            both = jnp.dot(
+                grad_scores,
+                jnp.concatenate([scaled, place], axis=1),
+                preferred_element_type=jnp.float32,
+            )
+            grad_key += both[:, :128]
+            table_ref[2 * pair + half] += both[:, 128:]
+            grad_value += jnp.dot(
+                probs.astype(jnp.bfloat16), above, preferred_element_type=jnp.float32
+            )
+            grad_query = jnp.dot(turned, grad_scores, preferred_element_type=jnp.float32)
+            halves.append(grad_query[half * HEAD : half * HEAD + HEAD])
+        out_ref[0, :, part] = jnp.concatenate(halves, axis=0).astype(jnp.bfloat16).T
+        out_ref[0, :, wide + pair * 128 : wide + pair * 128 + 128] = grad_key.astype(jnp.bfloat16)
+        out_ref[0, :, 2 * wide + pair * 128 : 2 * wide + pair * 128 + 128] = grad_value.astype(
+            jnp.bfloat16
+        )
+
+
+def attend_back(proj, grad, ublk, place):
+    quarters, rows, cols = proj.shape
+    count = place.shape[0]
+    heads = ublk.shape[0] // quarters
+    outs = (
+        jax.ShapeDtypeStruct(proj.shape, jnp.bfloat16),
+        jax.ShapeDtypeStruct((ublk.shape[0], count, 128), jnp.float32),
+    )
+    pairs = rows * count * heads * quarters
+    return pl.pallas_call(
+        attend_back_kernel,
+        out_shape=outs,
+        grid=(quarters, rows // count),
+        in_specs=[
+            pl.BlockSpec((1, count, cols), lambda q, w: (q, w, 0)),
+            pl.BlockSpec((count, heads * HEAD), lambda q, w: (w, q)),
+            pl.BlockSpec((heads, count, 128), lambda q, w: (q, 0, 0)),
+            full_block(count, 128),
+        ],
+        out_specs=(
+            pl.BlockSpec((1, count, cols), lambda q, w: (q, w, 0)),
+            pl.BlockSpec((heads, count, 128), lambda q, w: (q, 0, 0)),
+        ),
+        compiler_params=params(),
+        cost_estimate=cost(pairs * 1536, shaped(proj, grad, ublk, *outs), pairs),
+        name="attend_back",
+    )(proj, grad, ublk, place)
+
+
+def in_grad_kernel(list_ref, turned_ref, grad_ref, out_ref):
+    out_ref[0] = jnp.dot(
+        turned_ref[...], grad_ref[0], preferred_element_type=jnp.float32
+    ).astype(jnp.bfloat16)
+
+
+def in_grad(quarters, turned, grad):
+    width, rows = turned.shape
+    cols = grad.shape[2]
+    picked = quarters.shape[0]
+    out = jax.ShapeDtypeStruct((picked, width, cols), jnp.bfloat16)
+    grid_spec = pltpu.PrefetchScalarGridSpec(
+        num_scalar_prefetch=1,
+        grid=(picked, 2),
+        in_specs=[
+            pl.BlockSpec((width // 2, rows), lambda q, j, s: (j, 0)),
+            pl.BlockSpec((1, rows, cols), lambda q, j, s: (s[q], 0, 0)),
+        ],
+        out_specs=pl.BlockSpec((1, width // 2, cols), lambda q, j, s: (q, j, 0)),
+    )
+    return pl.pallas_call(
+        in_grad_kernel,
+        out_shape=out,
+        grid_spec=grid_spec,
+        compiler_params=params(),
+        cost_estimate=cost(2 * rows * width * cols * picked, shaped(turned, out) + 2 * rows * cols * picked),
+        name="in_grad",
+    )(quarters, turned, grad)
+
+
+def project_back_kernel(
+    grad_ref, weight_ref, x_ref, middle_ref, scale_ref, out_ref, sums_ref
+):
+    total = lax.dot_general(
+        grad_ref[0], weight_ref[0], CONTRACT_LAST, preferred_element_type=jnp.float32
+    )
+    for quarter in range(1, grad_ref.shape[0]):
+        total += lax.dot_general(
+            grad_ref[quarter], weight_ref[quarter], CONTRACT_LAST, preferred_element_type=jnp.float32
+        )
+    pulled, shift_sum, scale_sum = norm_back(x_ref[...], total, scale_ref[...])
+    out_ref[...] = middle_ref[...] + pulled
+    sums = jnp.concatenate([shift_sum, scale_sum], axis=0)
+
+    @pl.when(pl.program_id(0) == 0)
+    def _():
+        sums_ref[...] = sums
+
+    @pl.when(pl.program_id(0) > 0)
+    def _():
+        sums_ref[...] += sums
+
+
+def project_back(grad, weight, x, grad_middle, scale):
+    rows, width = x.shape
+    count, _, cols = weight.shape
+    outs = (
+        jax.ShapeDtypeStruct((rows, width), jnp.float32),
+        jax.ShapeDtypeStruct((2, width), jnp.float32),
+    )
+    tile = pl.BlockSpec((ROWS, width), lambda i: (i, 0))
+    return pl.pallas_call(
+        project_back_kernel,
+        out_shape=outs,
+        grid=(rows // ROWS,),
+        in_specs=[
+            pl.BlockSpec((count, ROWS, cols), lambda i: (0, i, 0)),
+            once_block(count, width, cols),
+            tile,
+            tile,
+            full_block(1, width),
+        ],
+        out_specs=(tile, full_block(2, width)),
+        compiler_params=params(),
+        cost_estimate=cost(2 * rows * width * cols * count, shaped(grad, weight, x, grad_middle, *outs)),
+        name="project_back",
+    )(grad, weight, x, grad_middle, scale)
+
+
+SWAP = [(0, 1), (1, 0)]
+
+
+def either(flag, one, two):
+    return jnp.where(flag, one, two)
+
+
+def split_bits(values):
+    parts = []
+    for _ in range(3):
+        part = lax.reduce_precision(values, 8, 7)
+        parts.append(part.astype(jnp.bfloat16))
+        values = values - part
+    return parts
+
+
+def place_maps(layer, frames):
+    extents = window_shape(layer)
+    count = extents[0] * extents[1] * extents[2]
+    place = np.arange(count)
+    positions = (place // (extents[1] * extents[2]), place // extents[2] % extents[1], place % extents[2])
+    hots = []
+    width = sum(e for e in extents if e > 1)
+    levels = sum(2 * e - 1 for e in extents if e > 1)
+    pick = np.zeros((levels, width, width), np.float32)
+    column = base = 0
+    for position, extent in zip(positions, extents):
+        if extent == 1:
+            continue
+        spots = jnp.asarray(position, jnp.int32)
+        if extent == FRAMES and layer == 1:
+            spots = frames[spots]
+        hots.append((spots[:, None] == jnp.arange(extent, dtype=jnp.int32)[None, :]).astype(jnp.float32))
+        for i in range(extent):
+            for j in range(extent):
+                pick[base + i - j + extent - 1, column + i, column + j] = 1
+        column += extent
+        base += 2 * extent - 1
+    return jnp.concatenate(hots, axis=1), pick
+
+
+def bias_blocks(table, hot, pick):
+    pairs = jnp.einsum("hx,xij->hij", table, pick, precision=HIGH)
+    spread = jnp.einsum("ai,hij->haj", hot, pairs, precision=HIGH)
+    parts = split_bits(spread)
+    room = 128 - 3 * hot.shape[1]
+    padded = jnp.concatenate(parts + [jnp.zeros(spread.shape[:2] + (room,), jnp.bfloat16)], axis=2)
+    one = hot.astype(jnp.bfloat16)
+    place = jnp.concatenate([one] * 3 + [jnp.zeros((hot.shape[0], room), jnp.bfloat16)], axis=1)
+    return padded, place
+
+
+def table_grad(acc, hot, pick):
+    width = hot.shape[1]
+    pairs = jnp.einsum("hbi,bj->hij", acc[:, :, :width], hot, precision=HIGH)
+    return jnp.einsum("hij,xij->hx", pairs, pick, precision=HIGH)
+
+
+def per_device_pair(
+    tokens,
+    cotangent,
+    group_start,
+    band_index,
+    class_label,
+    time_table,
+    class_table,
+    modulation_weight,
+    modulation_bias,
+    input_weight,
+    output_weight,
+    space_offsets,
+    time_offsets,
+    up_weight,
+    up_bias,
+    down_weight,
+):
+    core = lax.axis_index("core")
+    side = lax.axis_index("mp")
+    dp = ("chip", "core")
+    low_side = side == 0
+    rows, width = tokens.shape
+    bf16, f32 = jnp.bfloat16, jnp.float32
+
+    def swap_side(value):
+        return lax.ppermute(value, "mp", SWAP)
+
+    def swap_core(value):
+        return lax.ppermute(value, "core", SWAP)
+
+    def half_of(value, axis):
+        size = value.shape[axis] // 2
+        return lax.dynamic_slice_in_dim(value, core * size, size, axis)
+
+    def gather4(value):
+        got = lax.all_gather(value, ("core", "mp"))
+        return got.reshape((4,) + value.shape)
+
+    weights = []
+    for layer in range(2):
+        in_piece = jnp.concatenate(
+            [half_of(input_weight[layer, :, part], 1) for part in range(3)], axis=1
+        )
+        weights.append(
+            (
+                gather4(in_piece),
+                gather4(half_of(output_weight[layer], 0)),
+                gather4(half_of(up_weight[layer], 1)),
+                gather4(half_of(down_weight[layer], 0)),
+            )
+        )
+    heads = space_offsets.shape[0] // 2
+    small_sizes = [heads * space_offsets.shape[1], heads * time_offsets.shape[1], up_bias.shape[1]]
+    small = jnp.concatenate(
+        [half_of(space_offsets, 0).reshape(-1), half_of(time_offsets, 0).reshape(-1), half_of(up_bias, 1).reshape(-1)]
+    )
+    small = gather4(small)
+    cut_one, cut_two = small_sizes[0], small_sizes[0] + small_sizes[1]
+    tables = (
+        small[:, :cut_one].reshape(4 * heads, -1),
+        small[:, cut_one:cut_two].reshape(4 * heads, -1),
+    )
+    biases = small[:, cut_two:].reshape(4, 2, 1, -1)
+
+    marked = jnp.where(group_start > 0, band_index, -1)
+    every = lax.all_gather(marked, dp, tiled=True)
+    mine = lax.axis_index(dp)
+    order = jnp.arange(every.shape[0], dtype=jnp.int32)
+    latest = jnp.max(jnp.where((every >= 0) & (order <= mine), order, -1))
+    current = jnp.sum(jnp.where(order == latest, every, 0)) + jnp.where(latest < 0, -1, 0)
+    band_hot = (current == jnp.arange(time_table.shape[0], dtype=jnp.int32)).astype(f32)
+    class_hot = (class_label[0] == jnp.arange(class_table.shape[0], dtype=jnp.int32)).astype(f32)
+    condition = jnp.sum(band_hot[:, None] * time_table, axis=0) + jnp.sum(
+        class_hot[:, None] * class_table, axis=0
+    )
+    activated = jax.nn.silu(condition).astype(bf16)
+    local_modulation = (
+        jnp.einsum("d,ldcf->lcf", activated, modulation_weight, preferred_element_type=f32)
+        + modulation_bias
+    )
+    modulation = lax.all_gather(local_modulation, "mp", axis=2, tiled=True)
+    every_activated = lax.all_gather(activated, dp)
+
+    split = lax.dynamic_slice_in_dim(tokens, (1 - side) * (rows - ROWS), ROWS, 0).reshape(8, 2, 16, width)
+    kept = lax.dynamic_index_in_dim(split, side, 1, keepdims=False)
+    got = swap_side(lax.dynamic_index_in_dim(split, 1 - side, 1, keepdims=False))
+    shared = jnp.concatenate([either(low_side, kept, got), either(low_side, got, kept)], axis=0)
+    whole = lax.dynamic_slice_in_dim(tokens, side * ROWS, rows - ROWS, 0)
+    whole = whole.reshape(2, 16, 2, 16, width).transpose(0, 2, 1, 3, 4)
+    x = jnp.concatenate([whole.reshape(-1, width), shared.reshape(-1, width)], axis=0).astype(f32)
+
+    chunks = cotangent.reshape(5, ROWS, width)
+    got = swap_side(jnp.stack([chunks[1], chunks[3]]))
+    ordered = jnp.concatenate(
+        [
+            jnp.stack(
+                [
+                    either(low_side, chunks[0], chunks[2]),
+                    either(low_side, chunks[2], chunks[4]),
+                    either(low_side, chunks[4], chunks[0]),
+                ]
+            ),
+            got,
+        ]
+    )
+    g = ordered.reshape(5, 8, 4, 8, width).transpose(2, 0, 1, 3, 4).reshape(rows, width).astype(f32)
+
+    frames = jnp.where(
+        low_side,
+        jnp.asarray([0, 1, 2, 3, 4], jnp.int32),
+        jnp.asarray([3, 4, 2, 0, 1], jnp.int32),
+    )
+    maps = [place_maps(layer, frames) for layer in range(2)]
+    blocks = [bias_blocks(tables[layer], *maps[layer]) for layer in range(2)]
+
+    saved = []
+    for layer in range(2):
+        w_in, w_out, w_up, w_down = weights[layer]
+        w_out = w_out.reshape(width, width)
+        shift_one, scale_one, gate_one, shift_two, scale_two, gate_two = [
+            modulation[layer, number][None] for number in range(6)
+        ]
+        ublk, place = blocks[layer]
+        turned, proj = project(x, shift_one, scale_one, w_in)
+        att = attend(proj, ublk, place)
+        branch, middle, normed_two, turned_two = join(att, w_out, x, gate_one, shift_two, scale_two)
+        pre, hidden = up(normed_two, w_up, biases[:, layer])
+        branch_two, out = down(hidden, w_down, middle, gate_two)
+        saved.append((x, turned, proj, att, branch, middle, turned_two, pre, hidden, branch_two))
+        if layer == 0:
+            parts = out.reshape(5, 2, 128, width)
+            kept = lax.dynamic_index_in_dim(parts, side, 1, keepdims=False)
+            sent = lax.dynamic_index_in_dim(parts, 1 - side, 1, keepdims=False).astype(bf16)
+            got = swap_side(sent).astype(f32)
+            shared = jnp.stack([either(low_side, kept[4], got[4]), either(low_side, got[4], kept[4])])
+            x = jnp.concatenate([kept[:4], shared, got[:4]])
+            x = x.reshape(5, 2, 8, 2, 8, width).transpose(1, 3, 0, 2, 4, 5).reshape(rows, width)
+
+    parts = out.reshape(2, 2, 5, 8, 8, width).transpose(2, 0, 3, 1, 4, 5).reshape(5, 2, 8, 16, width)
+    got = swap_side(parts[3:])
+    pair = jnp.stack([either(low_side, parts[:2], got), either(low_side, got, parts[:2])], axis=2)
+    pair = pair.reshape(2, 2, 16, 16, width).transpose(0, 2, 1, 3, 4).reshape(-1, width)
+    shared = parts[2].transpose(1, 0, 2, 3).reshape(-1, width)
+    result = either(
+        low_side, jnp.concatenate([pair, shared], axis=0), jnp.concatenate([shared, pair], axis=0)
+    )
+
+    here = core * 2
+    there = (1 - core) * 2
+    keep_list = jnp.stack([here + side, here + 1 - side]).astype(jnp.int32)
+    send_list = jnp.stack([there + side, there + 1 - side]).astype(jnp.int32)
+
+    def reduced(send, keep):
+        got = swap_core(send)
+        own = keep[0].astype(f32) + got[0].astype(f32)
+        other = (keep[1].astype(f32) + got[1].astype(f32)).astype(bf16)
+        return (own + swap_side(other).astype(f32)).astype(bf16)
+
+    before = []
+
+    def over_chips(*values):
+        if before:
+            values = lax.optimization_barrier((values, before[-1]))[0]
+        before.append(lax.psum(values, "chip"))
+        return before[-1]
+
+    collected = [None, None]
+    for layer in (1, 0):
+        w_in, w_out, w_up, w_down = weights[layer]
+        w_out = w_out.reshape(width, width)
+        shift_one, scale_one, gate_one, shift_two, scale_two, gate_two = [
+            modulation[layer, number][None] for number in range(6)
+        ]
+        ublk, place = blocks[layer]
+        x, turned, proj, att, branch, middle, turned_two, pre, hidden, branch_two = saved[layer]
+        gdb = (gate_two * g).astype(bf16)
+        gate_two_grad = jnp.sum(g * branch_two, axis=0)
+        down_send, up_send, bias_send, grad_one = feed_back(
+            send_list, gdb, hidden, pre, turned_two, w_down, w_up
+        )
+        down_keep, up_keep, bias_keep, grad_two = feed_back(
+            keep_list, gdb, hidden, pre, turned_two, w_down, w_up
+        )
+        down_sum = reduced(down_send, down_keep)
+        up_sum = reduced(up_send, up_keep)
+        down_sum, up_sum = over_chips(down_sum, up_sum)
+        grad_middle, grad_att, out_grad, sums_two = join_back(
+            grad_one, grad_two, g, middle, branch, att, w_out, gate_one, scale_two
+        )
+        out_pieces = out_grad.reshape(2, 2, -1, width)
+        out_send = lax.dynamic_index_in_dim(out_pieces, 1 - core, 0, keepdims=False)
+        out_keep = lax.dynamic_index_in_dim(out_pieces, core, 0, keepdims=False)
+        out_send = either(low_side, out_send, out_send[::-1])
+        out_keep = either(low_side, out_keep, out_keep[::-1])
+        out_sum = reduced(out_send, out_keep)
+        grad_proj, acc = attend_back(proj, grad_att, ublk, place)
+        in_sum = reduced(in_grad(send_list, turned, grad_proj), in_grad(keep_list, turned, grad_proj))
+        out_sum, in_sum = over_chips(out_sum, in_sum)
+        offset_grad = table_grad(acc, *maps[layer])
+        g, sums_one = project_back(grad_proj, w_in, x, grad_middle, scale_one)
+        table_rows = jnp.stack(
+            [sums_one[0], sums_one[1], sums_two[2], sums_two[0], sums_two[1], gate_two_grad]
+        )
+        if layer == 1:
+            parts = g.reshape(2, 2, 5, 8, 8, width).transpose(2, 0, 3, 1, 4, 5).reshape(5, 2, 128, width)
+            kept = jnp.concatenate(
+                [parts[:2].reshape(4, 128, width), either(low_side, parts[2, 0], parts[2, 1])[None]]
+            )
+            sent = jnp.concatenate(
+                [parts[3:].reshape(4, 128, width), either(low_side, parts[2, 1], parts[2, 0])[None]]
+            )
+            got = swap_side(sent.astype(bf16)).astype(f32)
+            g = jnp.stack([either(low_side, kept, got), either(low_side, got, kept)], axis=1)
+            g = g.reshape(rows, width)
+        bias_rows = jnp.zeros((2, 2, bias_keep.shape[2]), f32)
+        bias_rows = lax.dynamic_update_slice_in_dim(
+            bias_rows, either(low_side, bias_keep[:, 0], bias_keep[::-1, 0])[None], core, 0
+        )
+        bias_rows = lax.dynamic_update_slice_in_dim(
+            bias_rows, either(low_side, bias_send[:, 0], bias_send[::-1, 0])[None], 1 - core, 0
+        )
+        half = width // 2
+        by_side = [
+            jnp.concatenate(
+                [
+                    table_rows[:, s * half : s * half + half].reshape(-1),
+                    offset_grad.reshape(2, 2, -1)[:, s].reshape(-1),
+                    bias_rows[:, s].reshape(-1),
+                ]
+            )
+            for s in range(2)
+        ]
+        summed = either(low_side, by_side[0], by_side[1]) + swap_side(
+            either(low_side, by_side[1], by_side[0])
+        )
+        spread = lax.all_gather(summed, dp)
+        row_part = spread[:, : 6 * half].reshape(-1, 6, half)
+        rest = jnp.sum(spread[:, 6 * half :], axis=0)
+        offsets_size = offset_grad.size // 2
+        offset_sum = rest[:offsets_size].reshape(2 * heads, -1)
+        bias_sum = rest[offsets_size:]
+        weight_rows = jnp.einsum(
+            "vd,vcf->dcf", every_activated.astype(f32), row_part, precision=HIGH
+        )
+        collected[layer] = (
+            weight_rows,
+            jnp.sum(row_part, axis=0),
+            (in_sum, out_sum, up_sum, down_sum),
+            offset_sum,
+            bias_sum,
+        )
+
+    parts = g.reshape(5, 2, 128, width)
+    kept = lax.dynamic_index_in_dim(parts[4], side, 0, keepdims=False).reshape(8, 16, width)
+    sent = lax.dynamic_index_in_dim(parts[4], 1 - side, 0, keepdims=False).reshape(8, 16, width)
+    got = swap_side(sent)
+    shared = jnp.stack([either(low_side, kept, got), either(low_side, got, kept)], axis=1).reshape(-1, width)
+    whole = parts[:4].reshape(2, 2, 16, 16, width).transpose(0, 2, 1, 3, 4).reshape(-1, width)
+    grad_tokens = either(
+        low_side, jnp.concatenate([whole, shared], axis=0), jnp.concatenate([shared, whole], axis=0)
+    )
+
+    first_core = core == 0
+
+    def whole_of(value, axis):
+        other = swap_core(value)
+        return jnp.concatenate(
+            [either(first_core, value, other), either(first_core, other, value)], axis=axis
+        ).astype(f32)
+
+    def pair_of(number, axis, shape=None):
+        both = []
+        for layer in range(2):
+            value = collected[layer][2][number]
+            if shape is not None:
+                value = value.reshape(shape)
+            both.append(whole_of(value, axis))
+        return jnp.stack(both)
+
+    return (
+        result,
+        grad_tokens,
+        jnp.stack([collected[0][0], collected[1][0]]),
+        jnp.stack([collected[0][1], collected[1][1]]),
+        pair_of(0, 2, (width, 3, -1)),
+        pair_of(1, 0),
+        collected[0][3],
+        collected[1][3],
+        pair_of(2, 1),
+        jnp.stack([collected[0][4], collected[1][4]]),
+        pair_of(3, 0),
+    )
+
+
 def solution(mesh):
+    if mesh.shape["mp"] == 2 and mesh.shape["dp"] % 2 == 0:
+        dp, run = ("chip", "core"), per_device_pair
+        mesh = Mesh(mesh.devices.reshape(-1, 2, 2), ("chip", "core", "mp"))
+    else:
+        dp, run = ("dp",), per_device
+    both = dp + ("mp",)
     return jax.shard_map(
-        per_device,
+        run,
         mesh=mesh,
         in_specs=(
-            P(("dp", "mp"), None),
-            P(("dp", "mp"), None),
-            P("dp"),
-            P("dp"),
-            P("dp"),
+            P(both, None),
+            P(both, None),
+            P(dp),
+            P(dp),
+            P(dp),
             P(),
             P(),
             P(None, None, None, "mp"),
@@ -389,8 +1312,8 @@
             P(None, "mp", None),
         ),
         out_specs=(
-            P(("dp", "mp"), None),
-            P(("dp", "mp"), None),
+            P(both, None),
+            P(both, None),
             P(None, None, None, "mp"),
             P(None, None, "mp"),
             P(None, None, None, "mp"),

time: 3010 us -> 1520 us (0.50)
  waiting for transfers between devices: 1660 us -> 536 us
  matrix products: 597 us -> 32.7 us
  Pallas kernels: 0 us -> 547 us
  local copies, waits for them, and re-layouts: 365 us -> 111 us
  other arithmetic: 258 us -> 170 us
    reduce_scatter x10 -> x0, waiting for transfers between devices: 656 us -> none  [the longest x4 478 us: scatter_rows(): lax.psum_scatter(term(jnp.int32(0), count * lax.axis_size('mp')), 'mp', s...]
    dot_general x42 -> x11, matrix products: 583 us -> 32.7 us  [the longest x2 10.2 us: per_device_pair(): jnp.einsum('vd,vcf->dcf', every_activated.astype(f32), row_part, precisio...]
    pallas_call x0 -> x24, Pallas kernels: none -> 547 us  [the longest x4 149 us: feed_back(): pl.pallas_call(feed_back_kernel, out_shape=outs, grid_spec=grid_spec, com...]
    all_gather x8, waiting for transfers between devices: 475 us -> 42.6 us  [gather4(): got = lax.all_gather(value, ('core', 'mp'))]
    psum x1 -> x4, waiting for transfers between devices: 533 us -> 291 us  [over_chips(): before.append(lax.psum(values, 'chip'))]
    another operation x14 -> x8, local copies, waits for them, and re-layouts: 139 us -> 1.02 us  [the longest x1 0.58 us: per_device_pair(): jnp.stack([either(low_side, parts[:2], got), either(low_side, got, parts[...]
    ppermute x0 -> x32, waiting for transfers between devices: none -> 124 us  [the longest x16 124 us: swap_side(): return lax.ppermute(value, 'mp', SWAP)]
    reduce_sum x20 -> x9, other arithmetic: 120 us -> 11.2 us  [the longest x2 9.57 us: per_device_pair(): gate_two_grad = jnp.sum(g * branch_two, axis=0)]
  transfers between devices with their start and end apart: 19 -> 45, of which waited for: 17 -> 13; matrix products, arithmetic and copies ran while one was open for 10% -> 17% of each run, Pallas kernels for 0% -> 23%
where the time goes in v1:
time: 1520 us; the launch traced here: 1510 us
  Pallas kernels  547 us (36%)
  waiting for transfers between devices  536 us (35%)
  other arithmetic  170 us (11%)
  local copies, waits for them, and re-layouts  111 us (7%)
  blocking collectives  68.9 us (5%)
  matrix products  32.7 us (2%)
  between operations  21.3 us (1%)
  starting transfers between devices  21.1 us (1%)
    psum x4, waiting for transfers between devices, over_chips(): before.append(lax.psum(values, 'chip'))  291 us
    pallas_call x4, Pallas kernels, feed_back(): pl.pallas_call(feed_back_kernel, out_shape=outs, grid_spec=grid_spec, com...  149 us
    ppermute x16, waiting for transfers between devices, swap_side(): return lax.ppermute(value, 'mp', SWAP)  124 us
    pallas_call x2, Pallas kernels, attend_back(): pl.pallas_call(attend_back_kernel, out_shape=outs, grid=(quarters, rows /...  89 us
    unnamed x14, waiting for transfers between devices  78 us
    pallas_call x2, Pallas kernels, attend(): pl.pallas_call(attend_kernel, out_shape=out, grid=(quarters, rows // coun...  62.6 us
    pallas_call x2, Pallas kernels, up(): pl.pallas_call(up_kernel, out_shape=outs, grid=(count,), in_specs=[once_b...  45.1 us
    all_gather x8, waiting for transfers between devices, gather4(): got = lax.all_gather(value, ('core', 'mp'))  42.6 us
  transfers between devices with their start and end apart: 45, of which 13 were waited for; matrix products, arithmetic and copies ran while one was open for 17% of the time, Pallas kernels for 23%

profile of v1, /device:TPU:0, one launch (start us, length us, event | category | flops | bytes accessed | tf_op | source)
XLA Modules:
  0.0 1507.9 jit_solution(14413481816676405246)
XLA Ops:
  73.2 28.2 %all-reduce.1 = f32[9808]{0:T(1024)S(1)} all-reduce(f32[9808]{0:T(1024)S(1)} %dynamic-update-slice.1), channel_id=3, replica_groups=mesh['chip'=8,'core'=2,'mp'=2] {'core','mp'}, use_global_device_ids=true, to_apply=%add.1 | all-reduce | flops 9808 | bytes 78464
  135.3 23.0 %all-gather.5 = bf16[16,1,1024]{2,1,0:T(2,128)(2,1)} all-gather(bf16[1,1,1024]{2,1,0:T(2,128)(2,1)S(1)} %convert_bitcast_fusion), channel_id=1, replica_groups=mesh['chip'=8,'core'=2,'mp'=2] {'chip','core'}, dimensions={0}, use_global_device_ids=true | all-gather | bytes 34816 | tf_op jit(solution)/shard_map/all_gather | solution.py:1073
  163.4 15.3 %project.2 = (bf16[1024,1280]{1,0:T(8,128)(2,1)}, bf16[4,1280,768]{2,1,0:T(8,128)(2,1)}) custom-call(f32[1280,1024]{1,0:T(8,128)} %maximum_convert_fusion.3.x_ref, f32[1,1024]{1,0:T(1,128)} %get-tuple-element.285.shift_ref, f32[1,1024]{1,0:T(1,128)} %get-tuple-element.284.scale_ref, bf16[4,1024,768]{2,1,0:T(8,128)(2,1)} %bitcast.419), custom_call_target="tpu_custom_call" | custom-call | flops 8053063680 | bytes 22020096 | tf_op jit(solution)/shard_map/project/pallas_call | solution.py:446
  178.7 30.1 %attend.2.att_ref = bf16[1280,1024]{1,0:T(8,128)(2,1)} custom-call(bf16[4,1280,768]{2,1,0:T(8,128)(2,1)} %get-tuple-element.69.proj_ref, bf16[16,256,128]{2,1,0:T(8,128)(2,1)} %maximum_maximum_fusion.1.ublk_ref, bf16[256,128]{1,0:T(8,128)(2,1)} %maximum_maximum_fusion.3.place_ref), custom_call_target="tpu_custom_call" | custom-call | flops 4026531840 | bytes 11534336 | tf_op jit(solution)/shard_map/attend/pallas_call | solution.py:505
  220.7 22.6 %up.2 = (f32[4,1280,1024]{2,1,0:T(8,128)}, bf16[4,1280,1024]{2,1,0:T(8,128)(2,1)}) custom-call(bf16[1280,1024]{1,0:T(8,128)(2,1)} %get-tuple-element.70.normed_ref, bf16[4,1024,1024]{2,1,0:T(8,128)(2,1)} %all-gather.17.cloned.1.call-done.weight_ref.up_ref, f32[4,1,1024]{2,1,0:T(1,128)} %get-tuple-element.291.bias_ref), custom_call_target="tpu_custom_call" | custom-call | flops 10737418240 | bytes 42467328 | tf_op jit(solution)/shard_map/up/pallas_call | solution.py:577
  243.3 18.4 %down.2 = (f32[1280,1024]{1,0:T(8,128)}, f32[1280,1024]{1,0:T(8,128)}) custom-call(bf16[4,1280,1024]{2,1,0:T(8,128)(2,1)} %get-tuple-element.71.hidden_ref, bf16[4,1024,1024]{2,1,0:T(8,128)(2,1)} %all-gather.19.cloned.1.call-done.weight_ref.down_ref, f32[1280,1024]{1,0:T(8,128)} %get-tuple-element.72.middle_ref, f32[1,1024]{1,0:T(1,128)} %get-tuple-element.273.gate_ref), custom_call_target="tpu_custom_call" | custom-call | flops 10737418240 | bytes 34603008 | tf_op jit(solution)/shard_map/down/pallas_call | solution.py:612
  276.1 29.6 %collective-permute-done.1 = bf16[5,128,1024]{2,1,0:T(8,128)(2,1)S(1)} collective-permute-done((bf16[5,128,1024]{2,1,0:T(8,128)(2,1)S(1)}, bf16[5,128,1024]{2,1,0:T(8,128)(2,1)S(1)}, u32[]{:S(2)}, u32[]{:S(2)}) %collective-permute-start.1) | collective-permute-done | bytes 1310752 | tf_op jit(solution)/shard_map/ppermute | solution.py:1017
  309.9 15.2 %project.3 = (bf16[1024,1280]{1,0:T(8,128)(2,1)}, bf16[4,1280,768]{2,1,0:T(8,128)(2,1)}) custom-call(f32[1280,1024]{1,0:T(8,128)} %bitcast.357, f32[1,1024]{1,0:T(1,128)} %get-tuple-element.279.shift_ref, f32[1,1024]{1,0:T(1,128)} %get-tuple-element.278.scale_ref, bf16[4,1024,768]{2,1,0:T(8,128)(2,1)} %bitcast.421), custom_call_target="tpu_custom_call" | custom-call | flops 8053063680 | bytes 22020096 | tf_op jit(solution)/shard_map/project/pallas_call | solution.py:446
  325.1 32.6 %attend.3.att_ref = bf16[1280,1024]{1,0:T(8,128)(2,1)} custom-call(bf16[4,1280,768]{2,1,0:T(8,128)(2,1)} %get-tuple-element.74.proj_ref, bf16[16,320,128]{2,1,0:T(8,128)(2,1)} %maximum_maximum_fusion.ublk_ref, bf16[320,128]{1,0:T(8,128)(2,1)} %maximum_maximum_fusion.2.place_ref), custom_call_target="tpu_custom_call" | custom-call | flops 5033164800 | bytes 11796480 | tf_op jit(solution)/shard_map/attend/pallas_call | solution.py:505
  374.7 22.5 %up.3 = (f32[4,1280,1024]{2,1,0:T(8,128)}, bf16[4,1280,1024]{2,1,0:T(8,128)(2,1)}) custom-call(bf16[1280,1024]{1,0:T(8,128)(2,1)} %get-tuple-element.75.normed_ref, bf16[4,1024,1024]{2,1,0:T(8,128)(2,1)} %all-gather.23.cloned.1.call-done.weight_ref.up_ref, f32[4,1,1024]{2,1,0:T(1,128)} %get-tuple-element.290.bias_ref), custom_call_target="tpu_custom_call" | custom-call | flops 10737418240 | bytes 42467328 | tf_op jit(solution)/shard_map/up/pallas_call | solution.py:577
  397.2 37.5 %all-gather.25.cloned.1.call-done.weight_ref.down_ref = bf16[4,1024,1024]{2,1,0:T(8,128)(2,1)} async-done(((bf16[1,1024,1024]{2,1,0:T(8,128)(2,1)}), bf16[4,1024,1024]{2,1,0:T(8,128)(2,1)}) %all-gather.25.cloned.1.call-update) | async-done | bytes 8388624 | tf_op jit(solution)/shard_map/all_gather | solution.py:1027
  434.7 17.9 %down.3 = (f32[1280,1024]{1,0:T(8,128)}, f32[1280,1024]{1,0:T(8,128)}) custom-call(bf16[4,1280,1024]{2,1,0:T(8,128)(2,1)} %get-tuple-element.76.hidden_ref, bf16[4,1024,1024]{2,1,0:T(8,128)(2,1)} %all-gather.25.cloned.1.call-done.weight_ref.down_ref, f32[1280,1024]{1,0:T(8,128)} %get-tuple-element.77.middle_ref, f32[1,1024]{1,0:T(1,128)} %get-tuple-element.274.gate_ref), custom_call_target="tpu_custom_call" | custom-call | flops 10737418240 | bytes 34603008 | tf_op jit(solution)/shard_map/down/pallas_call | solution.py:612
  459.4 37.1 %feed_back.4 = (bf16[2,1024,1024]{2,1,0:T(8,128)(2,1)}, bf16[2,1024,1024]{2,1,0:T(8,128)(2,1)}, f32[2,1,1024]{2,1,0:T(1,128)}, f32[1280,1024]{1,0:T(8,128)}) custom-call(s32[2]{0:T(128)} %get-tuple-element.301.list_ref, bf16[1280,1024]{1,0:T(8,128)(2,1)} %get-tuple-element.226.gdb_ref, bf16[4,1280,1024]{2,1,0:T(8,128)(2,1)} %get-tuple-element.76.hidden_ref, ...), custom_call_target="tpu_custom_call" | custom-call | flops 21474836480 | bytes 50339840 | tf_op jit(solution)/shard_map/feed_back/pallas_call | solution.py:706
  496.5 37.3 %feed_back.5 = (bf16[2,1024,1024]{2,1,0:T(8,128)(2,1)}, bf16[2,1024,1024]{2,1,0:T(8,128)(2,1)}, f32[2,1,1024]{2,1,0:T(1,128)}, f32[1280,1024]{1,0:T(8,128)}) custom-call(s32[2]{0:T(128)} %get-tuple-element.302.list_ref, bf16[1280,1024]{1,0:T(8,128)(2,1)} %get-tuple-element.226.gdb_ref, bf16[4,1280,1024]{2,1,0:T(8,128)(2,1)} %get-tuple-element.76.hidden_ref, ...), custom_call_target="tpu_custom_call" | custom-call | flops 21474836480 | bytes 50339840 | tf_op jit(solution)/shard_map/feed_back/pallas_call | solution.py:706
  533.8 19.5 %join_back.2 = (f32[1280,1024]{1,0:T(8,128)}, bf16[1280,1024]{1,0:T(8,128)(2,1)}, bf16[1024,1024]{1,0:T(8,128)(2,1)}, f32[3,1024]{1,0:T(4,128)}) custom-call(f32[1280,1024]{1,0:T(8,128)} %get-tuple-element.81.one_ref, f32[1280,1024]{1,0:T(8,128)} %get-tuple-element.82.two_ref, f32[1280,1024]{1,0:T(8,128)} %bitcast.355, ...), custom_call_target="tpu_custom_call" | custom-call | flops 5368709120 | bytes 40906752 | tf_op jit(solution)/shard_map/join_back/pallas_call | solution.py:760
  553.3 47.8 %attend_back.2 = (bf16[4,1280,768]{2,1,0:T(8,128)(2,1)}, f32[16,320,128]{2,1,0:T(8,128)}) custom-call(bf16[4,1280,768]{2,1,0:T(8,128)(2,1)} %get-tuple-element.74.proj_ref, bf16[1280,1024]{1,0:T(8,128)(2,1)} %get-tuple-element.84.grad_ref, bf16[16,320,128]{2,1,0:T(8,128)(2,1)} %maximum_maximum_fusion.ublk_ref, bf16[320,128]{1,0:T(8,128)(2,1)} %maximum_maximum_fusion.2.place_ref), custom_call_target="tpu_custom_call" | custom-call | flops 10066329600 | bytes 22282240 | tf_op jit(solution)/shard_map/attend_back/pallas_call | solution.py:834
  601.1 16.3 %project_back.2 = (f32[1280,1024]{1,0:T(8,128)}, f32[2,1024]{1,0:T(2,128)}) custom-call(bf16[4,1280,768]{2,1,0:T(8,128)(2,1)} %get-tuple-element.85.grad_ref, bf16[4,1024,768]{2,1,0:T(8,128)(2,1)} %bitcast.422, f32[1280,1024]{1,0:T(8,128)} %bitcast.359, f32[1280,1024]{1,0:T(8,128)} %get-tuple-element.86.middle_ref, f32[1,1024]{1,0:T(1,128)} %get-tuple-element.278.scale_ref), custom_call_target="tpu_custom_call" | custom-call | flops 8053063680 | bytes 29892608 | tf_op jit(solution)/shard_map/project_back/pallas_call | solution.py:915
  669.1 14.6 collective-permute-done.7
  695.7 37.2 %feed_back.6 = (bf16[2,1024,1024]{2,1,0:T(8,128)(2,1)}, bf16[2,1024,1024]{2,1,0:T(8,128)(2,1)}, f32[2,1,1024]{2,1,0:T(1,128)}, f32[1280,1024]{1,0:T(8,128)}) custom-call(s32[2]{0:T(128)} %get-tuple-element.301.list_ref, bf16[1280,1024]{1,0:T(8,128)(2,1)} %get-tuple-element.224.gdb_ref, bf16[4,1280,1024]{2,1,0:T(8,128)(2,1)} %get-tuple-element.71.hidden_ref, ...), custom_call_target="tpu_custom_call" | custom-call | flops 21474836480 | bytes 50339840 | tf_op jit(solution)/shard_map/feed_back/pallas_call | solution.py:706
  741.2 37.4 %feed_back.7 = (bf16[2,1024,1024]{2,1,0:T(8,128)(2,1)}, bf16[2,1024,1024]{2,1,0:T(8,128)(2,1)}, f32[2,1,1024]{2,1,0:T(1,128)}, f32[1280,1024]{1,0:T(8,128)}) custom-call(s32[2]{0:T(128)} %get-tuple-element.302.list_ref, bf16[1280,1024]{1,0:T(8,128)(2,1)} %get-tuple-element.224.gdb_ref, bf16[4,1280,1024]{2,1,0:T(8,128)(2,1)} %get-tuple-element.71.hidden_ref, ...), custom_call_target="tpu_custom_call" | custom-call | flops 21474836480 | bytes 50339840 | tf_op jit(solution)/shard_map/feed_back/pallas_call | solution.py:706
  778.6 19.9 %join_back.3 = (f32[1280,1024]{1,0:T(8,128)}, bf16[1280,1024]{1,0:T(8,128)(2,1)}, bf16[1024,1024]{1,0:T(8,128)(2,1)}, f32[3,1024]{1,0:T(4,128)}) custom-call(f32[1280,1024]{1,0:T(8,128)} %get-tuple-element.90.one_ref, f32[1280,1024]{1,0:T(8,128)} %get-tuple-element.91.two_ref, f32[1280,1024]{1,0:T(8,128)} %bitcast.356, ...), custom_call_target="tpu_custom_call" | custom-call | flops 5368709120 | bytes 40906752 | tf_op jit(solution)/shard_map/join_back/pallas_call | solution.py:760
  804.5 25.0 %collective-permute-done.23 = bf16[1024,1024]{1,0:T(8,128)(2,1)} collective-permute-done((bf16[1024,1024]{1,0:T(8,128)(2,1)S(1)}, bf16[1024,1024]{1,0:T(8,128)(2,1)}, u32[]{:S(2)}, u32[]{:S(2)}) %collective-permute-start.23) | collective-permute-done | bytes 2097184 | tf_op jit(solution)/shard_map/ppermute | solution.py:1017
  834.6 41.2 %attend_back.3 = (bf16[4,1280,768]{2,1,0:T(8,128)(2,1)}, f32[16,256,128]{2,1,0:T(8,128)}) custom-call(bf16[4,1280,768]{2,1,0:T(8,128)(2,1)} %get-tuple-element.69.proj_ref, bf16[1280,1024]{1,0:T(8,128)(2,1)} %get-tuple-element.93.grad_ref, bf16[16,256,128]{2,1,0:T(8,128)(2,1)} %maximum_maximum_fusion.1.ublk_ref, bf16[256,128]{1,0:T(8,128)(2,1)} %maximum_maximum_fusion.3.place_ref), custom_call_target="tpu_custom_call" | custom-call | flops 8053063680 | bytes 21495808 | tf_op jit(solution)/shard_map/attend_back/pallas_call | solution.py:834
  876.0 16.3 %project_back.3 = (f32[1280,1024]{1,0:T(8,128)}, f32[2,1024]{1,0:T(2,128)}) custom-call(bf16[4,1280,768]{2,1,0:T(8,128)(2,1)} %get-tuple-element.94.grad_ref, bf16[4,1024,768]{2,1,0:T(8,128)(2,1)} %bitcast.420, f32[1280,1024]{1,0:T(8,128)} %maximum_convert_fusion.3.x_ref, f32[1280,1024]{1,0:T(8,128)} %get-tuple-element.95.middle_ref, ...), custom_call_target="tpu_custom_call" | custom-call | flops 8053063680 | bytes 29892608 | tf_op jit(solution)/shard_map/project_back/pallas_call | solution.py:915
  932.3 18.7 %collective-permute-done.19 = bf16[1024,768]{1,0:T(8,128)(2,1)} collective-permute-done((bf16[1024,768]{1,0:T(8,128)(2,1)}, bf16[1024,768]{1,0:T(8,128)(2,1)}, u32[]{:S(2)}, u32[]{:S(2)}) %collective-permute-start.19) | collective-permute-done | bytes 1572896 | tf_op jit(solution)/shard_map/ppermute | solution.py:1017
  954.6 37.8 %all-reduce.23.cloned.1.call-done = (bf16[1024,1024]{1,0:T(8,128)(2,1)}, bf16[1024,1024]{1,0:T(8,128)(2,1)}) async-done(((bf16[1024,1024]{1,0:T(8,128)(2,1)}, bf16[1024,1024]{1,0:T(8,128)(2,1)}), (bf16[1024,1024]{1,0:T(8,128)(2,1)}, bf16[1024,1024]{1,0:T(8,128)(2,1)})) %all-reduce.23.cloned.1.call-update) | async-done | bytes 4194320 | tf_op jit(solution)/shard_map/psum | solution.py:1155
  1008.4 77.8 %all-reduce.15.cloned.1.call-done = (f32[86912]{0:T(1024)}, f32[89856]{0:T(1024)}) async-done(((f32[86912]{0:T(1024)}, f32[89856]{0:T(1024)}), (f32[86912]{0:T(1024)}, f32[89856]{0:T(1024)})) %all-reduce.15.cloned.1.call-update) | async-done | bytes 707088
  1101.6 91.5 %all-reduce.21.cloned.1.call-done = (bf16[1024,768]{1,0:T(8,128)(2,1)}, bf16[256,1024]{1,0:T(8,128)(2,1)}) async-done(((bf16[1024,768]{1,0:T(8,128)(2,1)}, bf16[256,1024]{1,0:T(8,128)(2,1)}), (bf16[1024,768]{1,0:T(8,128)(2,1)}, bf16[256,1024]{1,0:T(8,128)(2,1)})) %all-reduce.21.cloned.1.call-update) | async-done | bytes 2097168 | tf_op jit(solution)/shard_map/psum | solution.py:1155
  1229.8 35.1 %collective-permute-done.9 = bf16[256,1024]{1,0:T(8,128)(2,1)S(1)} collective-permute-done((bf16[256,1024]{1,0:T(8,128)(2,1)S(1)}, bf16[256,1024]{1,0:T(8,128)(2,1)S(1)}, u32[]{:S(2)}, u32[]{:S(2)}) %collective-permute-start.9) | collective-permute-done | bytes 524320 | tf_op jit(solution)/shard_map/ppermute | solution.py:1017
  1270.3 83.8 %all-reduce.19.cloned.1.call-done = (bf16[1024,1024]{1,0:T(8,128)(2,1)}, bf16[1024,1024]{1,0:T(8,128)(2,1)}) async-done(((bf16[1024,1024]{1,0:T(8,128)(2,1)}, bf16[1024,1024]{1,0:T(8,128)(2,1)}), (bf16[1024,1024]{1,0:T(8,128)(2,1)}, bf16[1024,1024]{1,0:T(8,128)(2,1)})) %all-reduce.19.cloned.1.call-update) | async-done | bytes 4194320 | tf_op jit(solution)/shard_map/psum | solution.py:1155
  1381.6 77.8 %all-reduce.17.cloned.1.call-done = (bf16[1024,3,256]{0,2,1:T(8,128)(2,1)}, bf16[256,1024]{1,0:T(8,128)(2,1)}) async-done(((bf16[1024,3,256]{0,2,1:T(8,128)(2,1)}, bf16[256,1024]{1,0:T(8,128)(2,1)}), (bf16[1024,3,256]{0,2,1:T(8,128)(2,1)}, bf16[256,1024]{1,0:T(8,128)(2,1)})) %all-reduce.17.cloned.1.call-update) | async-done | bytes 2097168 | tf_op jit(solution)/shard_map/psum | solution.py:1155
  1488.2 12.8 copy.236
  (499 shorter events, 409.0 us)
Async XLA Ops:
  7.2 156.2 %all-gather.27.cloned.1.call-start = ((), (), s32[]{:S(2)}) async-start(), calls=%async_computation.6 | async-start | bytes 7864320 | tf_op jit(solution)/shard_map/all_gather | solution.py:1027
  16.6 192.2 %all-gather.15.cloned.1.call-start = ((), (), s32[]{:S(2)}) async-start(), calls=%async_computation | async-start | bytes 2621440 | tf_op jit(solution)/shard_map/all_gather | solution.py:1027
  20.2 200.5 %all-gather.17.cloned.1.call-start = ((), (), s32[]{:S(2)}) async-start(), calls=%async_computation.1 | async-start | bytes 10485760 | tf_op jit(solution)/shard_map/all_gather | solution.py:1027
  27.1 216.2 %all-gather.19.cloned.1.call-start = ((), (), s32[]{:S(2)}) async-start(), calls=%async_computation.2 | async-start | bytes 10485760 | tf_op jit(solution)/shard_map/all_gather | solution.py:1027
  35.9 274.0 %all-gather.29.cloned.1.call-start = ((), (), s32[]{:S(2)}) async-start(), calls=%async_computation.7 | async-start | bytes 7864320 | tf_op jit(solution)/shard_map/all_gather | solution.py:1027
  39.7 318.0 %all-gather.21.cloned.1.call-start = ((), (), s32[]{:S(2)}) async-start(), calls=%async_computation.3 | async-start | bytes 2621440 | tf_op jit(solution)/shard_map/all_gather | solution.py:1027
  41.6 333.1 %all-gather.23.cloned.1.call-start = ((), (), s32[]{:S(2)}) async-start(), calls=%async_computation.4 | async-start | bytes 10485760 | tf_op jit(solution)/shard_map/all_gather | solution.py:1027
  44.8 389.9 %all-gather.25.cloned.1.call-start = ((), (), s32[]{:S(2)}) async-start(), calls=%async_computation.5 | async-start | bytes 10485760 | tf_op jit(solution)/shard_map/all_gather | solution.py:1027
  45.7 114.7 %collective-permute-start = (bf16[8,16,1024]{2,1,0:T(8,128)(2,1)}, bf16[8,16,1024]{2,1,0:T(8,128)(2,1)S(1)}, u32[]{:S(2)}, u32[]{:S(2)}) collective-permute-start(bf16[8,16,1024]{2,1,0:T(8,128)(2,1)} %dynamic-slice_bitcast_fusion.12), channel_id=1, source_target_pairs={{0,1},{1,0},{2,3},{3,2},{4,5},{5,4},{6,7},{7,6},{8,9},{9,8},{10,11... | collective-permute-start | bytes 786440 | tf_op jit(solution)/shard_map/ppermute | solution.py:1017
  51.9 220.1 %collective-permute-start.3 = (bf16[2,256,1024]{2,1,0:T(8,128)(2,1)}, bf16[2,256,1024]{2,1,0:T(8,128)(2,1)}, u32[]{:S(2)}, u32[]{:S(2)}) collective-permute-start(bf16[2,256,1024]{2,1,0:T(8,128)(2,1)} %pad_maximum_fusion.9), channel_id=1, source_target_pairs={{0,1},{1,0},{2,3},{3,2},{4,5},{5,4},{6,7},{7,6},{8,9},{9,8},{10,11... | collective-permute-start | bytes 3145736 | tf_op jit(solution)/shard_map/ppermute | solution.py:1017
  53.5 939.0 %all-reduce.23.cloned.1.call-start = ((), (), s32[]{:S(2)}) async-start(), calls=%async_computation.12 | async-start | bytes 8388608 | tf_op jit(solution)/shard_map/psum | solution.py:1155
  662.2 70.9 %collective-permute-start.20 = (bf16[2,1024,1024]{2,1,0:T(8,128)(2,1)}, bf16[2,1024,1024]{2,1,0:T(8,128)(2,1)}, u32[]{:S(2)}, u32[]{:S(2)}) collective-permute-start(bf16[2,1024,1024]{2,1,0:T(8,128)(2,1)} %get-tuple-element.118), channel_id=1, source_target_pairs={{0,2},{2,0},{1,3},{3,1},{4,6},{6,4},{5,7},{7,5},{8,10},{10,8},{9,1... | collective-permute-start | bytes 12582920 | tf_op jit(solution)/shard_map/ppermute | solution.py:1020
  662.5 75.8 %collective-permute-start.22 = (bf16[2,1024,1024]{2,1,0:T(8,128)(2,1)}, bf16[2,1024,1024]{2,1,0:T(8,128)(2,1)}, u32[]{:S(2)}, u32[]{:S(2)}) collective-permute-start(bf16[2,1024,1024]{2,1,0:T(8,128)(2,1)} %get-tuple-element.120), channel_id=1, source_target_pairs={{0,2},{2,0},{1,3},{3,1},{4,6},{6,4},{5,7},{7,5},{8,10},{10,8},{9,1... | collective-permute-start | bytes 12582920 | tf_op jit(solution)/shard_map/ppermute | solution.py:1020
  683.7 226.7 %collective-permute-start.18 = (bf16[2,1024,768]{2,1,0:T(8,128)(2,1)}, bf16[2,1024,768]{2,1,0:T(8,128)(2,1)}, u32[]{:S(2)}, u32[]{:S(2)}) collective-permute-start(bf16[2,1024,768]{2,1,0:T(8,128)(2,1)} %in_grad.7), channel_id=1, source_target_pairs={{0,2},{2,0},{1,3},{3,1},{4,6},{6,4},{5,7},{7,5},{8,10},{10,8},{9,1... | collective-permute-start | bytes 9437192 | tf_op jit(solution)/shard_map/ppermute | solution.py:1020
  686.3 231.5 %collective-permute-start.17 = (bf16[256,1024]{1,0:T(8,128)(2,1)}, bf16[256,1024]{1,0:T(8,128)(2,1)}, u32[]{:S(2)}, u32[]{:S(2)}) collective-permute-start(bf16[256,1024]{1,0:T(8,128)(2,1)} %fusion.26), channel_id=1, source_target_pairs={{0,1},{1,0},{2,3},{3,2},{4,5},{5,4},{6,7},{7,6},{8,9},{9,8},{10,11... | collective-permute-start | bytes 1572872 | tf_op jit(solution)/shard_map/ppermute | solution.py:1017
  732.9 188.5 %collective-permute-start.12 = (bf16[2,1024,1024]{2,1,0:T(8,128)(2,1)}, bf16[2,1024,1024]{2,1,0:T(8,128)(2,1)}, u32[]{:S(2)}, u32[]{:S(2)}) collective-permute-start(bf16[2,1024,1024]{2,1,0:T(8,128)(2,1)} %get-tuple-element.112), channel_id=1, source_target_pairs={{0,2},{2,0},{1,3},{3,1},{4,6},{6,4},{5,7},{7,5},{8,10},{10,8},{9,1... | collective-permute-start | bytes 12582920 | tf_op jit(solution)/shard_map/ppermute | solution.py:1020
  736.5 62.1 %collective-permute-start.21 = (bf16[1024,1024]{1,0:T(8,128)(2,1)S(1)}, bf16[1024,1024]{1,0:T(8,128)(2,1)}, u32[]{:S(2)}, u32[]{:S(2)}) collective-permute-start(bf16[1024,1024]{1,0:T(8,128)(2,1)S(1)} %fusion.16), channel_id=1, source_target_pairs={{0,1},{1,0},{2,3},{3,2},{4,5},{5,4},{6,7},{7,6},{8,9},{9,8},{10,11... | collective-permute-start | bytes 6291464 | tf_op jit(solution)/shard_map/ppermute | solution.py:1017
  740.8 88.7 %collective-permute-start.23 = (bf16[1024,1024]{1,0:T(8,128)(2,1)S(1)}, bf16[1024,1024]{1,0:T(8,128)(2,1)}, u32[]{:S(2)}, u32[]{:S(2)}) collective-permute-start(bf16[1024,1024]{1,0:T(8,128)(2,1)S(1)} %fusion.17), channel_id=1, source_target_pairs={{0,1},{1,0},{2,3},{3,2},{4,5},{5,4},{6,7},{7,6},{8,9},{9,8},{10,11... | collective-permute-start | bytes 6291464 | tf_op jit(solution)/shard_map/ppermute | solution.py:1017
  834.5 251.7 %all-reduce.15.cloned.1.call-start = ((), (), s32[]{:S(2)}) async-start(), calls=%async_computation.8 | async-start | bytes 1417216
  915.6 309.6 %collective-permute-start.2 = (f32[2,2,8,16,1024]{4,3,2,1,0:T(8,128)}, f32[2,2,8,16,1024]{4,3,2,1,0:T(8,128)}, u32[]{:S(2)}, u32[]{:S(2)}) collective-permute-start(f32[2,2,8,16,1024]{4,3,2,1,0:T(8,128)} %slice_bitcast_fusion), channel_id=1, source_target_pairs={{0,1},{1,0},{2,3},{3,2},{4,5},{5,4},{6,7},{7,6},{8,9},{9,8},{10,11... | collective-permute-start | bytes 6291464 | tf_op jit(solution)/shard_map/ppermute | solution.py:1017
  917.6 275.4 %all-reduce.21.cloned.1.call-start = ((), (), s32[]{:S(2)}) async-start(), calls=%async_computation.11 | async-start | bytes 4194304 | tf_op jit(solution)/shard_map/psum | solution.py:1155
  917.8 301.5 %collective-permute-start.5 = (f32[8,16,1024]{2,1,0:T(8,128)}, f32[8,16,1024]{2,1,0:T(8,128)S(1)}, u32[]{:S(2)}, u32[]{:S(2)}) collective-permute-start(f32[8,16,1024]{2,1,0:T(8,128)} %bitcast.404), channel_id=1, source_target_pairs={{0,1},{1,0},{2,3},{3,2},{4,5},{5,4},{6,7},{7,6},{8,9},{9,8},{10,11... | collective-permute-start | bytes 1572872 | tf_op jit(solution)/shard_map/ppermute | solution.py:1017
  926.2 162.6 %collective-permute-start.13 = (bf16[1024,1024]{1,0:T(8,128)(2,1)}, bf16[1024,1024]{1,0:T(8,128)(2,1)}, u32[]{:S(2)}, u32[]{:S(2)}) collective-permute-start(bf16[1024,1024]{1,0:T(8,128)(2,1)} %fusion.14), channel_id=1, source_target_pairs={{0,1},{1,0},{2,3},{3,2},{4,5},{5,4},{6,7},{7,6},{8,9},{9,8},{10,11... | collective-permute-start | bytes 6291464 | tf_op jit(solution)/shard_map/ppermute | solution.py:1017
  931.3 165.2 %collective-permute-start.15 = (bf16[1024,1024]{1,0:T(8,128)(2,1)}, bf16[1024,1024]{1,0:T(8,128)(2,1)}, u32[]{:S(2)}, u32[]{:S(2)}) collective-permute-start(bf16[1024,1024]{1,0:T(8,128)(2,1)} %fusion.15), channel_id=1, source_target_pairs={{0,1},{1,0},{2,3},{3,2},{4,5},{5,4},{6,7},{7,6},{8,9},{9,8},{10,11... | collective-permute-start | bytes 6291464 | tf_op jit(solution)/shard_map/ppermute | solution.py:1017
  992.5 361.6 %all-reduce.19.cloned.1.call-start = ((), (), s32[]{:S(2)}) async-start(), calls=%async_computation.10 | async-start | bytes 8388608 | tf_op jit(solution)/shard_map/psum | solution.py:1155
  998.6 216.9 %collective-permute-start.10 = (bf16[2,1024,768]{2,1,0:T(8,128)(2,1)}, bf16[2,1024,768]{2,1,0:T(8,128)(2,1)}, u32[]{:S(2)}, u32[]{:S(2)}) collective-permute-start(bf16[2,1024,768]{2,1,0:T(8,128)(2,1)} %in_grad.5), channel_id=1, source_target_pairs={{0,2},{2,0},{1,3},{3,1},{4,6},{6,4},{5,7},{7,5},{8,10},{10,8},{9,1... | collective-permute-start | bytes 9437192 | tf_op jit(solution)/shard_map/ppermute | solution.py:1020
  1088.8 130.8 %collective-permute-start.8 = (bf16[2,256,1024]{2,1,0:T(8,128)(2,1)}, bf16[2,256,1024]{2,1,0:T(8,128)(2,1)}, u32[]{:S(2)}, u32[]{:S(2)}) collective-permute-start(bf16[2,256,1024]{2,1,0:T(8,128)(2,1)} %reverse_select_fusion.2), channel_id=1, source_target_pairs={{0,2},{2,0},{1,3},{3,1},{4,6},{6,4},{5,7},{7,5},{8,10},{10,8},{9,1... | collective-permute-start | bytes 3145736 | tf_op jit(solution)/shard_map/ppermute | solution.py:1020
  1193.0 266.4 %all-reduce.17.cloned.1.call-start = ((), (), s32[]{:S(2)}) async-start(), calls=%async_computation.9 | async-start | bytes 4194304 | tf_op jit(solution)/shard_map/psum | solution.py:1155
  1221.7 147.7 %collective-permute-start.29 = (bf16[1024,1024]{1,0:T(8,128)(2,1)}, bf16[1024,1024]{1,0:T(8,128)(2,1)}, u32[]{:S(2)}, u32[]{:S(2)}) collective-permute-start(bf16[1024,1024]{1,0:T(8,128)(2,1)} %get-tuple-element.206), channel_id=1, source_target_pairs={{0,2},{2,0},{1,3},{3,1},{4,6},{6,4},{5,7},{7,5},{8,10},{10,8},{9,1... | collective-permute-start | bytes 6291464 | tf_op jit(solution)/shard_map/ppermute | solution.py:1020
  1224.7 149.7 %collective-permute-start.31 = (bf16[1024,1024]{1,0:T(8,128)(2,1)}, bf16[1024,1024]{1,0:T(8,128)(2,1)}, u32[]{:S(2)}, u32[]{:S(2)}) collective-permute-start(bf16[1024,1024]{1,0:T(8,128)(2,1)} %get-tuple-element.205), channel_id=1, source_target_pairs={{0,2},{2,0},{1,3},{3,1},{4,6},{6,4},{5,7},{7,5},{8,10},{10,8},{9,1... | collective-permute-start | bytes 6291464 | tf_op jit(solution)/shard_map/ppermute | solution.py:1020
  1354.1 105.8 %collective-permute-start.28 = (bf16[1024,1024]{1,0:T(8,128)(2,1)}, bf16[1024,1024]{1,0:T(8,128)(2,1)}, u32[]{:S(2)}, u32[]{:S(2)}) collective-permute-start(bf16[1024,1024]{1,0:T(8,128)(2,1)} %get-tuple-element.202), channel_id=1, source_target_pairs={{0,2},{2,0},{1,3},{3,1},{4,6},{6,4},{5,7},{7,5},{8,10},{10,8},{9,1... | collective-permute-start | bytes 6291464 | tf_op jit(solution)/shard_map/ppermute | solution.py:1020
  1373.9 95.5 %collective-permute-start.30 = (bf16[1024,1024]{1,0:T(8,128)(2,1)}, bf16[1024,1024]{1,0:T(8,128)(2,1)}, u32[]{:S(2)}, u32[]{:S(2)}) collective-permute-start(bf16[1024,1024]{1,0:T(8,128)(2,1)} %get-tuple-element.201), channel_id=1, source_target_pairs={{0,2},{2,0},{1,3},{3,1},{4,6},{6,4},{5,7},{7,5},{8,10},{10,8},{9,1... | collective-permute-start | bytes 6291464 | tf_op jit(solution)/shard_map/ppermute | solution.py:1020
  (101 other events, 1502.0 us)
Sparse Core Ops, SparseCore 0:
  16.7 64.3 all-gather.26
  82.6 23.8 all-gather.14
  108.7 58.8 all-gather.16
  169.5 58.2 all-gather.18
  229.3 53.4 all-gather.28
  284.2 30.6 all-gather.20
  316.4 58.2 all-gather.22
  376.3 58.3 all-gather.24
  834.7 157.7 all-reduce.22
  995.8 90.3 all-reduce.14
  1090.3 102.6 all-reduce.20
  1197.6 156.4 all-reduce.18
  1358.2 101.1 all-reduce.16

commit v2 on v0

--- a/solution.py
+++ b/solution.py
@@ -1,6 +1,12 @@
+import functools
+
 import jax
 import jax.numpy as jnp
+import numpy as np
 from jax import lax
+from jax.experimental import pallas as pl
+from jax.experimental.pallas import tpu as pltpu
+from jax.sharding import Mesh
 from jax.sharding import PartitionSpec as P
 
 FRAMES = 5
@@ -366,16 +372,1273 @@
     )
 
 
+VMEM = 58 * 2**20
+COST_SHARE = 64
+ROWS = 256
+HEAD = 64
+
+
+def full_block(*shape):
+    return pl.BlockSpec(shape, lambda *_: (0,) * len(shape))
+
+
+def once_block(*shape):
+    return pl.BlockSpec(shape, lambda *_: (0,) * len(shape), pipeline_mode=pl.Buffered(1))
+
+
+def params():
+    return pltpu.CompilerParams(vmem_limit_bytes=VMEM)
+
+
+def cost(flops, moved, exps=0):
+    return pl.CostEstimate(
+        flops=int(flops) // COST_SHARE,
+        bytes_accessed=int(moved) // COST_SHARE,
+        transcendentals=int(exps) // COST_SHARE,
+    )
+
+
+def shaped(*arrays):
+    return sum(int(np.prod(a.shape)) * a.dtype.itemsize for a in arrays)
+
+
+def row_norm(values):
+    centred = values - jnp.mean(values, axis=-1, keepdims=True)
+    spread = jnp.mean(centred * centred, axis=-1, keepdims=True)
+    scale = lax.rsqrt(spread + EPSILON)
+    return centred * scale, scale
+
+
+def norm_back(values, grad, shift_scale):
+    unit, inverse = row_norm(values)
+    inner = grad * (1.0 + shift_scale)
+    first = jnp.mean(inner, axis=-1, keepdims=True)
+    second = jnp.mean(inner * unit, axis=-1, keepdims=True)
+    pulled = inverse * (inner - first - unit * second)
+    return (
+        pulled,
+        jnp.sum(grad, axis=0, keepdims=True),
+        jnp.sum(grad * unit, axis=0, keepdims=True),
+    )
+
+
+def call(kernel, name, grid, in_specs, out_specs, out_shape, flops, exps=0, scratch=()):
+    def run(spots, *operands):
+        moved = shaped(*operands, *jax.tree.leaves(out_shape))
+        return pl.pallas_call(
+            kernel,
+            out_shape=out_shape,
+            grid_spec=pltpu.PrefetchScalarGridSpec(
+                num_scalar_prefetch=1,
+                grid=grid,
+                in_specs=in_specs,
+                out_specs=out_specs,
+                scratch_shapes=scratch,
+            ),
+            compiler_params=params(),
+            cost_estimate=cost(flops, min(moved, 64 * 2**20), exps),
+            name=name,
+        )(spots, *operands)
+
+    return run
+
+
+def project_kernel(_, x_ref, shift_ref, scale_ref, weight_ref, turned_ref, normed_ref, out_ref):
+    rows = x_ref.shape[0]
+
+    @pl.when(pl.program_id(0) == 0)
+    def _():
+        for start in range(0, rows, ROWS):
+            part = pl.ds(start, ROWS)
+            unit, _ = row_norm(x_ref[part, :])
+            value = (unit * (1.0 + scale_ref[...]) + shift_ref[...]).astype(jnp.bfloat16)
+            normed_ref[part, :] = value
+            turned_ref[:, part] = value.T
+
+    project_rows(normed_ref, weight_ref, out_ref)
+
+
+def side_by_side(ref):
+    return jnp.concatenate([ref[0, part] for part in range(3)], axis=1)
+
+
+def project_more_kernel(_, normed_ref, mine_ref, sib_ref, out_ref):
+    @pl.when(pl.program_id(0) == 0)
+    def _():
+        project_rows(normed_ref, mine_ref, out_ref)
+
+    @pl.when(pl.program_id(0) == 1)
+    def _():
+        project_rows(normed_ref, sib_ref, out_ref)
+
+
+def project_rows(normed_ref, weight_ref, out_ref):
+    weight = side_by_side(weight_ref)
+    for start in range(0, normed_ref.shape[0], ROWS):
+        part = pl.ds(start, ROWS)
+        out_ref[0, part, :] = jnp.dot(
+            normed_ref[part, :], weight, preferred_element_type=jnp.float32
+        ).astype(jnp.bfloat16)
+
+
+def in_spec(layer, width, cols, order):
+    return pl.BlockSpec((1, 3, width, cols // 3), lambda *a: (layer, 0, 0, a[-1][order(*a[:-1])]))
+
+
+def project(spots, layer, x, shift, scale, weight):
+    rows, width = x.shape
+    cols = 3 * weight.shape[3] // 2
+    return call(
+        project_kernel,
+        "project",
+        (2,),
+        [
+            once_block(rows, width),
+            full_block(1, width),
+            full_block(1, width),
+            in_spec(layer, width, cols, lambda q: q),
+        ],
+        (
+            full_block(width, rows),
+            full_block(rows, width),
+            pl.BlockSpec((1, rows, cols), lambda q, s: (q, 0, 0)),
+        ),
+        (
+            jax.ShapeDtypeStruct((width, rows), jnp.bfloat16),
+            jax.ShapeDtypeStruct((rows, width), jnp.bfloat16),
+            jax.ShapeDtypeStruct((2, rows, cols), jnp.bfloat16),
+        ),
+        4 * rows * width * cols,
+    )(spots, x, shift, scale, weight)
+
+
+def project_more(spots, normed, mine, sib):
+    rows, width = normed.shape
+    size = mine.shape[2]
+    return call(
+        project_more_kernel,
+        "project_more",
+        (2,),
+        [once_block(rows, width), full_block(1, 3, width, size), full_block(1, 3, width, size)],
+        pl.BlockSpec((1, rows, 3 * size), lambda q, s: (q, 0, 0)),
+        jax.ShapeDtypeStruct((2, rows, 3 * size), jnp.bfloat16),
+        12 * rows * width * size,
+    )(spots, normed, mine[None], sib[None])
+
+
+def window_heads(proj_ref, ublk_ref, place, extra_ref=None):
+    count = place.shape[0]
+    heads = ublk_ref.shape[0]
+    wide = heads * HEAD
+    lane = lax.broadcasted_iota(jnp.int32, (count, 128), 1)
+    items = []
+    for window in range(proj_ref.shape[1] // count):
+        rows = pl.ds(window * count, count)
+        for pair in range(heads // 2):
+            cols = pl.ds(pair * 128, 128)
+            query, key, value = (
+                proj_ref[0, rows, part * wide + pair * 128 : part * wide + pair * 128 + 128]
+                for part in range(3)
+            )
+            kk = jnp.concatenate([key, place], axis=1)
+            for half in range(2):
+                mine = (lane < HEAD) if half == 0 else (lane >= HEAD)
+                scaled = jnp.where(mine, query * HEAD**-0.5, 0.0).astype(jnp.bfloat16)
+                above = None
+                if extra_ref is not None:
+                    above = jnp.where(mine, extra_ref[rows, cols], 0.0).astype(jnp.bfloat16)
+                items.append((rows, pair, 2 * pair + half, kk, key, value, scaled, above))
+    return items, lane
+
+
+def head_scores(item, ublk_ref):
+    query = jnp.concatenate([item[6], ublk_ref[item[2]]], axis=1)
+    return lax.dot_general(item[3], query, CONTRACT_LAST, preferred_element_type=jnp.float32)
+
+
+def head_probs(scores):
+    expo = jnp.exp(scores - jnp.max(scores, axis=0, keepdims=True))
+    return expo * (1.0 / jnp.sum(expo, axis=0, keepdims=True))
+
+
+def ahead(items, first, middle, last):
+    ready, count = first(items[0]), len(items)
+    held = None
+    for i in range(count):
+        later = first(items[i + 1]) if i + 1 < count else None
+        now = middle(ready)
+        if i > 0:
+            last(i - 1, held)
+        ready, held = later, now
+    last(count - 1, held)
+
+
+def attend_kernel(_, proj_ref, ublk_ref, place_ref, out_ref):
+    items, lane = window_heads(proj_ref, ublk_ref, place_ref[...])
+    done = []
+
+    def mix(i, probs):
+        rows, pair, value = items[i][0], items[i][1], items[i][5]
+        done.append(
+            lax.dot_general(probs, value, CONTRACT_FIRST, preferred_element_type=jnp.float32)
+        )
+        if i % 2:
+            out_ref[rows, pair * 128 : pair * 128 + 128] = jnp.where(
+                lane < HEAD, done[i - 1], done[i]
+            ).astype(jnp.bfloat16)
+
+    ahead(
+        items,
+        lambda item: head_scores(item, ublk_ref),
+        lambda scores: head_probs(scores).astype(jnp.bfloat16),
+        mix,
+    )
+
+
+def attend(spots, first, proj, ublk, place):
+    quarters, rows, cols = proj.shape
+    count = place.shape[0]
+    heads = ublk.shape[0] // 4
+    pairs = rows * count * heads * quarters
+    return call(
+        attend_kernel,
+        "attend",
+        (quarters,),
+        [
+            pl.BlockSpec((1, rows, cols), lambda q, s: (q, 0, 0)),
+            pl.BlockSpec((heads, count, 128), lambda q, s: (first + s[q], 0, 0)),
+            full_block(count, 128),
+        ],
+        pl.BlockSpec((rows, heads * HEAD), lambda q, s: (0, q)),
+        jax.ShapeDtypeStruct((rows, quarters * heads * HEAD), jnp.bfloat16),
+        pairs * 768,
+        pairs,
+    )(spots, proj, ublk, place)
+
+
+def join_kernel(
+    _, own_ref, far_ref, w0_ref, w1_ref, w2_ref, w3_ref, x_ref, gate_ref, shift_ref, scale_ref,
+    branch_ref, middle_ref, normed_ref, turned_ref,
+):
+    weights = [w0_ref[0], w1_ref[0], w2_ref[...], w3_ref[...]]
+    branch = jnp.dot(
+        jnp.concatenate([own_ref[...], far_ref[...]], axis=1),
+        jnp.concatenate(weights, axis=0),
+        preferred_element_type=jnp.float32,
+    )
+    branch_ref[...] = branch
+    middle = x_ref[...] + gate_ref[...] * branch
+    middle_ref[...] = middle
+    unit, _ = row_norm(middle)
+    normed = (unit * (1.0 + scale_ref[...]) + shift_ref[...]).astype(jnp.bfloat16)
+    normed_ref[...] = normed
+    turned_ref[...] = normed.T
+
+
+def row_tile(cols):
+    return pl.BlockSpec((ROWS, cols), lambda i, s: (i, 0))
+
+
+def quarter_rows(layer, r, size, width):
+    return pl.BlockSpec(
+        (1, size, width), lambda i, s: (layer, s[r], 0), pipeline_mode=pl.Buffered(1)
+    )
+
+
+def join(spots, layer, own, far, weight, recv, sib, x, gate, shift, scale):
+    rows, width = x.shape
+    half = own.shape[1]
+    tile = row_tile(width)
+    size = half // 2
+    return call(
+        join_kernel,
+        "join",
+        (rows // ROWS,),
+        [
+            row_tile(half),
+            row_tile(half),
+            quarter_rows(layer, 0, size, width),
+            quarter_rows(layer, 1, size, width),
+            once_block(size, width),
+            once_block(size, width),
+            tile,
+        ]
+        + [full_block(1, width)] * 3,
+        (tile, tile, tile, pl.BlockSpec((width, ROWS), lambda i, s: (0, i))),
+        (
+            jax.ShapeDtypeStruct((rows, width), jnp.float32),
+            jax.ShapeDtypeStruct((rows, width), jnp.float32),
+            jax.ShapeDtypeStruct((rows, width), jnp.bfloat16),
+            jax.ShapeDtypeStruct((width, rows), jnp.bfloat16),
+        ),
+        2 * rows * width * width,
+    )(spots, own, far, weight, weight, recv, sib, x, gate, shift, scale)
+
+
+SLOPE = float(np.sqrt(2 / np.pi))
+
+
+def up_kernel(_, normed_ref, weight_ref, bias_ref, pre_ref, hidden_ref):
+    starts = list(range(0, normed_ref.shape[0], ROWS))
+
+    def product(start):
+        return (
+            jnp.dot(
+                normed_ref[pl.ds(start, ROWS), :], weight_ref[0], preferred_element_type=jnp.float32
+            )
+            + bias_ref[0, 0]
+        )
+
+    pre = product(starts[0])
+    for start, following in zip(starts, starts[1:] + [None]):
+        later = None if following is None else product(following)
+        part = pl.ds(start, ROWS)
+        pre_ref[0, part, :] = pre
+        bent = jnp.tanh(pre * (SLOPE + (SLOPE * 0.044715) * (pre * pre)))
+        half = 0.5 * pre
+        hidden_ref[0, part, :] = (half + half * bent).astype(jnp.bfloat16)
+        pre = later
+
+
+def up_spec(layer, own, width, cols, step, order):
+    if own:
+        per = cols // step
+        return pl.BlockSpec(
+            (1, width, step), lambda *a: (layer, 0, a[-1][order(*a[:-1])[0]] * per + order(*a[:-1])[1])
+        )
+    return pl.BlockSpec((1, width, step), lambda *a: (0, 0, order(*a[:-1])[1]))
+
+
+def up(spots, layer, quarter, normed, weight, bias):
+    rows, width = normed.shape
+    cols = bias.shape[3]
+    step = cols // 2
+    own = quarter is None
+    count = 2 if own else 1
+    tile = pl.BlockSpec((1, rows, step), lambda q, j, s: (q, 0, j))
+    return call(
+        up_kernel,
+        "up",
+        (count, cols // step),
+        [
+            once_block(rows, width),
+            up_spec(layer, own, width, cols, step, lambda q, j: (q, j)),
+            pl.BlockSpec((1, 1, 1, step), lambda q, j, s: (layer, s[q if own else quarter], 0, j)),
+        ],
+        (tile, tile),
+        (
+            jax.ShapeDtypeStruct((count, rows, cols), jnp.float32),
+            jax.ShapeDtypeStruct((count, rows, cols), jnp.bfloat16),
+        ),
+        2 * count * rows * width * cols,
+        count * rows * cols,
+    )(spots, normed, weight if own else weight[None], bias)
+
+
+def down_kernel(
+    _, own_ref, far_ref, sib_ref, w0_ref, w1_ref, w2_ref, w3_ref, middle_ref, gate_ref, branch_ref, out_ref
+):
+    total = jnp.dot(own_ref[0], w0_ref[0], preferred_element_type=jnp.float32)
+    total += jnp.dot(own_ref[1], w1_ref[0], preferred_element_type=jnp.float32)
+    total += jnp.dot(far_ref[0], w2_ref[...], preferred_element_type=jnp.float32)
+    total += jnp.dot(sib_ref[0], w3_ref[...], preferred_element_type=jnp.float32)
+    branch_ref[...] = total
+    out_ref[...] = middle_ref[...] + gate_ref[...] * total
+
+
+def down(spots, layer, own, far, far_sib, weight, recv, sib, middle, gate):
+    rows, width = middle.shape
+    cols = own.shape[2]
+    tile = row_tile(width)
+    hidden, single = (pl.BlockSpec((n, ROWS, cols), lambda i, s: (0, i, 0)) for n in (2, 1))
+    return call(
+        down_kernel,
+        "down",
+        (rows // ROWS,),
+        [
+            hidden,
+            single,
+            single,
+            quarter_rows(layer, 0, cols, width),
+            quarter_rows(layer, 1, cols, width),
+            once_block(cols, width),
+            once_block(cols, width),
+            tile,
+            full_block(1, width),
+        ],
+        (tile, tile),
+        (
+            jax.ShapeDtypeStruct((rows, width), jnp.float32),
+            jax.ShapeDtypeStruct((rows, width), jnp.float32),
+        ),
+        8 * rows * width * cols,
+    )(spots, own, far, far_sib, weight, weight, recv, sib, middle, gate)
+
+
+def feed_back_kernel(
+    _, gdb_ref, hidden_ref, pre_ref, turned_ref, down_ref, up_ref,
+    down_grad_ref, up_grad_ref, bias_grad_ref, normed_grad_ref, gpre_ref, total_ref,
+):
+    starts = list(range(0, gdb_ref.shape[0], ROWS))
+    columns = gdb_ref.shape[1] // 4
+    sums = jnp.zeros(bias_grad_ref.shape, jnp.float32)
+
+    def product(start):
+        return lax.dot_general(
+            gdb_ref[pl.ds(start, ROWS), :], down_ref[0], CONTRACT_LAST, preferred_element_type=jnp.float32
+        )
+
+    grad_hidden = product(starts[0])
+    for i, start in enumerate(starts):
+        later = product(starts[i + 1]) if i + 1 < len(starts) else None
+        if i < 4:
+            part = pl.ds(i * columns, columns)
+            down_grad_ref[:, part] = lax.dot_general(
+                hidden_ref[0], gdb_ref[:, part], CONTRACT_FIRST, preferred_element_type=jnp.float32
+            ).astype(jnp.bfloat16)
+        part = pl.ds(start, ROWS)
+        pre = pre_ref[0, part, :]
+        square = pre * pre
+        bent = jnp.tanh(pre * (SLOPE + (SLOPE * 0.044715) * square))
+        half = 0.5 + 0.5 * bent
+        slope = half + (pre * (half * (1.0 - bent))) * (SLOPE + (3 * 0.044715 * SLOPE) * square)
+        grad_pre = (grad_hidden * slope).astype(jnp.bfloat16)
+        gpre_ref[part, :] = grad_pre
+        sums += jnp.sum(grad_pre.astype(jnp.float32), axis=0, keepdims=True)
+        grad_hidden = later
+    bias_grad_ref[...] = sums
+    up_grad_ref[...] = jnp.dot(
+        turned_ref[...], gpre_ref[...], preferred_element_type=jnp.float32
+    ).astype(jnp.bfloat16)
+
+    def each(store):
+        for start in starts:
+            part = pl.ds(start, ROWS)
+            term = lax.dot_general(
+                gpre_ref[part, :], up_ref[0], CONTRACT_LAST, preferred_element_type=jnp.float32
+            )
+            store(part, term)
+
+    step, steps = pl.program_id(0), pl.num_programs(0)
+
+    @pl.when(step == 0)
+    def _():
+        def store(part, term):
+            total_ref[part, :] = term
+
+        each(store)
+
+    @pl.when(step == steps - 1)
+    def _():
+        def store(part, term):
+            normed_grad_ref[part, :] = (total_ref[part, :] + term).astype(jnp.bfloat16)
+
+        each(store)
+
+
+def feed_back(spots, layer, own, r, gdb, hidden, pre, turned, down_weight, up_weight):
+    rows, width = gdb.shape
+    cols = hidden.shape[2]
+    step = cols // 2
+    per = cols // step
+    if own:
+        down_spec = pl.BlockSpec((1, step, width), lambda j, s: (layer, s[r] * per + j, 0))
+    else:
+        down_weight, up_weight = down_weight[None], up_weight[None]
+        down_spec = pl.BlockSpec((1, step, width), lambda j, s: (0, j, 0))
+    return call(
+        feed_back_kernel,
+        "feed_back",
+        (per,),
+        [
+            once_block(rows, width),
+            pl.BlockSpec((1, rows, step), lambda j, s: (r if own else 0, 0, j)),
+            pl.BlockSpec((1, rows, step), lambda j, s: (r if own else 0, 0, j)),
+            once_block(width, rows),
+            down_spec,
+            up_spec(layer, own, width, cols, step, lambda j: (r, j)),
+        ],
+        (
+            pl.BlockSpec((step, width), lambda j, s: (j, 0)),
+            pl.BlockSpec((width, step), lambda j, s: (0, j)),
+            pl.BlockSpec((1, step), lambda j, s: (0, j)),
+            full_block(rows, width),
+        ),
+        (
+            jax.ShapeDtypeStruct((cols, width), jnp.bfloat16),
+            jax.ShapeDtypeStruct((width, cols), jnp.bfloat16),
+            jax.ShapeDtypeStruct((1, cols), jnp.float32),
+            jax.ShapeDtypeStruct((rows, width), jnp.bfloat16),
+        ),
+        8 * rows * width * cols,
+        rows * cols,
+        scratch=[pltpu.VMEM((rows, step), jnp.bfloat16), pltpu.VMEM((rows, width), jnp.float32)],
+    )(spots, gdb, hidden, pre, turned, down_weight, up_weight)
+
+
+def join_back_kernel(
+    _, one_ref, two_ref, three_ref, four_ref, g_ref, middle_ref, branch_ref, own_ref, far_ref,
+    w0_ref, w1_ref, w2_ref, w3_ref, gate_ref, scale_ref,
+    grad_middle_ref, grad_own_ref, grad_far_ref, own_grad_ref, far_grad_ref, sums_ref, total_ref,
+):
+    one, two, three, four = (
+        ref[...].astype(jnp.float32) for ref in (one_ref, two_ref, three_ref, four_ref)
+    )
+    partial = (one + two) + (three + four)
+    pulled, shift_sum, scale_sum = norm_back(middle_ref[...], partial, scale_ref[...])
+    grad_middle = g_ref[...] + pulled
+    grad_middle_ref[...] = grad_middle
+    gate_sum = jnp.sum(grad_middle * branch_ref[...], axis=0, keepdims=True)
+    grad_branch = (gate_ref[...] * grad_middle).astype(jnp.bfloat16)
+    weights = jnp.concatenate([w0_ref[0], w1_ref[0], w2_ref[...], w3_ref[...]], axis=0)
+    grad_att = lax.dot_general(
+        grad_branch, weights, CONTRACT_LAST, preferred_element_type=jnp.float32
+    ).astype(jnp.bfloat16)
+    half = own_ref.shape[1]
+    grad_own_ref[...] = grad_att[:, :half]
+    grad_far_ref[...] = grad_att[:, half:]
+    att = jnp.concatenate([own_ref[...], far_ref[...]], axis=1)
+    weight_term = lax.dot_general(
+        att, grad_branch, CONTRACT_FIRST, preferred_element_type=jnp.float32
+    )
+    sums = jnp.concatenate([shift_sum, scale_sum, gate_sum], axis=0)
+    step = pl.program_id(0)
+
+    @pl.when(step == 0)
+    def _():
+        total_ref[...] = weight_term
+        sums_ref[...] = sums
+
+    @pl.when(step > 0)
+    def _():
+        total_ref[...] += weight_term
+        sums_ref[...] += sums
+
+    @pl.when(step == pl.num_programs(0) - 1)
+    def _():
+        own_grad_ref[...] = total_ref[:half, :].astype(jnp.bfloat16)
+        far_grad_ref[...] = total_ref[half:, :].astype(jnp.bfloat16)
+
+
+def join_back(spots, layer, partials, g, middle, branch, own, far, weight, recv, sib, gate, scale):
+    rows, width = g.shape
+    half = own.shape[1]
+    size = half // 2
+    tile = row_tile(width)
+    return call(
+        join_back_kernel,
+        "join_back",
+        (rows // ROWS,),
+        [tile] * 7
+        + [
+            row_tile(half),
+            row_tile(half),
+            quarter_rows(layer, 0, size, width),
+            quarter_rows(layer, 1, size, width),
+            once_block(size, width),
+            once_block(size, width),
+        ]
+        + [full_block(1, width)] * 2,
+        (
+            tile,
+            row_tile(half),
+            row_tile(half),
+            full_block(half, width),
+            full_block(half, width),
+            full_block(3, width),
+        ),
+        (
+            jax.ShapeDtypeStruct((rows, width), jnp.float32),
+            jax.ShapeDtypeStruct((rows, half), jnp.bfloat16),
+            jax.ShapeDtypeStruct((rows, half), jnp.bfloat16),
+            jax.ShapeDtypeStruct((half, width), jnp.bfloat16),
+            jax.ShapeDtypeStruct((half, width), jnp.bfloat16),
+            jax.ShapeDtypeStruct((3, width), jnp.float32),
+        ),
+        4 * rows * width * width,
+        scratch=[pltpu.VMEM((width, width), jnp.float32)],
+    )(spots, *partials, g, middle, branch, own, far, weight, weight, recv, sib, gate, scale)
+
+
+def attend_back_kernel(_, proj_ref, grad_ref, ublk_ref, place_ref, out_ref, table_ref):
+    place = place_ref[...]
+    items, lane = window_heads(proj_ref, ublk_ref, place, grad_ref)
+    wide = ublk_ref.shape[0] * HEAD
+    tables = {}
+    done = []
+
+    def first(item):
+        grad_probs = lax.dot_general(
+            item[5], item[7], CONTRACT_LAST, preferred_element_type=jnp.float32
+        )
+        return head_scores(item, ublk_ref), grad_probs
+
+    def middle(pair):
+        probs, grad_probs = head_probs(pair[0]), pair[1]
+        inner = jnp.sum(probs * grad_probs, axis=0, keepdims=True)
+        return probs.astype(jnp.bfloat16), (probs * (grad_probs - inner)).astype(jnp.bfloat16)
+
+    def last(i, held):
+        probs, grad_scores = held
+        rows, pair, head, _, key, _, scaled, above = items[i]
+        both = jnp.dot(
+            grad_scores, jnp.concatenate([scaled, place], axis=1), preferred_element_type=jnp.float32
+        )
+        grad_value = jnp.dot(probs, above, preferred_element_type=jnp.float32)
+        grad_query = lax.dot_general(
+            grad_scores,
+            (key * HEAD**-0.5).astype(jnp.bfloat16),
+            CONTRACT_FIRST,
+            preferred_element_type=jnp.float32,
+        )
+        tables[head] = both[:, 128:] if head not in tables else tables[head] + both[:, 128:]
+        done.append((grad_query, both[:, :128], grad_value))
+        if i % 2:
+            (q0, k0, v0), (q1, k1, v1) = done[i - 1], done[i]
+            for part, value in enumerate((jnp.where(lane < HEAD, q0, q1), k0 + k1, v0 + v1)):
+                out_ref[0, rows, part * wide + pair * 128 : part * wide + pair * 128 + 128] = (
+                    value.astype(jnp.bfloat16)
+                )
+
+    ahead(items, first, middle, last)
+    for head, value in tables.items():
+        table_ref[head] = value
+
+
+def attend_back(spots, first, proj, grad, ublk, place):
+    quarters, rows, cols = proj.shape
+    count = place.shape[0]
+    heads = ublk.shape[0] // 4
+    pairs = rows * count * heads * quarters
+    return call(
+        attend_back_kernel,
+        "attend_back",
+        (quarters,),
+        [
+            pl.BlockSpec((1, rows, cols), lambda q, s: (q, 0, 0)),
+            pl.BlockSpec((rows, heads * HEAD), lambda q, s: (0, q)),
+            pl.BlockSpec((heads, count, 128), lambda q, s: (first + s[q], 0, 0)),
+            full_block(count, 128),
+        ],
+        (
+            pl.BlockSpec((1, rows, cols), lambda q, s: (q, 0, 0)),
+            pl.BlockSpec((heads, count, 128), lambda q, s: (s[q], 0, 0)),
+        ),
+        (
+            jax.ShapeDtypeStruct(proj.shape, jnp.bfloat16),
+            jax.ShapeDtypeStruct((ublk.shape[0] // 2, count, 128), jnp.float32),
+        ),
+        pairs * 1536,
+        pairs,
+    )(spots, proj, grad, ublk, place)
+
+
+def in_grad_kernel(_, turned_ref, grad_ref, mine_ref, sib_ref):
+    def store(ref):
+        for part in range(3):
+            size = ref.shape[2]
+            ref[part] = jnp.dot(
+                turned_ref[...],
+                grad_ref[0, :, part * size : part * size + size],
+                preferred_element_type=jnp.float32,
+            ).astype(jnp.bfloat16)
+
+    @pl.when(pl.program_id(0) == 0)
+    def _():
+        store(sib_ref)
+
+    @pl.when(pl.program_id(0) == 1)
+    def _():
+        store(mine_ref)
+
+
+def in_grad(spots, turned, grad):
+    width, rows = turned.shape
+    cols = grad.shape[2]
+    size = cols // 3
+    out = jax.ShapeDtypeStruct((3, width, size), jnp.bfloat16)
+    return call(
+        in_grad_kernel,
+        "in_grad",
+        (2, 2),
+        [
+            pl.BlockSpec((width // 2, rows), lambda q, j, s: (j, 0)),
+            pl.BlockSpec((1, rows, cols), lambda q, j, s: (1 - q, 0, 0)),
+        ],
+        (
+            pl.BlockSpec((3, width // 2, size), lambda q, j, s: (0, q * j, 0)),
+            pl.BlockSpec((3, width // 2, size), lambda q, j, s: (0, jnp.maximum(q, j), 0)),
+        ),
+        (out, out),
+        4 * rows * width * cols,
+    )(spots, turned, grad)
+
+
+def project_back_kernel(
+    _, own_ref, far_ref, w0_ref, w1_ref, w2_ref, w3_ref, x_ref, middle_ref, scale_ref, out_ref, sums_ref
+):
+    total = None
+    for grad, weight in (
+        (own_ref[0], w0_ref), (own_ref[1], w1_ref), (far_ref[0], w2_ref), (far_ref[1], w3_ref)
+    ):
+        term = lax.dot_general(
+            grad, side_by_side(weight), CONTRACT_LAST, preferred_element_type=jnp.float32
+        )
+        total = term if total is None else total + term
+    pulled, shift_sum, scale_sum = norm_back(x_ref[...], total, scale_ref[...])
+    out_ref[...] = middle_ref[...] + pulled
+    sums = jnp.concatenate([shift_sum, scale_sum], axis=0)
+
+    @pl.when(pl.program_id(0) == 0)
+    def _():
+        sums_ref[...] = sums
+
+    @pl.when(pl.program_id(0) > 0)
+    def _():
+        sums_ref[...] += sums
+
+
+def project_back(spots, layer, own, far, weight, mine, sib, x, grad_middle, scale):
+    rows, width = x.shape
+    cols = own.shape[2]
+    tile = row_tile(width)
+    grad = pl.BlockSpec((2, ROWS, cols), lambda i, s: (0, i, 0))
+
+    return call(
+        project_back_kernel,
+        "project_back",
+        (rows // ROWS,),
+        [grad, grad]
+        + [in_spec(layer, width, cols, lambda i, r=r: r) for r in (0, 1)]
+        + [full_block(1, 3, width, cols // 3)] * 2
+        + [tile, tile, full_block(1, width)],
+        (tile, full_block(2, width)),
+        (
+            jax.ShapeDtypeStruct((rows, width), jnp.float32),
+            jax.ShapeDtypeStruct((2, width), jnp.float32),
+        ),
+        8 * rows * width * cols,
+    )(spots, own, far, weight, weight, mine[None], sib[None], x, grad_middle, scale)
+
+
+def modulation_kernel(_, activated_ref, rows_ref, out_ref):
+    out_ref[0, 0] = lax.dot_general(
+        activated_ref[...], rows_ref[0, 0], CONTRACT_FIRST, preferred_element_type=jnp.float32
+    )
+
+
+def modulation_back(spots, activated, rows):
+    layers, kinds, _, cols = rows.shape
+    count, width = activated.shape
+    values = jnp.concatenate(split_bits(rows), axis=2)
+    return call(
+        modulation_kernel,
+        "modulation_back",
+        (layers, kinds),
+        [
+            full_block(3 * count, width),
+            pl.BlockSpec((1, 1, 3 * count, cols), lambda l, k, s: (l, k, 0, 0)),
+        ],
+        pl.BlockSpec((1, 1, width, cols), lambda l, k, s: (l, k, 0, 0)),
+        jax.ShapeDtypeStruct((layers, kinds, width, cols), jnp.float32),
+        6 * layers * kinds * count * width * cols,
+    )(spots, jnp.concatenate([activated.astype(jnp.bfloat16)] * 3), values)
+
+
+SWAP = [(0, 1), (1, 0)]
+
+
+def either(flag, one, two):
+    return jnp.where(flag, one, two)
+
+
+def split_bits(values):
+    parts = []
+    for _ in range(3):
+        part = lax.reduce_precision(values, 8, 7)
+        parts.append(part.astype(jnp.bfloat16))
+        values = values - part
+    return parts
+
+
+def place_maps(layer, frames):
+    extents = window_shape(layer)
+    count = extents[0] * extents[1] * extents[2]
+    place = np.arange(count)
+    positions = (place // (extents[1] * extents[2]), place // extents[2] % extents[1], place % extents[2])
+    hots = []
+    width = sum(e for e in extents if e > 1)
+    levels = sum(2 * e - 1 for e in extents if e > 1)
+    pick = np.zeros((levels, width, width), np.float32)
+    column = base = 0
+    for position, extent in zip(positions, extents):
+        if extent == 1:
+            continue
+        spots = jnp.asarray(position, jnp.int32)
+        if extent == FRAMES and layer == 1:
+            spots = frames[spots]
+        hots.append((spots[:, None] == jnp.arange(extent, dtype=jnp.int32)[None, :]).astype(jnp.float32))
+        for i in range(extent):
+            for j in range(extent):
+                pick[base + i - j + extent - 1, column + i, column + j] = 1
+        column += extent
+        base += 2 * extent - 1
+    return jnp.concatenate(hots, axis=1), pick
+
+
+def bias_blocks(table, hot, pick):
+    pairs = jnp.einsum("hx,xij->hij", table, pick, precision=HIGH)
+    spread = jnp.einsum("ai,hij->haj", hot, pairs, precision=HIGH)
+    parts = split_bits(spread)
+    room = 128 - 3 * hot.shape[1]
+    padded = jnp.concatenate(parts + [jnp.zeros(spread.shape[:2] + (room,), jnp.bfloat16)], axis=2)
+    one = hot.astype(jnp.bfloat16)
+    place = jnp.concatenate([one] * 3 + [jnp.zeros((hot.shape[0], room), jnp.bfloat16)], axis=1)
+    return padded, place
+
+
+def table_grad(acc, hot, pick):
+    width = hot.shape[1]
+    pairs = jnp.einsum("hbi,bj->hij", acc[:, :, :width], hot, precision=HIGH)
+    return jnp.einsum("hij,xij->hx", pairs, pick, precision=HIGH)
+
+
+def per_device_pair(
+    tokens,
+    cotangent,
+    group_start,
+    band_index,
+    class_label,
+    time_table,
+    class_table,
+    modulation_weight,
+    modulation_bias,
+    input_weight,
+    output_weight,
+    space_offsets,
+    time_offsets,
+    up_weight,
+    up_bias,
+    down_weight,
+):
+    core = lax.axis_index("core")
+    chip_axes = ("z", "y")
+    chip = lax.axis_index(chip_axes)
+    side = lax.axis_index("mp")
+    chips = lax.axis_size(chip_axes)
+    low_side, first_core = side == 0, core == 0
+    rows, width = tokens.shape
+    half = width // 2
+    bf16, f32 = jnp.bfloat16, jnp.float32
+    spots = jnp.stack([core, 1 - core]).astype(jnp.int32)
+
+    def swap_side(value):
+        return lax.ppermute(value, "mp", SWAP)
+
+    def swap_core(value):
+        return lax.ppermute(value, "core", SWAP)
+
+    def half_of(value, axis):
+        size = value.shape[axis] // 2
+        return lax.dynamic_slice_in_dim(value, core * size, size, axis)
+
+    def after(value, *others):
+        return lax.optimization_barrier((value,) + others)[0]
+
+    def in_order(flag, one, two):
+        return [either(flag, one, two), either(flag, two, one)]
+
+    def gather_dp(value):
+        stack = value[None]
+        stack = jnp.concatenate(in_order(first_core, stack, swap_core(stack)))
+        distance = 1
+        while distance < chips:
+            got = lax.ppermute(stack, chip_axes, [(i, i ^ distance) for i in range(chips)])
+            stack = jnp.concatenate(in_order((chip // distance) % 2 == 0, stack, got))
+            distance *= 2
+        return stack
+
+    here_y, here_z = lax.axis_index("y"), lax.axis_index("z")
+    size_z = lax.axis_size("z")
+
+    def swap_y(value):
+        return lax.ppermute(value, "y", SWAP)
+
+    def eighth(value, axis):
+        size = value.shape[axis] // 4
+        return lax.dynamic_slice_in_dim(value, (2 * core + here_y) * size, size, axis)
+
+    def quarter(got, axis, start=None, use=None):
+        got = got if start is None else after(got, start)
+        other = swap_y(got)
+        other = other if use is None else after(other, use)
+        return jnp.concatenate(in_order(here_y == 0, got, other), axis=axis)
+
+    in_weight = input_weight.transpose(0, 2, 1, 3)
+    first_piece = eighth(in_weight[0], 2)
+    marked = after(jnp.where(group_start > 0, band_index, -1), first_piece)
+    every = lax.all_gather(marked, chip_axes + ("core",), tiled=True)
+    mine = lax.axis_index(chip_axes + ("core",))
+    order = jnp.arange(every.shape[0], dtype=jnp.int32)
+    latest = jnp.max(jnp.where((every >= 0) & (order <= mine), order, -1))
+    current = jnp.sum(jnp.where(order == latest, every, 0)) + jnp.where(latest < 0, -1, 0)
+    band_hot = (current == jnp.arange(time_table.shape[0], dtype=jnp.int32)).astype(f32)
+    class_hot = (class_label[0] == jnp.arange(class_table.shape[0], dtype=jnp.int32)).astype(f32)
+    condition = jnp.sum(band_hot[:, None] * time_table, axis=0) + jnp.sum(
+        class_hot[:, None] * class_table, axis=0
+    )
+    activated = jax.nn.silu(condition).astype(bf16)
+    local_modulation = (
+        jnp.einsum("d,ldcf->lcf", activated, modulation_weight, preferred_element_type=f32)
+        + modulation_bias
+    )
+    modulation_got = swap_side(local_modulation)
+    modulation = jnp.concatenate(in_order(low_side, local_modulation, modulation_got), axis=2)
+
+    far_in, far_up, far_down = ([None, None] for _ in range(3))
+    far_small = swap_side(
+        jnp.concatenate([space_offsets.reshape(-1), time_offsets.reshape(-1), up_bias.reshape(-1)])
+    )
+    cut_one = space_offsets.size
+    cut_two = cut_one + time_offsets.size
+    tables = (
+        jnp.concatenate([space_offsets, far_small[:cut_one].reshape(space_offsets.shape)]),
+        jnp.concatenate([time_offsets, far_small[cut_one:cut_two].reshape(time_offsets.shape)]),
+    )
+    biases = (up_bias.reshape(2, 2, 1, -1), far_small[cut_two:].reshape(2, 2, 1, -1))
+
+    def after_all(values, *others):
+        return lax.optimization_barrier((values,) + others)[0]
+
+    def fetch(layer, trigger):
+        sources = after_all((in_weight, up_weight, down_weight), trigger)
+        return [
+            swap_side(eighth(source[layer], axis)) for source, axis in zip(sources, (2, 1, 0))
+        ]
+
+    fetched = [fetch(0, modulation_got), None]
+    fetched[0][0] = swap_side(first_piece)
+    out_got = swap_side(eighth(after(output_weight, modulation_got), 1))
+    far_out, far_in, far_up, far_down = ([None, None] for _ in range(4))
+
+    split = lax.dynamic_slice_in_dim(tokens, (1 - side) * (rows - ROWS), ROWS, 0).reshape(8, 2, 16, width)
+    kept = lax.dynamic_index_in_dim(split, side, 1, keepdims=False)
+    got = swap_side(lax.dynamic_index_in_dim(split, 1 - side, 1, keepdims=False))
+    shared = jnp.concatenate(in_order(low_side, kept, got), axis=0)
+    whole = lax.dynamic_slice_in_dim(tokens, side * ROWS, rows - ROWS, 0)
+    whole = whole.reshape(2, 16, 2, 16, width).transpose(0, 2, 1, 3, 4)
+    x = jnp.concatenate([whole.reshape(-1, width), shared.reshape(-1, width)], axis=0).astype(f32)
+
+    frames = jnp.where(
+        low_side,
+        jnp.asarray([0, 1, 2, 3, 4], jnp.int32),
+        jnp.asarray([3, 4, 2, 0, 1], jnp.int32),
+    )
+    maps = [place_maps(layer, frames) for layer in range(2)]
+
+    def send_cotangent(value):
+        chunks = value.reshape(5, ROWS, width)
+        return chunks, swap_side(jnp.stack([chunks[1], chunks[3]]))
+
+    def turn_cotangent(chunks, got):
+        kept = [
+            either(low_side, chunks[0], chunks[2]),
+            either(low_side, chunks[2], chunks[4]),
+            either(low_side, chunks[4], chunks[0]),
+        ]
+        ordered = jnp.concatenate([jnp.stack(kept), got]).reshape(5, 8, 4, 8, width)
+        return ordered.transpose(2, 0, 1, 3, 4).reshape(rows, width).astype(f32)
+
+    saved = []
+    for layer in range(2):
+        shift_one, scale_one, gate_one, shift_two, scale_two, gate_two = [
+            modulation[layer, number][None] for number in range(6)
+        ]
+        ublk, place = bias_blocks(tables[layer], *maps[layer])
+        turned, normed, own_proj = project(
+            spots, layer, x, after(shift_one, far_small, fetched[layer][0]), scale_one, in_weight
+        )
+        if layer == 0:
+            fetched[1] = fetch(1, own_proj)
+            out_quarters = quarter(out_got, 1, own_proj)
+            far_in[0] = [quarter(fetched[0][0], 2)]
+        else:
+            far_in[1] = [quarter(fetched[1][0], 2, first_hidden, x)]
+        own_att = attend(spots, 0, after(own_proj, far_in[layer][0]), ublk, place)
+        far_in[layer].append(swap_core(far_in[layer][0]))
+        far_proj = project_more(spots, after(normed, own_att), *far_in[layer])
+        far_out[layer] = [out_quarters[layer], swap_core(after(out_quarters, own_att)[layer])]
+        far_att = attend(spots, 2, far_proj, ublk, place)
+        branch, middle, normed_two, turned_two = join(
+            spots, layer, own_att, far_att, output_weight, *far_out[layer], x, gate_one, shift_two, scale_two
+        )
+        start, use = (far_proj, normed_two) if layer == 0 else (first_hidden, own_proj)
+        far_up[layer] = [quarter(fetched[layer][1], 1, start, use)]
+        far_down[layer] = [quarter(fetched[layer][2], 0, start, use)]
+        for kept in (far_up, far_down):
+            kept[layer].append(swap_core(kept[layer][0]))
+        if layer == 1:
+            chunks, cotangent_got = send_cotangent(after(cotangent, far_att))
+        own_pre, own_hidden = up(spots, layer, None, normed_two, up_weight, biases[0])
+        far_pre, far_hidden = [None, None], [None, None]
+        for r in range(2):
+            ready = after(normed_two, far_hidden[0], *fetched[1]) if layer == 0 and r == 1 else normed_two
+            far_pre[r], far_hidden[r] = up(spots, layer, r, ready, far_up[layer][r], biases[1])
+        first_hidden = far_hidden[1]
+        if layer == 1:
+            g = turn_cotangent(chunks, after(cotangent_got, far_hidden[1]))
+        branch_two, out = down(
+            spots, layer, own_hidden, *far_hidden, down_weight, *far_down[layer],
+            middle if layer == 0 else after(middle, g), gate_two,
+        )
+        saved.append(
+            (
+                x, turned, own_proj, far_proj, own_att, far_att, branch, middle, turned_two,
+                own_pre, own_hidden, far_pre, far_hidden, branch_two, ublk, place,
+            )
+        )
+        if layer == 0:
+            parts = out.reshape(5, 2, 128, width)
+            kept = lax.dynamic_index_in_dim(parts, side, 1, keepdims=False)
+            sent = lax.dynamic_index_in_dim(parts, 1 - side, 1, keepdims=False).astype(bf16)
+            got = swap_side(sent).astype(f32)
+            shared = jnp.stack(in_order(low_side, kept[4], got[4]))
+            x = jnp.concatenate([kept[:4], shared, got[:4]])
+            x = x.reshape(5, 2, 8, 2, 8, width).transpose(1, 3, 0, 2, 4, 5).reshape(rows, width)
+
+    parts = out.reshape(2, 2, 5, 8, 8, width).transpose(2, 0, 3, 1, 4, 5).reshape(5, 2, 8, 16, width)
+    result_sent = parts[3:].astype(bf16)
+    result_got = swap_side(result_sent)
+    got = result_got.astype(f32)
+    pair = jnp.stack(in_order(low_side, parts[:2], got), axis=2)
+    pair = pair.reshape(2, 2, 16, 16, width).transpose(0, 2, 1, 3, 4).reshape(-1, width)
+    shared = parts[2].transpose(1, 0, 2, 3).reshape(-1, width)
+    result = either(
+        low_side, jnp.concatenate([pair, shared], axis=0), jnp.concatenate([shared, pair], axis=0)
+    )
+
+    def crossing(mine, sib):
+        return (mine.astype(f32) + swap_core(sib).astype(f32)).astype(bf16)
+
+    def joined(mine, sib, got):
+        return (mine.astype(f32) + swap_core(sib).astype(f32) + got.astype(f32)).astype(bf16)
+
+    def turn_z(value, distance):
+        return lax.ppermute(value, "z", [(i, (i + distance) % size_z) for i in range(size_z)])
+
+    def y_sent(value):
+        halves = value.reshape((2, -1) + value.shape[1:])
+        kept = lax.dynamic_index_in_dim(halves, here_y, 0, keepdims=False)
+        return kept, swap_y(lax.dynamic_index_in_dim(halves, 1 - here_y, 0, keepdims=False))
+
+    def z_sent(kept, got):
+        total = (kept.astype(f32) + got.astype(f32)).astype(bf16)
+        parts = total.reshape((size_z, -1) + total.shape[1:])
+        sent = [
+            lax.dynamic_index_in_dim(parts, (here_z + k) % size_z, 0, keepdims=False)
+            for k in range(size_z)
+        ]
+        return [sent[0]] + [turn_z(sent[k], k) for k in range(1, size_z)]
+
+    def z_back(parts):
+        total = sum(part.astype(f32) for part in parts).astype(bf16)
+        return [total] + [turn_z(total, k) for k in range(1, size_z)]
+
+    def y_back(parts):
+        row = jnp.stack(parts[::-1] + parts[:0:-1])
+        half = lax.dynamic_slice_in_dim(row, size_z - 1 - here_z, size_z, 0)
+        half = half.reshape((-1,) + half.shape[2:])
+        return half, swap_y(half)
+
+    def both_quarters(half, got):
+        full = jnp.concatenate(in_order(here_y == 0, half, got))
+        other = jnp.concatenate(in_order(here_y == 0, swap_core(half), swap_core(got)))
+        return in_order(first_core, full, other)
+
+    def by_quarter(value):
+        parts = value.reshape(2, -1, value.shape[-1])
+        return parts[0], parts[1]
+
+    collected, waiting, first_sums = [None, None], (result_sent,), ()
+    sums = [{}, {}]
+    steps = (y_sent, z_sent, z_back, y_back)
+
+    def advance(trigger, *names):
+        marks = []
+        for name in names:
+            value, step = sums[0][name]
+            value = after_all(tuple(value), trigger)
+            sums[0][name] = (steps[step](*value) if step < 2 else steps[step](value), step + 1)
+            marks.append(sums[0][name][0][0])
+        return marks
+
+    def both_cores(value):
+        return in_order(first_core, value, swap_core(value))
+
+    for layer in (1, 0):
+        shift_one, scale_one, gate_one, shift_two, scale_two, gate_two = [
+            modulation[layer, number][None] for number in range(6)
+        ]
+        (
+            x, turned, own_proj, far_proj, own_att, far_att, branch, middle, turned_two,
+            own_pre, own_hidden, far_pre, far_hidden, branch_two, ublk, place,
+        ) = saved[layer]
+        gdb = (gate_two * g).astype(bf16)
+        gate_two_grad = jnp.sum(g * branch_two, axis=0)
+
+        def feed(own, r, *first):
+            hidden, pre = (own_hidden, own_pre) if own else (far_hidden[r], far_pre[r])
+            weights = (down_weight, up_weight) if own else (far_down[layer][r], far_up[layer][r])
+            return feed_back(
+                spots, layer, own, r, after(gdb, *first), hidden, pre, turned_two, *weights
+            )
+
+        far_sib = feed(False, 1, *waiting)
+        far_mine = feed(False, 0, far_sib[0])
+        far_down_sum, far_up_sum = crossing(far_mine[0], far_sib[0]), crossing(far_mine[1], far_sib[1])
+        own_sib = feed(True, 1, far_down_sum, far_up_sum, *([result_got] if layer == 1 else []))
+        down_got = swap_side(far_down_sum)
+        own_mine = feed(True, 0, own_sib[0])
+        far, own = (far_mine, far_sib), (own_mine, own_sib)
+        grad_middle, grad_own, grad_far, own_out, far_out_grad, sums_two = join_back(
+            spots, layer, [far[1][3], far[0][3], own[1][3], own[0][3]], g, middle, branch, own_att, far_att,
+            output_weight, *far_out[layer], gate_one, scale_two,
+        )
+        down_sum = joined(own_mine[0], own_sib[0], down_got)
+        up_got = swap_side(after(far_up_sum, down_got))
+
+        far_grad, far_acc = attend_back(
+            spots, 2, far_proj, after(grad_far, down_sum), ublk, place
+        )
+        in_mine, in_sib = in_grad(spots, turned, far_grad)
+        own_grad, own_acc = attend_back(
+            spots, 0, own_proj, after(grad_own, in_mine), ublk, place
+        )
+        far_in_sum = crossing(in_mine, in_sib)
+        far_out_sum = crossing(*by_quarter(after(far_out_grad, in_mine)))
+        up_sum = joined(own_mine[1], own_sib[1], up_got)
+        in_mine, in_sib = in_grad(
+            spots, after(turned, far_in_sum, far_out_sum, up_sum), own_grad
+        )
+        in_got, out_got = swap_side(far_in_sum), swap_side(far_out_sum)
+        g, sums_one = project_back(
+            spots, layer, own_grad, far_grad, in_weight, *far_in[layer], x,
+            after(grad_middle, in_mine, *first_sums), scale_one,
+        )
+        out_sum = joined(*by_quarter(own_out), out_got)
+        in_sum = joined(in_mine, in_sib, in_got)
+        cut = in_sum.size // in_sum.shape[2]
+        last = jnp.concatenate([part.reshape(-1, in_sum.shape[2]) for part in (in_sum, out_sum)])
+        sums[layer]["last"] = ((last,), 0)
+        if layer == 0:
+            sums_one, g = after_all((sums_one, g), *advance(g, "last"))
+            second_sums = lax.psum(after_all((down_sum, up_sum), *first_sums), chip_axes)
+        table_rows = jnp.stack(
+            [sums_one[0], sums_one[1], sums_two[2], sums_two[0], sums_two[1], gate_two_grad]
+        )
+        if layer == 1:
+            parts = g.reshape(2, 2, 5, 8, 8, width).transpose(2, 0, 3, 1, 4, 5).reshape(5, 2, 128, width)
+            kept = jnp.concatenate(
+                [parts[:2].reshape(4, 128, width), either(low_side, parts[2, 0], parts[2, 1])[None]]
+            )
+            sent = jnp.concatenate(
+                [parts[3:].reshape(4, 128, width), either(low_side, parts[2, 1], parts[2, 0])[None]]
+            )
+            got = swap_side(after(sent.astype(bf16), in_got, out_got)).astype(f32)
+            g = jnp.stack(in_order(low_side, kept, got), axis=1).reshape(rows, width)
+            first_sums = lax.psum((down_sum, up_sum, last), chip_axes)
+            waiting = (last,)
+        rows_by_side = table_rows.reshape(6, 2, half)
+
+        def packed(place, acc, pieces):
+            return jnp.concatenate(
+                [
+                    lax.dynamic_index_in_dim(rows_by_side, place, 1, keepdims=False).reshape(-1),
+                    table_grad(acc, *maps[layer]).reshape(-1),
+                ]
+                + [part.reshape(-1) for part in in_order(first_core, pieces[0][2], pieces[1][2])]
+            )
+
+        collected[layer] = (packed(side, own_acc, own), packed(1 - side, far_acc, far))
+
+    small = jnp.concatenate([collected[0][0], collected[1][0]])
+    small += swap_side(jnp.concatenate([collected[0][1], collected[1][1]]))
+    spread = gather_dp(jnp.concatenate([small, activated.astype(f32)]))
+    modulation_rows, offset_sums, bias_sums, start = [], [], [], 0
+    for layer in range(2):
+        modulation_rows.append(spread[:, start : start + 6 * half].reshape(-1, 6, half))
+        start += 6 * half
+        heads, levels = tables[layer].shape[0] // 2, tables[layer].shape[1]
+        offset_sums.append(
+            jnp.sum(spread[:, start : start + heads * levels], axis=0).reshape(heads, levels)
+        )
+        start += heads * levels
+        bias_sums.append(jnp.sum(spread[:, start : start + up_bias.shape[1]], axis=0))
+        start += up_bias.shape[1]
+    modulation_rows = jnp.stack(modulation_rows).transpose(0, 2, 1, 3)
+
+    parts = g.reshape(5, 2, 128, width)
+    kept = lax.dynamic_index_in_dim(parts[4], side, 0, keepdims=False).reshape(8, 16, width)
+    sent = lax.dynamic_index_in_dim(parts[4], 1 - side, 0, keepdims=False).reshape(8, 16, width)
+    shared = jnp.stack(in_order(low_side, kept, swap_side(sent)), axis=1).reshape(-1, width)
+    whole = parts[:4].reshape(2, 2, 16, 16, width).transpose(0, 2, 1, 3, 4).reshape(-1, width)
+    grad_tokens = either(
+        low_side, jnp.concatenate([whole, shared], axis=0), jnp.concatenate([shared, whole], axis=0)
+    )
+
+    for _ in range(3):
+        advance(g, "last")
+    quarters = []
+    for layer in range(2):
+        parts = dict(zip(("down", "up", "last"), map(both_cores, (second_sums, first_sums)[layer])))
+        if layer == 0:
+            parts["last"] = both_quarters(*sums[0]["last"][0])
+        quarters.append(
+            (
+                [part[:cut].reshape(in_sum.shape) for part in parts["last"]],
+                [part[cut:].reshape(out_sum.shape) for part in parts["last"]],
+                parts["up"],
+                parts["down"],
+            )
+        )
+
+    def pair_of(number, axis):
+        return jnp.stack(
+            [jnp.concatenate(quarters[layer][number], axis=axis).astype(f32) for layer in range(2)]
+        )
+
+    return (
+        result,
+        grad_tokens,
+        modulation_back(spots, spread[:, start:], modulation_rows).transpose(0, 2, 1, 3),
+        jnp.sum(modulation_rows, axis=2),
+        pair_of(0, 2).transpose(0, 2, 1, 3),
+        pair_of(1, 0),
+        offset_sums[0],
+        offset_sums[1],
+        pair_of(2, 1),
+        jnp.stack(bias_sums),
+        pair_of(3, 0),
+    )
+
+
 def solution(mesh):
+    chips, odd = divmod(mesh.shape["dp"], 2)
+    if mesh.shape["mp"] == 2 and not odd and chips > 1 and chips & (chips - 1) == 0:
+        dp, run = ("z", "y", "core"), per_device_pair
+        mesh = Mesh(mesh.devices.reshape(-1, 2, 2, 2), dp + ("mp",))
+    else:
+        dp, run = ("dp",), per_device
+    both = dp + ("mp",)
     return jax.shard_map(
-        per_device,
+        run,
         mesh=mesh,
         in_specs=(
-            P(("dp", "mp"), None),
-            P(("dp", "mp"), None),
-            P("dp"),
-            P("dp"),
-            P("dp"),
+            P(both, None),
+            P(both, None),
+            P(dp),
+            P(dp),
+            P(dp),
             P(),
             P(),
             P(None, None, None, "mp"),
@@ -389,8 +1652,8 @@
             P(None, "mp", None),
         ),
         out_specs=(
-            P(("dp", "mp"), None),
-            P(("dp", "mp"), None),
+            P(both, None),
+            P(both, None),
             P(None, None, None, "mp"),
             P(None, None, "mp"),
             P(None, None, None, "mp"),

time: 3010 us -> 1330 us (0.44)
  waiting for transfers between devices: 1660 us -> 352 us
  matrix products: 597 us -> 21.4 us
  Pallas kernels: 0 us -> 571 us
  local copies, waits for them, and re-layouts: 365 us -> 107 us
  other arithmetic: 258 us -> 168 us
  blocking collectives: 83.6 us -> 12.3 us
  starting transfers between devices: 0.96 us -> 67.9 us
    reduce_scatter x10 -> x0, waiting for transfers between devices: 656 us -> none  [the longest x4 478 us: scatter_rows(): lax.psum_scatter(term(jnp.int32(0), count * lax.axis_size('mp')), 'mp', s...]
    pallas_call x0 -> x39, Pallas kernels: none -> 571 us  [run(): pl.pallas_call(kernel, out_shape=out_shape, grid_spec=pltpu.PrefetchScala...]
    dot_general x42 -> x13, matrix products: 583 us -> 21.4 us  [the longest x1 6.33 us: per_device_pair(): jnp.einsum('d,ldcf->lcf', activated, modulation_weight, preferred_element...]
    all_gather x8 -> x0, waiting for transfers between devices: 475 us -> none  [the longest x4 259 us: gather_grads(): return lax.all_gather(values, 'mp', axis=0, tiled=True)]
    psum x1 -> x2, waiting for transfers between devices: 533 us -> 104 us  [the longest x1 62.6 us: per_device_pair(): first_sums = lax.psum((down_sum, up_sum, last), chip_axes)]
    ppermute x0 -> x74, waiting for transfers between devices: none -> 248 us  [the longest x24 132 us: swap_side(): return lax.ppermute(value, 'mp', SWAP)]
    another operation x14 -> x17, local copies, waits for them, and re-layouts: 139 us -> 6.85 us  [the longest x4 6.28 us: per_device_pair(): modulation_rows = jnp.stack(modulation_rows).transpose(0, 2, 1, 3)]
    reduce_sum x20 -> x9, other arithmetic: 120 us -> 9.06 us  [the longest x2 5.51 us: per_device_pair(): gate_two_grad = jnp.sum(g * branch_two, axis=0)]
  transfers between devices with their start and end apart: 19 -> 76, of which waited for: 17 -> 22; matrix products, arithmetic and copies ran while one was open for 10% -> 17% of each run, Pallas kernels for 0% -> 35%
where the time goes in v2:
time: 1330 us; the launch traced here: 1320 us
  Pallas kernels  571 us (43%)
  waiting for transfers between devices  352 us (26%)
  other arithmetic  168 us (13%)
  local copies, waits for them, and re-layouts  107 us (8%)
  starting transfers between devices  67.9 us (5%)
  matrix products  21.4 us (2%)
  between operations  19.6 us (1%)
    pallas_call x39, Pallas kernels, run(): pl.pallas_call(kernel, out_shape=out_shape, grid_spec=pltpu.PrefetchScala...  571 us
    ppermute x24, waiting for transfers between devices, swap_side(): return lax.ppermute(value, 'mp', SWAP)  132 us
    ppermute x9, waiting for transfers between devices, swap_y(): return lax.ppermute(value, 'y', SWAP)  64.3 us
    psum x1, waiting for transfers between devices, per_device_pair(): first_sums = lax.psum((down_sum, up_sum, last), chip_axes)  62.6 us
    ppermute x6, waiting for transfers between devices, turn_z(): lax.ppermute(value, 'z', [(i, (i + distance) % size_z) for i in range(siz...  48.3 us
    psum x1, waiting for transfers between devices, per_device_pair(): lax.psum(after_all((down_sum, up_sum), *first_sums), chip_axes)  41.8 us
    ppermute x24, starting transfers between devices, swap_side(): return lax.ppermute(value, 'mp', SWAP)  27.8 us
    select_n x27, other arithmetic, either(): return jnp.where(flag, one, two)  27.5 us
  transfers between devices with their start and end apart: 76, of which 22 were waited for; matrix products, arithmetic and copies ran while one was open for 17% of the time, Pallas kernels for 35%

profile of v2, /device:TPU:0, one launch (start us, length us, event | category | flops | bytes accessed | tf_op | source)
XLA Modules:
  0.0 1318.9 jit_solution(5285763823697041435)
XLA Ops:
  138.2 16.3 %collective-permute-done.10 = bf16[1024,512]{1,0:T(8,128)(2,1)S(1)} collective-permute-done((bf16[1024,512]{1,0:T(8,128)(2,1)S(1)}, bf16[1024,512]{1,0:T(8,128)(2,1)S(1)}, u32[]{:S(2)}, u32[]{:S(2)}) %collective-permute-start.10) | collective-permute-done | bytes 1048608 | tf_op jit(solution)/shard_map/ppermute | solution.py:1265
  197.9 30.8 %collective-permute-done.11 = bf16[3,1024,128]{2,1,0:T(8,128)(2,1)} collective-permute-done((bf16[3,1024,128]{2,1,0:T(8,128)(2,1)}, bf16[3,1024,128]{2,1,0:T(8,128)(2,1)}, u32[]{:S(2)}, u32[]{:S(2)}) %collective-permute-start.11) | collective-permute-done | bytes 786464 | tf_op jit(solution)/shard_map/ppermute | solution.py:1236
  239.0 18.7 %down.2 = (f32[1280,1024]{1,0:T(8,128)}, f32[1280,1024]{1,0:T(8,128)}) custom-call(s32[2]{0:T(128)} %pad_add_fusion.2._, bf16[2,1280,1024]{2,1,0:T(8,128)(2,1)} %get-tuple-element.181.own_ref.hidden_ref, bf16[1,1280,1024]{2,1,0:T(8,128)(2,1)} %get-tuple-element.185.far_ref.hidden_ref, bf16[1,1280,1024]{2,1,0:T(8,128)(2,1)} %get-tuple-element.190.sib_ref.hidden_ref, ...), custom_call_target="tpu_custom_call" | custom-call | flops 167772160 | bytes 737344 | tf_op jit(solution)/shard_map/down/pallas_call | solution.py:428
  269.3 22.1 %collective-permute-done.18 = bf16[5,128,1024]{2,1,0:T(8,128)(2,1)S(1)} collective-permute-done((bf16[5,128,1024]{2,1,0:T(8,128)(2,1)}, bf16[5,128,1024]{2,1,0:T(8,128)(2,1)S(1)}, u32[]{:S(2)}, u32[]{:S(2)}) %collective-permute-start.18) | collective-permute-done | bytes 1310752 | tf_op jit(solution)/shard_map/ppermute | solution.py:1236
  393.8 13.1 up.9
  420.6 19.9 %down.3 = (f32[1280,1024]{1,0:T(8,128)}, f32[1280,1024]{1,0:T(8,128)}) custom-call(s32[2]{0:T(128)} %pad_add_fusion.2._, bf16[2,1280,1024]{2,1,0:T(8,128)(2,1)} %get-tuple-element.205.own_ref.hidden_ref, bf16[1,1280,1024]{2,1,0:T(8,128)(2,1)} %get-tuple-element.208.far_ref.hidden_ref, bf16[1,1280,1024]{2,1,0:T(8,128)(2,1)} %get-tuple-element.209.sib_ref.hidden_ref, ...), custom_call_target="tpu_custom_call" | custom-call | flops 167772160 | bytes 737344 | tf_op jit(solution)/shard_map/down/pallas_call | solution.py:428
  450.0 20.9 %feed_back.8 = (bf16[1024,1024]{1,0:T(8,128)(2,1)}, bf16[1024,1024]{1,0:T(8,128)(2,1)}, f32[1,1024]{1,0:T(1,128)}, bf16[1280,1024]{1,0:T(8,128)(2,1)}) custom-call(s32[2]{0:T(128)} %pad_add_fusion.2._, bf16[1280,1024]{1,0:T(8,128)(2,1)} %get-tuple-element.232.gdb_ref, bf16[1,1280,1024]{2,1,0:T(8,128)(2,1)} %get-tuple-element.209.sib_ref.hidden_ref, ...), custom_call_target="tpu_custom_call" | custom-call | flops 167772160 | bytes 376896 | tf_op jit(solution)/shard_map/feed_back/pallas_call | solution.py:428
  472.1 20.8 %feed_back.9 = (bf16[1024,1024]{1,0:T(8,128)(2,1)}, bf16[1024,1024]{1,0:T(8,128)(2,1)}, f32[1,1024]{1,0:T(1,128)}, bf16[1280,1024]{1,0:T(8,128)(2,1)}) custom-call(s32[2]{0:T(128)} %pad_add_fusion.2._, bf16[1280,1024]{1,0:T(8,128)(2,1)} %get-tuple-element.232.gdb_ref, bf16[1,1280,1024]{2,1,0:T(8,128)(2,1)} %get-tuple-element.208.far_ref.hidden_ref, ...), custom_call_target="tpu_custom_call" | custom-call | flops 167772160 | bytes 376896 | tf_op jit(solution)/shard_map/feed_back/pallas_call | solution.py:428
  503.0 21.0 %feed_back.10 = (bf16[1024,1024]{1,0:T(8,128)(2,1)}, bf16[1024,1024]{1,0:T(8,128)(2,1)}, f32[1,1024]{1,0:T(1,128)}, bf16[1280,1024]{1,0:T(8,128)(2,1)}) custom-call(s32[2]{0:T(128)} %pad_add_fusion.2._, bf16[1280,1024]{1,0:T(8,128)(2,1)} %get-tuple-element.232.gdb_ref, bf16[2,1280,1024]{2,1,0:T(8,128)(2,1)} %get-tuple-element.205.own_ref.hidden_ref, ...), custom_call_target="tpu_custom_call" | custom-call | flops 167772160 | bytes 696384 | tf_op jit(solution)/shard_map/feed_back/pallas_call | solution.py:428
  524.0 21.2 %feed_back.11 = (bf16[1024,1024]{1,0:T(8,128)(2,1)}, bf16[1024,1024]{1,0:T(8,128)(2,1)}, f32[1,1024]{1,0:T(1,128)}, bf16[1280,1024]{1,0:T(8,128)(2,1)}) custom-call(s32[2]{0:T(128)} %pad_add_fusion.2._, bf16[1280,1024]{1,0:T(8,128)(2,1)} %get-tuple-element.232.gdb_ref, bf16[2,1280,1024]{2,1,0:T(8,128)(2,1)} %get-tuple-element.205.own_ref.hidden_ref, ...), custom_call_target="tpu_custom_call" | custom-call | flops 167772160 | bytes 696384 | tf_op jit(solution)/shard_map/feed_back/pallas_call | solution.py:428
  545.3 20.8 %join_back.2 = (f32[1280,1024]{1,0:T(8,128)}, bf16[1280,512]{1,0:T(8,128)(2,1)}, bf16[1280,512]{1,0:T(8,128)(2,1)}, bf16[512,1024]{1,0:T(8,128)(2,1)}, bf16[512,1024]{1,0:T(8,128)(2,1)}, /*index=5*/f32[3,1024]{1,0:T(4,128)}) custom-call(s32[2]{0:T(128)} %pad_add_fusion.2._, bf16[1280,1024]{1,0:T(8,128)(2,1)} %get-tuple-element.220.one_ref, ...), custom_call_target="tpu_custom_call" | custom-call | flops 83886080 | bytes 688448 | tf_op jit(solution)/shard_map/join_back/pallas_call | solution.py:428
  571.8 19.9 %attend_back.4 = (bf16[2,1280,768]{2,1,0:T(8,128)(2,1)}, f32[8,320,128]{2,1,0:T(8,128)}) custom-call(s32[2]{0:T(128)} %pad_add_fusion.2._, bf16[2,1280,768]{2,1,0:T(8,128)(2,1)} %project_more.3.proj_ref, bf16[1280,512]{1,0:T(8,128)(2,1)} %get-tuple-element.239.grad_ref, bf16[16,320,128]{2,1,0:T(8,128)(2,1)} %maximum_maximum_fusion.ublk_ref, ...), custom_call_target="tpu_custom_call" | custom-call | flops 78643200 | bytes 185600 | tf_op jit(solution)/shard_map/attend_back/pallas_call | solution.py:428
  603.8 20.1 %attend_back.5 = (bf16[2,1280,768]{2,1,0:T(8,128)(2,1)}, f32[8,320,128]{2,1,0:T(8,128)}) custom-call(s32[2]{0:T(128)} %pad_add_fusion.2._, bf16[2,1280,768]{2,1,0:T(8,128)(2,1)} %get-tuple-element.200.proj_ref, bf16[1280,512]{1,0:T(8,128)(2,1)} %get-tuple-element.242.grad_ref, bf16[16,320,128]{2,1,0:T(8,128)(2,1)} %maximum_maximum_fusion.ublk_ref, ...), custom_call_target="tpu_custom_call" | custom-call | flops 78643200 | bytes 185600 | tf_op jit(solution)/shard_map/attend_back/pallas_call | solution.py:428
  630.5 20.2 %collective-permute-done.35 = bf16[1024,1024]{1,0:T(8,128)(2,1)} collective-permute-done((bf16[1024,1024]{1,0:T(8,128)(2,1)S(1)}, bf16[1024,1024]{1,0:T(8,128)(2,1)}, u32[]{:S(2)}, u32[]{:S(2)}) %collective-permute-start.35) | collective-permute-done | bytes 2097184 | tf_op jit(solution)/shard_map/ppermute | solution.py:1236
  666.1 16.9 %project_back.2 = (f32[1280,1024]{1,0:T(8,128)}, f32[2,1024]{1,0:T(2,128)}) custom-call(s32[2]{0:T(128)} %pad_add_fusion.2._, bf16[2,1280,768]{2,1,0:T(8,128)(2,1)} %get-tuple-element.243.grad_ref.own_ref, bf16[2,1280,768]{2,1,0:T(8,128)(2,1)} %get-tuple-element.240.grad_ref.far_ref, bf16[2,3,1024,512]{3,2,1,0:T(8,128)(2,1)} %bitcast.309, ...), custom_call_target="tpu_custom_call" | custom-call | flops 125829120 | bytes 614592 | tf_op jit(solution)/shard_map/project_back/pallas_call | solution.py:428
  704.3 21.5 %collective-permute-done.38 = bf16[5,128,1024]{2,1,0:T(8,128)(2,1)} collective-permute-done((bf16[5,128,1024]{2,1,0:T(8,128)(2,1)}, bf16[5,128,1024]{2,1,0:T(8,128)(2,1)}, u32[]{:S(2)}, u32[]{:S(2)}) %collective-permute-start.38) | collective-permute-done | bytes 1310752 | tf_op jit(solution)/shard_map/ppermute | solution.py:1236
  735.0 21.2 %feed_back.12 = (bf16[1024,1024]{1,0:T(8,128)(2,1)}, bf16[1024,1024]{1,0:T(8,128)(2,1)}, f32[1,1024]{1,0:T(1,128)}, bf16[1280,1024]{1,0:T(8,128)(2,1)}) custom-call(s32[2]{0:T(128)} %pad_add_fusion.2._, bf16[1280,1024]{1,0:T(8,128)(2,1)} %get-tuple-element.273.gdb_ref, bf16[1,1280,1024]{2,1,0:T(8,128)(2,1)} %get-tuple-element.190.sib_ref.hidden_ref, ...), custom_call_target="tpu_custom_call" | custom-call | flops 167772160 | bytes 376896 | tf_op jit(solution)/shard_map/feed_back/pallas_call | solution.py:428
  756.8 20.9 %feed_back.13 = (bf16[1024,1024]{1,0:T(8,128)(2,1)}, bf16[1024,1024]{1,0:T(8,128)(2,1)}, f32[1,1024]{1,0:T(1,128)}, bf16[1280,1024]{1,0:T(8,128)(2,1)}) custom-call(s32[2]{0:T(128)} %pad_add_fusion.2._, bf16[1280,1024]{1,0:T(8,128)(2,1)} %get-tuple-element.273.gdb_ref, bf16[1,1280,1024]{2,1,0:T(8,128)(2,1)} %get-tuple-element.185.far_ref.hidden_ref, ...), custom_call_target="tpu_custom_call" | custom-call | flops 167772160 | bytes 376896 | tf_op jit(solution)/shard_map/feed_back/pallas_call | solution.py:428
  784.6 20.9 %feed_back.14 = (bf16[1024,1024]{1,0:T(8,128)(2,1)}, bf16[1024,1024]{1,0:T(8,128)(2,1)}, f32[1,1024]{1,0:T(1,128)}, bf16[1280,1024]{1,0:T(8,128)(2,1)}) custom-call(s32[2]{0:T(128)} %pad_add_fusion.2._, bf16[1280,1024]{1,0:T(8,128)(2,1)} %get-tuple-element.273.gdb_ref, bf16[2,1280,1024]{2,1,0:T(8,128)(2,1)} %get-tuple-element.181.own_ref.hidden_ref, ...), custom_call_target="tpu_custom_call" | custom-call | flops 167772160 | bytes 696384 | tf_op jit(solution)/shard_map/feed_back/pallas_call | solution.py:428
  808.0 21.3 %feed_back.15 = (bf16[1024,1024]{1,0:T(8,128)(2,1)}, bf16[1024,1024]{1,0:T(8,128)(2,1)}, f32[1,1024]{1,0:T(1,128)}, bf16[1280,1024]{1,0:T(8,128)(2,1)}) custom-call(s32[2]{0:T(128)} %pad_add_fusion.2._, bf16[1280,1024]{1,0:T(8,128)(2,1)} %get-tuple-element.273.gdb_ref, bf16[2,1280,1024]{2,1,0:T(8,128)(2,1)} %get-tuple-element.181.own_ref.hidden_ref, ...), custom_call_target="tpu_custom_call" | custom-call | flops 167772160 | bytes 696384 | tf_op jit(solution)/shard_map/feed_back/pallas_call | solution.py:428
  829.3 21.5 %join_back.3 = (f32[1280,1024]{1,0:T(8,128)}, bf16[1280,512]{1,0:T(8,128)(2,1)}, bf16[1280,512]{1,0:T(8,128)(2,1)}, bf16[512,1024]{1,0:T(8,128)(2,1)}, bf16[512,1024]{1,0:T(8,128)(2,1)}, /*index=5*/f32[3,1024]{1,0:T(4,128)}) custom-call(s32[2]{0:T(128)} %pad_add_fusion.2._, bf16[1280,1024]{1,0:T(8,128)(2,1)} %get-tuple-element.261.one_ref, ...), custom_call_target="tpu_custom_call" | custom-call | flops 83886080 | bytes 688448 | tf_op jit(solution)/shard_map/join_back/pallas_call | solution.py:428
  857.5 14.1 %attend_back.6 = (bf16[2,1280,768]{2,1,0:T(8,128)(2,1)}, f32[8,256,128]{2,1,0:T(8,128)}) custom-call(s32[2]{0:T(128)} %pad_add_fusion.2._, bf16[2,1280,768]{2,1,0:T(8,128)(2,1)} %project_more.2.proj_ref, bf16[1280,512]{1,0:T(8,128)(2,1)} %get-tuple-element.280.grad_ref, bf16[16,256,128]{2,1,0:T(8,128)(2,1)} %maximum_maximum_fusion.1.ublk_ref, ...), custom_call_target="tpu_custom_call" | custom-call | flops 62914560 | bytes 177152 | tf_op jit(solution)/shard_map/attend_back/pallas_call | solution.py:428
  886.0 14.2 %attend_back.7 = (bf16[2,1280,768]{2,1,0:T(8,128)(2,1)}, f32[8,256,128]{2,1,0:T(8,128)}) custom-call(s32[2]{0:T(128)} %pad_add_fusion.2._, bf16[2,1280,768]{2,1,0:T(8,128)(2,1)} %get-tuple-element.174.proj_ref, bf16[1280,512]{1,0:T(8,128)(2,1)} %get-tuple-element.283.grad_ref, bf16[16,256,128]{2,1,0:T(8,128)(2,1)} %maximum_maximum_fusion.1.ublk_ref, ...), custom_call_target="tpu_custom_call" | custom-call | flops 62914560 | bytes 177152 | tf_op jit(solution)/shard_map/attend_back/pallas_call | solution.py:428
  929.0 23.6 %collective-permute-done.52 = bf16[256,1024]{1,0:T(8,128)(2,1)} collective-permute-done((bf16[256,1024]{1,0:T(8,128)(2,1)S(1)}, bf16[256,1024]{1,0:T(8,128)(2,1)}, u32[]{:S(2)}, u32[]{:S(2)}) %collective-permute-start.52) | collective-permute-done | bytes 524320 | tf_op jit(solution)/shard_map/ppermute | solution.py:1236
  954.6 62.6 %all-reduce.8.cloned.1.call-done = (bf16[1024,1024]{1,0:T(8,128)(2,1)}, bf16[1024,1024]{1,0:T(8,128)(2,1)}, bf16[4096,256]{1,0:T(8,128)(2,1)}) async-done(((bf16[1024,1024]{1,0:T(8,128)(2,1)}, bf16[1024,1024]{1,0:T(8,128)(2,1)}, bf16[4096,256]{1,0:T(8,128)(2,1)}), (bf16[1024,1024]{1,0:T(8,128)(2,1)}, bf16[1024,1024]{1,0:T(8,128)(2,1)}, bf16[4096,256]{1,0:T(8,128)(2,1)})) %all-reduce.8.cloned.1.call-update) | async-done | bytes 6291472 | tf_op jit(solution)/shard_map/psum | solution.py:1549
  1017.2 17.0 %project_back.3 = (f32[1280,1024]{1,0:T(8,128)}, f32[2,1024]{1,0:T(2,128)}) custom-call(s32[2]{0:T(128)} %pad_add_fusion.2._, bf16[2,1280,768]{2,1,0:T(8,128)(2,1)} %get-tuple-element.284.grad_ref.own_ref, bf16[2,1280,768]{2,1,0:T(8,128)(2,1)} %get-tuple-element.281.grad_ref.far_ref, bf16[2,3,1024,512]{3,2,1,0:T(8,128)(2,1)} %bitcast.311, ...), custom_call_target="tpu_custom_call" | custom-call | flops 125829120 | bytes 614592 | tf_op jit(solution)/shard_map/project_back/pallas_call | solution.py:428
  1083.9 15.7 %collective-permute-done.59 = bf16[2048,256]{1,0:T(8,128)(2,1)} collective-permute-done((bf16[2048,256]{1,0:T(8,128)(2,1)}, bf16[2048,256]{1,0:T(8,128)(2,1)}, u32[]{:S(2)}, u32[]{:S(2)}) %collective-permute-start.59) | collective-permute-done | bytes 1048608 | tf_op jit(solution)/shard_map/ppermute | solution.py:1265
  1117.6 19.4 %collective-permute-done.61 = bf16[512,256]{1,0:T(8,128)(2,1)S(1)} collective-permute-done((bf16[512,256]{1,0:T(8,128)(2,1)S(1)}, bf16[512,256]{1,0:T(8,128)(2,1)S(1)}, u32[]{:S(2)}, u32[]{:S(2)}) %collective-permute-start.61) | collective-permute-done | bytes 262176 | tf_op jit(solution)/shard_map/ppermute | solution.py:1427
  1157.5 18.9 %collective-permute-done.64 = bf16[512,256]{1,0:T(8,128)(2,1)S(1)} collective-permute-done((bf16[512,256]{1,0:T(8,128)(2,1)S(1)}, bf16[512,256]{1,0:T(8,128)(2,1)S(1)}, u32[]{:S(2)}, u32[]{:S(2)}) %collective-permute-start.64) | collective-permute-done | bytes 262176 | tf_op jit(solution)/shard_map/ppermute | solution.py:1427
  1189.1 21.6 %collective-permute-done.66 = bf16[2048,256]{1,0:T(8,128)(2,1)} collective-permute-done((bf16[2048,256]{1,0:T(8,128)(2,1)}, bf16[2048,256]{1,0:T(8,128)(2,1)}, u32[]{:S(2)}, u32[]{:S(2)}) %collective-permute-start.66) | collective-permute-done | bytes 1048608 | tf_op jit(solution)/shard_map/ppermute | solution.py:1265
  1215.5 13.1 modulation_back.1
  1229.4 41.8 %all-reduce.6.cloned.1.call-done = (bf16[1024,1024]{1,0:T(8,128)(2,1)}, bf16[1024,1024]{1,0:T(8,128)(2,1)}) async-done(((bf16[1024,1024]{1,0:T(8,128)(2,1)}, bf16[1024,1024]{1,0:T(8,128)(2,1)}), (bf16[1024,1024]{1,0:T(8,128)(2,1)}, bf16[1024,1024]{1,0:T(8,128)(2,1)})) %all-reduce.6.cloned.1.call-update) | async-done | bytes 4194320 | tf_op jit(solution)/shard_map/psum | solution.py:1535
  (635 shorter events, 607.2 us)
Async XLA Ops:
  7.2 1010.0 %all-reduce.8.cloned.1.call-start = ((), (), s32[]{:S(2)}) async-start(), calls=%async_computation.1 | async-start | bytes 12582912 | tf_op jit(solution)/shard_map/psum | solution.py:1549
  59.6 46.9 %collective-permute-start.15 = (bf16[512,1024]{1,0:T(8,128)(2,1)S(1)}, bf16[512,1024]{1,0:T(8,128)(2,1)}, u32[]{:S(2)}, u32[]{:S(2)}) collective-permute-start(bf16[512,1024]{1,0:T(8,128)(2,1)S(1)} %dynamic-slice_bitcast_fusion.3), channel_id=1, source_target_pairs={{0,1},{1,0},{2,3},{3,2},{4,5},{5,4},{6,7},{7,6},{8,9},{9,8},{10,11... | collective-permute-start | bytes 3145736 | tf_op jit(solution)/shard_map/ppermute | solution.py:1236
  62.9 50.2 %collective-permute-start.9 = (bf16[1024,512]{1,0:T(8,128)(2,1)}, bf16[1024,512]{1,0:T(8,128)(2,1)S(1)}, u32[]{:S(2)}, u32[]{:S(2)}) collective-permute-start(bf16[1024,512]{1,0:T(8,128)(2,1)} %dynamic-slice_bitcast_fusion.6), channel_id=1, source_target_pairs={{0,1},{1,0},{2,3},{3,2},{4,5},{5,4},{6,7},{7,6},{8,9},{9,8},{10,11... | collective-permute-start | bytes 3145736 | tf_op jit(solution)/shard_map/ppermute | solution.py:1236
  113.1 41.5 %collective-permute-start.10 = (bf16[1024,512]{1,0:T(8,128)(2,1)S(1)}, bf16[1024,512]{1,0:T(8,128)(2,1)S(1)}, u32[]{:S(2)}, u32[]{:S(2)}) collective-permute-start(bf16[1024,512]{1,0:T(8,128)(2,1)S(1)} %collective-permute-done.9), channel_id=1, source_target_pairs={{0,4},{4,0},{1,5},{5,1},{2,6},{6,2},{3,7},{7,3},{8,12},{12,8},{9,1... | collective-permute-start | bytes 3145736 | tf_op jit(solution)/shard_map/ppermute | solution.py:1265
  157.2 71.6 %collective-permute-start.14 = (bf16[1024,1024]{1,0:T(8,128)(2,1)}, bf16[1024,1024]{1,0:T(8,128)(2,1)S(1)}, u32[]{:S(2)}, u32[]{:S(2)}) collective-permute-start(bf16[1024,1024]{1,0:T(8,128)(2,1)} %get-tuple-element.410), channel_id=1, source_target_pairs={{0,2},{2,0},{1,3},{3,1},{4,6},{6,4},{5,7},{7,5},{8,10},{10,8},{9,1... | collective-permute-start | bytes 6291464 | tf_op jit(solution)/shard_map/ppermute | solution.py:1239
  160.0 79.1 %collective-permute-start.17 = (bf16[1024,1024]{1,0:T(8,128)(2,1)}, bf16[1024,1024]{1,0:T(8,128)(2,1)}, u32[]{:S(2)}, u32[]{:S(2)}) collective-permute-start(bf16[1024,1024]{1,0:T(8,128)(2,1)} %get-tuple-element.399.w2_ref), channel_id=1, source_target_pairs={{0,2},{2,0},{1,3},{3,1},{4,6},{6,4},{5,7},{7,5},{8,10},{10,8},{9,1... | collective-permute-start | bytes 6291464 | tf_op jit(solution)/shard_map/ppermute | solution.py:1239
  163.6 65.2 %collective-permute-start.12 = (bf16[1024,512]{1,0:T(8,128)(2,1)}, bf16[1024,512]{1,0:T(8,128)(2,1)}, u32[]{:S(2)}, u32[]{:S(2)}) collective-permute-start(bf16[1024,512]{1,0:T(8,128)(2,1)} %dynamic-slice_bitcast_fusion.5), channel_id=1, source_target_pairs={{0,1},{1,0},{2,3},{3,2},{4,5},{5,4},{6,7},{7,6},{8,9},{9,8},{10,11... | collective-permute-start | bytes 3145736 | tf_op jit(solution)/shard_map/ppermute | solution.py:1236
  166.9 61.9 %collective-permute-start.13 = (bf16[512,1024]{1,0:T(8,128)(2,1)}, bf16[512,1024]{1,0:T(8,128)(2,1)}, u32[]{:S(2)}, u32[]{:S(2)}) collective-permute-start(bf16[512,1024]{1,0:T(8,128)(2,1)} %dynamic-slice_bitcast_fusion.4), channel_id=1, source_target_pairs={{0,1},{1,0},{2,3},{3,2},{4,5},{5,4},{6,7},{7,6},{8,9},{9,8},{10,11... | collective-permute-start | bytes 3145736 | tf_op jit(solution)/shard_map/ppermute | solution.py:1236
  168.8 60.0 %collective-permute-start.11 = (bf16[3,1024,128]{2,1,0:T(8,128)(2,1)}, bf16[3,1024,128]{2,1,0:T(8,128)(2,1)}, u32[]{:S(2)}, u32[]{:S(2)}) collective-permute-start(bf16[3,1024,128]{2,1,0:T(8,128)(2,1)} %dynamic-slice_bitcast_fusion.7), channel_id=1, source_target_pairs={{0,1},{1,0},{2,3},{3,2},{4,5},{5,4},{6,7},{7,6},{8,9},{9,8},{10,11... | collective-permute-start | bytes 2359304 | tf_op jit(solution)/shard_map/ppermute | solution.py:1236
  265.4 46.1 %collective-permute-start.22 = (bf16[1024,512]{1,0:T(8,128)(2,1)}, bf16[1024,512]{1,0:T(8,128)(2,1)S(1)}, u32[]{:S(2)}, u32[]{:S(2)}) collective-permute-start(bf16[1024,512]{1,0:T(8,128)(2,1)} %collective-permute-done.12), channel_id=1, source_target_pairs={{0,4},{4,0},{1,5},{5,1},{2,6},{6,2},{3,7},{7,3},{8,12},{12,8},{9,1... | collective-permute-start | bytes 3145736 | tf_op jit(solution)/shard_map/ppermute | solution.py:1265
  267.7 59.0 %collective-permute-start.24 = (bf16[512,1024]{1,0:T(8,128)(2,1)}, bf16[512,1024]{1,0:T(8,128)(2,1)}, u32[]{:S(2)}, u32[]{:S(2)}) collective-permute-start(bf16[512,1024]{1,0:T(8,128)(2,1)} %collective-permute-done.13), channel_id=1, source_target_pairs={{0,4},{4,0},{1,5},{5,1},{2,6},{6,2},{3,7},{7,3},{8,12},{12,8},{9,1... | collective-permute-start | bytes 3145736 | tf_op jit(solution)/shard_map/ppermute | solution.py:1265
  300.0 45.7 %collective-permute-start.20 = (bf16[3,1024,256]{2,1,0:T(8,128)(2,1)}, bf16[3,1024,256]{2,1,0:T(8,128)(2,1)S(1)}, u32[]{:S(2)}, u32[]{:S(2)}) collective-permute-start(bf16[3,1024,256]{2,1,0:T(8,128)(2,1)} %get-tuple-element.418), channel_id=1, source_target_pairs={{0,2},{2,0},{1,3},{3,1},{4,6},{6,4},{5,7},{7,5},{8,10},{10,8},{9,1... | collective-permute-start | bytes 4718600 | tf_op jit(solution)/shard_map/ppermute | solution.py:1239
  315.5 91.5 %collective-permute-start.23 = (bf16[1024,1024]{1,0:T(8,128)(2,1)}, bf16[1024,1024]{1,0:T(8,128)(2,1)S(1)}, u32[]{:S(2)}, u32[]{:S(2)}) collective-permute-start(bf16[1024,1024]{1,0:T(8,128)(2,1)} %get-tuple-element.404), channel_id=1, source_target_pairs={{0,2},{2,0},{1,3},{3,1},{4,6},{6,4},{5,7},{7,5},{8,10},{10,8},{9,1... | collective-permute-start | bytes 6291464 | tf_op jit(solution)/shard_map/ppermute | solution.py:1239
  331.1 89.5 %collective-permute-start.25 = (bf16[1024,1024]{1,0:T(8,128)(2,1)}, bf16[1024,1024]{1,0:T(8,128)(2,1)}, u32[]{:S(2)}, u32[]{:S(2)}) collective-permute-start(bf16[1024,1024]{1,0:T(8,128)(2,1)} %get-tuple-element.401.w2_ref), channel_id=1, source_target_pairs={{0,2},{2,0},{1,3},{3,1},{4,6},{6,4},{5,7},{7,5},{8,10},{10,8},{9,1... | collective-permute-start | bytes 6291464 | tf_op jit(solution)/shard_map/ppermute | solution.py:1239
  368.0 49.7 %collective-permute-start.26 = (bf16[2,256,1024]{2,1,0:T(8,128)(2,1)S(1)}, bf16[2,256,1024]{2,1,0:T(8,128)(2,1)S(1)}, u32[]{:S(2)}, u32[]{:S(2)}) collective-permute-start(bf16[2,256,1024]{2,1,0:T(8,128)(2,1)S(1)} %pad_maximum_fusion.17), channel_id=1, source_target_pairs={{0,1},{1,0},{2,3},{3,2},{4,5},{5,4},{6,7},{7,6},{8,9},{9,8},{10,11... | collective-permute-start | bytes 3145736 | tf_op jit(solution)/shard_map/ppermute | solution.py:1236
  497.6 68.5 %collective-permute-start.31 = (bf16[1024,1024]{1,0:T(8,128)(2,1)S(1)}, bf16[1024,1024]{1,0:T(8,128)(2,1)}, u32[]{:S(2)}, u32[]{:S(2)}) collective-permute-start(bf16[1024,1024]{1,0:T(8,128)(2,1)S(1)} %add_convert_fusion.7), channel_id=1, source_target_pairs={{0,1},{1,0},{2,3},{3,2},{4,5},{5,4},{6,7},{7,6},{8,9},{9,8},{10,11... | collective-permute-start | bytes 6291464 | tf_op jit(solution)/shard_map/ppermute | solution.py:1236
  524.0 42.2 %collective-permute-start.30 = (bf16[1024,1024]{1,0:T(8,128)(2,1)}, bf16[1024,1024]{1,0:T(8,128)(2,1)}, u32[]{:S(2)}, u32[]{:S(2)}) collective-permute-start(bf16[1024,1024]{1,0:T(8,128)(2,1)} %get-tuple-element.231), channel_id=1, source_target_pairs={{0,2},{2,0},{1,3},{3,1},{4,6},{6,4},{5,7},{7,5},{8,10},{10,8},{9,1... | collective-permute-start | bytes 6291464 | tf_op jit(solution)/shard_map/ppermute | solution.py:1239
  602.1 48.5 %collective-permute-start.35 = (bf16[1024,1024]{1,0:T(8,128)(2,1)S(1)}, bf16[1024,1024]{1,0:T(8,128)(2,1)}, u32[]{:S(2)}, u32[]{:S(2)}) collective-permute-start(bf16[1024,1024]{1,0:T(8,128)(2,1)S(1)} %add_convert_fusion.6), channel_id=1, source_target_pairs={{0,1},{1,0},{2,3},{3,2},{4,5},{5,4},{6,7},{7,6},{8,9},{9,8},{10,11... | collective-permute-start | bytes 6291464 | tf_op jit(solution)/shard_map/ppermute | solution.py:1236
  627.0 68.1 %collective-permute-start.36 = (bf16[3,1024,256]{2,1,0:T(8,128)(2,1)}, bf16[3,1024,256]{2,1,0:T(8,128)(2,1)S(1)}, u32[]{:S(2)}, u32[]{:S(2)}) collective-permute-start(bf16[3,1024,256]{2,1,0:T(8,128)(2,1)} %add_convert_fusion.11), channel_id=1, source_target_pairs={{0,1},{1,0},{2,3},{3,2},{4,5},{5,4},{6,7},{7,6},{8,9},{9,8},{10,11... | collective-permute-start | bytes 4718600 | tf_op jit(solution)/shard_map/ppermute | solution.py:1236
  781.7 69.1 %collective-permute-start.44 = (bf16[1024,1024]{1,0:T(8,128)(2,1)}, bf16[1024,1024]{1,0:T(8,128)(2,1)}, u32[]{:S(2)}, u32[]{:S(2)}) collective-permute-start(bf16[1024,1024]{1,0:T(8,128)(2,1)} %add_convert_fusion.3), channel_id=1, source_target_pairs={{0,1},{1,0},{2,3},{3,2},{4,5},{5,4},{6,7},{7,6},{8,9},{9,8},{10,11... | collective-permute-start | bytes 6291464 | tf_op jit(solution)/shard_map/ppermute | solution.py:1236
  805.5 46.9 %collective-permute-start.43 = (bf16[1024,1024]{1,0:T(8,128)(2,1)}, bf16[1024,1024]{1,0:T(8,128)(2,1)}, u32[]{:S(2)}, u32[]{:S(2)}) collective-permute-start(bf16[1024,1024]{1,0:T(8,128)(2,1)} %get-tuple-element.272), channel_id=1, source_target_pairs={{0,2},{2,0},{1,3},{3,1},{4,6},{6,4},{5,7},{7,5},{8,10},{10,8},{9,1... | collective-permute-start | bytes 6291464 | tf_op jit(solution)/shard_map/ppermute | solution.py:1239
  805.6 465.5 %all-reduce.6.cloned.1.call-start = ((), (), s32[]{:S(2)}) async-start(), calls=%async_computation | async-start | bytes 8388608 | tf_op jit(solution)/shard_map/psum | solution.py:1535
  807.4 97.9 %collective-permute-start.47 = (bf16[1024,1024]{1,0:T(8,128)(2,1)}, bf16[1024,1024]{1,0:T(8,128)(2,1)}, u32[]{:S(2)}, u32[]{:S(2)}) collective-permute-start(bf16[1024,1024]{1,0:T(8,128)(2,1)} %get-tuple-element.290), channel_id=1, source_target_pairs={{0,2},{2,0},{1,3},{3,1},{4,6},{6,4},{5,7},{7,5},{8,10},{10,8},{9,1... | collective-permute-start | bytes 6291464 | tf_op jit(solution)/shard_map/ppermute | solution.py:1239
  850.7 54.5 %collective-permute-start.48 = (bf16[1024,1024]{1,0:T(8,128)(2,1)}, bf16[1024,1024]{1,0:T(8,128)(2,1)}, u32[]{:S(2)}, u32[]{:S(2)}) collective-permute-start(bf16[1024,1024]{1,0:T(8,128)(2,1)} %add_convert_fusion.2), channel_id=1, source_target_pairs={{0,1},{1,0},{2,3},{3,2},{4,5},{5,4},{6,7},{7,6},{8,9},{9,8},{10,11... | collective-permute-start | bytes 6291464 | tf_op jit(solution)/shard_map/ppermute | solution.py:1236
  904.7 129.5 %collective-permute-start.50 = (bf16[3,1024,256]{2,1,0:T(8,128)(2,1)}, bf16[3,1024,256]{2,1,0:T(8,128)(2,1)}, u32[]{:S(2)}, u32[]{:S(2)}) collective-permute-start(bf16[3,1024,256]{2,1,0:T(8,128)(2,1)} %add_convert_fusion.9), channel_id=1, source_target_pairs={{0,1},{1,0},{2,3},{3,2},{4,5},{5,4},{6,7},{7,6},{8,9},{9,8},{10,11... | collective-permute-start | bytes 4718600 | tf_op jit(solution)/shard_map/ppermute | solution.py:1236
  920.9 113.4 %collective-permute-start.49 = (bf16[3,1024,256]{2,1,0:T(8,128)(2,1)}, bf16[3,1024,256]{2,1,0:T(8,128)(2,1)}, u32[]{:S(2)}, u32[]{:S(2)}) collective-permute-start(bf16[3,1024,256]{2,1,0:T(8,128)(2,1)} %get-tuple-element.297), channel_id=1, source_target_pairs={{0,2},{2,0},{1,3},{3,1},{4,6},{6,4},{5,7},{7,5},{8,10},{10,8},{9,1... | collective-permute-start | bytes 4718600 | tf_op jit(solution)/shard_map/ppermute | solution.py:1239
  1053.9 50.1 %collective-permute-start.73 = (bf16[1024,1024]{1,0:T(8,128)(2,1)}, bf16[1024,1024]{1,0:T(8,128)(2,1)}, u32[]{:S(2)}, u32[]{:S(2)}) collective-permute-start(bf16[1024,1024]{1,0:T(8,128)(2,1)} %get-tuple-element.357), channel_id=1, source_target_pairs={{0,2},{2,0},{1,3},{3,1},{4,6},{6,4},{5,7},{7,5},{8,10},{10,8},{9,1... | collective-permute-start | bytes 6291464 | tf_op jit(solution)/shard_map/ppermute | solution.py:1239
  1054.0 97.2 %collective-permute-start.71 = (bf16[1024,1024]{1,0:T(8,128)(2,1)}, bf16[1024,1024]{1,0:T(8,128)(2,1)}, u32[]{:S(2)}, u32[]{:S(2)}) collective-permute-start(bf16[1024,1024]{1,0:T(8,128)(2,1)} %get-tuple-element.358), channel_id=1, source_target_pairs={{0,2},{2,0},{1,3},{3,1},{4,6},{6,4},{5,7},{7,5},{8,10},{10,8},{9,1... | collective-permute-start | bytes 6291464 | tf_op jit(solution)/shard_map/ppermute | solution.py:1239
  1058.4 41.1 %collective-permute-start.59 = (bf16[2048,256]{1,0:T(8,128)(2,1)}, bf16[2048,256]{1,0:T(8,128)(2,1)}, u32[]{:S(2)}, u32[]{:S(2)}) collective-permute-start(bf16[2048,256]{1,0:T(8,128)(2,1)} %get-tuple-element.396), channel_id=1, source_target_pairs={{0,4},{4,0},{1,5},{5,1},{2,6},{6,2},{3,7},{7,3},{8,12},{12,8},{9,1... | collective-permute-start | bytes 3145736 | tf_op jit(solution)/shard_map/ppermute | solution.py:1265
  1065.8 113.2 %collective-permute-start.58 = (f32[8,12072]{1,0:T(8,128)}, f32[8,12072]{1,0:T(8,128)}, u32[]{:S(2)}, u32[]{:S(2)}) collective-permute-start(f32[8,12072]{1,0:T(8,128)} %pad_maximum_fusion.21), channel_id=1, source_target_pairs={{0,16},{4,20},{8,24},{12,28},{16,0},{20,4},{24,8},{28,12},{1,17},{... | collective-permute-start | bytes 1158920 | tf_op jit(solution)/shard_map/ppermute | solution.py:1256
  1189.1 84.3 %collective-permute-start.67 = (bf16[2048,256]{1,0:T(8,128)(2,1)}, bf16[2048,256]{1,0:T(8,128)(2,1)}, u32[]{:S(2)}, u32[]{:S(2)}) collective-permute-start(bf16[2048,256]{1,0:T(8,128)(2,1)} %bitcast.143), channel_id=1, source_target_pairs={{0,2},{2,0},{1,3},{3,1},{4,6},{6,4},{5,7},{7,5},{8,10},{10,8},{9,1... | collective-permute-start | bytes 3145736 | tf_op jit(solution)/shard_map/ppermute | solution.py:1239
  1210.6 62.7 %collective-permute-start.68 = (bf16[2048,256]{1,0:T(8,128)(2,1)}, bf16[2048,256]{1,0:T(8,128)(2,1)}, u32[]{:S(2)}, u32[]{:S(2)}) collective-permute-start(bf16[2048,256]{1,0:T(8,128)(2,1)} %collective-permute-done.66), channel_id=1, source_target_pairs={{0,2},{2,0},{1,3},{3,1},{4,6},{6,4},{5,7},{7,5},{8,10},{10,8},{9,1... | collective-permute-start | bytes 3145736 | tf_op jit(solution)/shard_map/ppermute | solution.py:1239
  (155 other events, 2027.2 us)
Sparse Core Ops, SparseCore 0:
  805.8 211.3 all-reduce.7
  1054.7 216.3 all-reduce.5

commit v3 on v2

--- a/solution.py
+++ b/solution.py
@@ -1382,11 +1382,12 @@
         own_pre, own_hidden = up(spots, layer, None, normed_two, up_weight, biases[0])
         far_pre, far_hidden = [None, None], [None, None]
         for r in range(2):
-            ready = after(normed_two, far_hidden[0], *fetched[1]) if layer == 0 and r == 1 else normed_two
-            far_pre[r], far_hidden[r] = up(spots, layer, r, ready, far_up[layer][r], biases[1])
+            far_pre[r], far_hidden[r] = up(spots, layer, r, normed_two, far_up[layer][r], biases[1])
         first_hidden = far_hidden[1]
         if layer == 1:
             g = turn_cotangent(chunks, after(cotangent_got, far_hidden[1]))
+        if layer == 0:
+            far_hidden[1] = after(far_hidden[1], *fetched[1])
         branch_two, out = down(
             spots, layer, own_hidden, *far_hidden, down_weight, *far_down[layer],
             middle if layer == 0 else after(middle, g), gate_two,
@@ -1518,12 +1519,12 @@
         far_out_sum = crossing(*by_quarter(after(far_out_grad, in_mine)))
         up_sum = joined(own_mine[1], own_sib[1], up_got)
         in_mine, in_sib = in_grad(
-            spots, after(turned, far_in_sum, far_out_sum, up_sum), own_grad
+            spots, after(turned, far_in_sum, far_out_sum, up_sum, *first_sums), own_grad
         )
         in_got, out_got = swap_side(far_in_sum), swap_side(far_out_sum)
         g, sums_one = project_back(
             spots, layer, own_grad, far_grad, in_weight, *far_in[layer], x,
-            after(grad_middle, in_mine, *first_sums), scale_one,
+            after(grad_middle, in_mine), scale_one,
         )
         out_sum = joined(*by_quarter(own_out), out_got)
         in_sum = joined(in_mine, in_sib, in_got)
@@ -1532,7 +1533,7 @@
         sums[layer]["last"] = ((last,), 0)
         if layer == 0:
             sums_one, g = after_all((sums_one, g), *advance(g, "last"))
-            second_sums = lax.psum(after_all((down_sum, up_sum), *first_sums), chip_axes)
+            second_sums = lax.psum(after_all((down_sum, up_sum, first_last), *first_sums), chip_axes)
         table_rows = jnp.stack(
             [sums_one[0], sums_one[1], sums_two[2], sums_two[0], sums_two[1], gate_two_grad]
         )
@@ -1546,7 +1547,7 @@
             )
             got = swap_side(after(sent.astype(bf16), in_got, out_got)).astype(f32)
             g = jnp.stack(in_order(low_side, kept, got), axis=1).reshape(rows, width)
-            first_sums = lax.psum((down_sum, up_sum, last), chip_axes)
+            first_sums, first_last = lax.psum((down_sum, up_sum), chip_axes), last
             waiting = (last,)
         rows_by_side = table_rows.reshape(6, 2, half)
 
@@ -1590,9 +1591,12 @@
         advance(g, "last")
     quarters = []
     for layer in range(2):
-        parts = dict(zip(("down", "up", "last"), map(both_cores, (second_sums, first_sums)[layer])))
+        down_up = (second_sums[:2], first_sums)[layer]
+        parts = {"down": both_cores(down_up[0]), "up": both_cores(down_up[1])}
         if layer == 0:
             parts["last"] = both_quarters(*sums[0]["last"][0])
+        else:
+            parts["last"] = both_cores(second_sums[2])
         quarters.append(
             (
                 [part[:cut].reshape(in_sum.shape) for part in parts["last"]],

time: 1330 us -> 1390 us (1.045)
  waiting for transfers between devices: 352 us -> 421 us
    psum x2, waiting for transfers between devices: 104 us -> 167 us  [the longest x1 123 us: per_device_pair(): lax.psum(after_all((down_sum, up_sum, first_last), *first_sums), chip_axes)]
    ppermute x24, waiting for transfers between devices: 132 us -> 104 us  [swap_side(): return lax.ppermute(value, 'mp', SWAP)]
    ppermute x9, waiting for transfers between devices: 64.3 us -> 89.3 us  [swap_y(): return lax.ppermute(value, 'y', SWAP)]
  transfers between devices with their start and end apart: 76 -> 76, of which waited for: 22 -> 22; matrix products, arithmetic and copies ran while one was open for 17% -> 15% of each run, Pallas kernels for 35% -> 33%
where the time goes in v3:
time: 1390 us; the launch traced here: 1380 us
  Pallas kernels  570 us (41%)
  waiting for transfers between devices  421 us (30%)
  other arithmetic  161 us (12%)
  local copies, waits for them, and re-layouts  101 us (7%)
  starting transfers between devices  71.8 us (5%)
  matrix products  21.4 us (2%)
  between operations  19.6 us (1%)
    pallas_call x39, Pallas kernels, run(): pl.pallas_call(kernel, out_shape=out_shape, grid_spec=pltpu.PrefetchScala...  570 us
    psum x1, waiting for transfers between devices, per_device_pair(): lax.psum(after_all((down_sum, up_sum, first_last), *first_sums), chip_axes)  123 us
    ppermute x24, waiting for transfers between devices, swap_side(): return lax.ppermute(value, 'mp', SWAP)  104 us
    ppermute x9, waiting for transfers between devices, swap_y(): return lax.ppermute(value, 'y', SWAP)  89.3 us
    ppermute x6, waiting for transfers between devices, turn_z(): lax.ppermute(value, 'z', [(i, (i + distance) % size_z) for i in range(siz...  57.3 us
    psum x1, waiting for transfers between devices, per_device_pair(): first_sums, first_last = (lax.psum((down_sum, up_sum), chip_axes), last)  43.5 us
    select_n x27, other arithmetic, either(): return jnp.where(flag, one, two)  29.3 us
  transfers between devices with their start and end apart: 76, of which 22 were waited for; matrix products, arithmetic and copies ran while one was open for 15% of the time, Pallas kernels for 33%

profile of v3, /device:TPU:0, one launch (start us, length us, event | category | flops | bytes accessed | tf_op | source)
XLA Modules:
  0.0 1378.0 jit_solution(3403890031479423049)
XLA Ops:
  138.2 16.7 %collective-permute-done.10 = bf16[1024,512]{1,0:T(8,128)(2,1)S(1)} collective-permute-done((bf16[1024,512]{1,0:T(8,128)(2,1)S(1)}, bf16[1024,512]{1,0:T(8,128)(2,1)S(1)}, u32[]{:S(2)}, u32[]{:S(2)}) %collective-permute-start.10) | collective-permute-done | bytes 1048608 | tf_op jit(solution)/shard_map/ppermute | solution.py:1265
  208.4 20.8 %collective-permute-done.12 = bf16[3,1024,128]{2,1,0:T(8,128)(2,1)} collective-permute-done((bf16[3,1024,128]{2,1,0:T(8,128)(2,1)}, bf16[3,1024,128]{2,1,0:T(8,128)(2,1)}, u32[]{:S(2)}, u32[]{:S(2)}) %collective-permute-start.12) | collective-permute-done | bytes 786464 | tf_op jit(solution)/shard_map/ppermute | solution.py:1236
  229.2 18.7 %down.2 = (f32[1280,1024]{1,0:T(8,128)}, f32[1280,1024]{1,0:T(8,128)}) custom-call(s32[2]{0:T(128)} %pad_add_fusion.2._, bf16[2,1280,1024]{2,1,0:T(8,128)(2,1)} %get-tuple-element.182.own_ref.hidden_ref, bf16[1,1280,1024]{2,1,0:T(8,128)(2,1)} %get-tuple-element.186.far_ref.hidden_ref, bf16[1,1280,1024]{2,1,0:T(8,128)(2,1)} %get-tuple-element.191.sib_ref.hidden_ref, ...), custom_call_target="tpu_custom_call" | custom-call | flops 167772160 | bytes 737344 | tf_op jit(solution)/shard_map/down/pallas_call | solution.py:428
  259.5 22.1 %collective-permute-done.18 = bf16[5,128,1024]{2,1,0:T(8,128)(2,1)S(1)} collective-permute-done((bf16[5,128,1024]{2,1,0:T(8,128)(2,1)}, bf16[5,128,1024]{2,1,0:T(8,128)(2,1)S(1)}, u32[]{:S(2)}, u32[]{:S(2)}) %collective-permute-start.18) | collective-permute-done | bytes 1310752 | tf_op jit(solution)/shard_map/ppermute | solution.py:1236
  384.2 13.1 up.9
  410.9 19.9 %down.3 = (f32[1280,1024]{1,0:T(8,128)}, f32[1280,1024]{1,0:T(8,128)}) custom-call(s32[2]{0:T(128)} %pad_add_fusion.2._, bf16[2,1280,1024]{2,1,0:T(8,128)(2,1)} %get-tuple-element.206.own_ref.hidden_ref, bf16[1,1280,1024]{2,1,0:T(8,128)(2,1)} %get-tuple-element.209.far_ref.hidden_ref, bf16[1,1280,1024]{2,1,0:T(8,128)(2,1)} %get-tuple-element.210.sib_ref.hidden_ref, ...), custom_call_target="tpu_custom_call" | custom-call | flops 167772160 | bytes 737344 | tf_op jit(solution)/shard_map/down/pallas_call | solution.py:428
  440.3 20.9 %feed_back.8 = (bf16[1024,1024]{1,0:T(8,128)(2,1)}, bf16[1024,1024]{1,0:T(8,128)(2,1)}, f32[1,1024]{1,0:T(1,128)}, bf16[1280,1024]{1,0:T(8,128)(2,1)}) custom-call(s32[2]{0:T(128)} %pad_add_fusion.2._, bf16[1280,1024]{1,0:T(8,128)(2,1)} %get-tuple-element.233.gdb_ref, bf16[1,1280,1024]{2,1,0:T(8,128)(2,1)} %get-tuple-element.210.sib_ref.hidden_ref, ...), custom_call_target="tpu_custom_call" | custom-call | flops 167772160 | bytes 376896 | tf_op jit(solution)/shard_map/feed_back/pallas_call | solution.py:428
  462.3 21.1 %feed_back.9 = (bf16[1024,1024]{1,0:T(8,128)(2,1)}, bf16[1024,1024]{1,0:T(8,128)(2,1)}, f32[1,1024]{1,0:T(1,128)}, bf16[1280,1024]{1,0:T(8,128)(2,1)}) custom-call(s32[2]{0:T(128)} %pad_add_fusion.2._, bf16[1280,1024]{1,0:T(8,128)(2,1)} %get-tuple-element.233.gdb_ref, bf16[1,1280,1024]{2,1,0:T(8,128)(2,1)} %get-tuple-element.209.far_ref.hidden_ref, ...), custom_call_target="tpu_custom_call" | custom-call | flops 167772160 | bytes 376896 | tf_op jit(solution)/shard_map/feed_back/pallas_call | solution.py:428
  493.4 20.9 %feed_back.10 = (bf16[1024,1024]{1,0:T(8,128)(2,1)}, bf16[1024,1024]{1,0:T(8,128)(2,1)}, f32[1,1024]{1,0:T(1,128)}, bf16[1280,1024]{1,0:T(8,128)(2,1)}) custom-call(s32[2]{0:T(128)} %pad_add_fusion.2._, bf16[1280,1024]{1,0:T(8,128)(2,1)} %get-tuple-element.233.gdb_ref, bf16[2,1280,1024]{2,1,0:T(8,128)(2,1)} %get-tuple-element.206.own_ref.hidden_ref, ...), custom_call_target="tpu_custom_call" | custom-call | flops 167772160 | bytes 696384 | tf_op jit(solution)/shard_map/feed_back/pallas_call | solution.py:428
  514.4 20.9 %feed_back.11 = (bf16[1024,1024]{1,0:T(8,128)(2,1)}, bf16[1024,1024]{1,0:T(8,128)(2,1)}, f32[1,1024]{1,0:T(1,128)}, bf16[1280,1024]{1,0:T(8,128)(2,1)}) custom-call(s32[2]{0:T(128)} %pad_add_fusion.2._, bf16[1280,1024]{1,0:T(8,128)(2,1)} %get-tuple-element.233.gdb_ref, bf16[2,1280,1024]{2,1,0:T(8,128)(2,1)} %get-tuple-element.206.own_ref.hidden_ref, ...), custom_call_target="tpu_custom_call" | custom-call | flops 167772160 | bytes 696384 | tf_op jit(solution)/shard_map/feed_back/pallas_call | solution.py:428
  535.3 20.9 %join_back.2 = (f32[1280,1024]{1,0:T(8,128)}, bf16[1280,512]{1,0:T(8,128)(2,1)}, bf16[1280,512]{1,0:T(8,128)(2,1)}, bf16[512,1024]{1,0:T(8,128)(2,1)}, bf16[512,1024]{1,0:T(8,128)(2,1)}, /*index=5*/f32[3,1024]{1,0:T(4,128)}) custom-call(s32[2]{0:T(128)} %pad_add_fusion.2._, bf16[1280,1024]{1,0:T(8,128)(2,1)} %get-tuple-element.221.one_ref, ...), custom_call_target="tpu_custom_call" | custom-call | flops 83886080 | bytes 688448 | tf_op jit(solution)/shard_map/join_back/pallas_call | solution.py:428
  561.9 20.2 %attend_back.4 = (bf16[2,1280,768]{2,1,0:T(8,128)(2,1)}, f32[8,320,128]{2,1,0:T(8,128)}) custom-call(s32[2]{0:T(128)} %pad_add_fusion.2._, bf16[2,1280,768]{2,1,0:T(8,128)(2,1)} %project_more.3.proj_ref, bf16[1280,512]{1,0:T(8,128)(2,1)} %get-tuple-element.240.grad_ref, bf16[16,320,128]{2,1,0:T(8,128)(2,1)} %maximum_maximum_fusion.ublk_ref, ...), custom_call_target="tpu_custom_call" | custom-call | flops 78643200 | bytes 185600 | tf_op jit(solution)/shard_map/attend_back/pallas_call | solution.py:428
  594.0 20.2 %attend_back.5 = (bf16[2,1280,768]{2,1,0:T(8,128)(2,1)}, f32[8,320,128]{2,1,0:T(8,128)}) custom-call(s32[2]{0:T(128)} %pad_add_fusion.2._, bf16[2,1280,768]{2,1,0:T(8,128)(2,1)} %get-tuple-element.201.proj_ref, bf16[1280,512]{1,0:T(8,128)(2,1)} %get-tuple-element.243.grad_ref, bf16[16,320,128]{2,1,0:T(8,128)(2,1)} %maximum_maximum_fusion.ublk_ref, ...), custom_call_target="tpu_custom_call" | custom-call | flops 78643200 | bytes 185600 | tf_op jit(solution)/shard_map/attend_back/pallas_call | solution.py:428
  620.9 20.1 %collective-permute-done.35 = bf16[1024,1024]{1,0:T(8,128)(2,1)} collective-permute-done((bf16[1024,1024]{1,0:T(8,128)(2,1)S(1)}, bf16[1024,1024]{1,0:T(8,128)(2,1)}, u32[]{:S(2)}, u32[]{:S(2)}) %collective-permute-start.35) | collective-permute-done | bytes 2097184 | tf_op jit(solution)/shard_map/ppermute | solution.py:1236
  656.4 16.9 %project_back.2 = (f32[1280,1024]{1,0:T(8,128)}, f32[2,1024]{1,0:T(2,128)}) custom-call(s32[2]{0:T(128)} %pad_add_fusion.2._, bf16[2,1280,768]{2,1,0:T(8,128)(2,1)} %get-tuple-element.244.grad_ref.own_ref, bf16[2,1280,768]{2,1,0:T(8,128)(2,1)} %get-tuple-element.241.grad_ref.far_ref, bf16[2,3,1024,512]{3,2,1,0:T(8,128)(2,1)} %bitcast.309, ...), custom_call_target="tpu_custom_call" | custom-call | flops 125829120 | bytes 614592 | tf_op jit(solution)/shard_map/project_back/pallas_call | solution.py:428
  693.5 22.6 %collective-permute-done.38 = bf16[5,128,1024]{2,1,0:T(8,128)(2,1)} collective-permute-done((bf16[5,128,1024]{2,1,0:T(8,128)(2,1)}, bf16[5,128,1024]{2,1,0:T(8,128)(2,1)}, u32[]{:S(2)}, u32[]{:S(2)}) %collective-permute-start.38) | collective-permute-done | bytes 1310752 | tf_op jit(solution)/shard_map/ppermute | solution.py:1236
  725.3 21.0 %feed_back.12 = (bf16[1024,1024]{1,0:T(8,128)(2,1)}, bf16[1024,1024]{1,0:T(8,128)(2,1)}, f32[1,1024]{1,0:T(1,128)}, bf16[1280,1024]{1,0:T(8,128)(2,1)}) custom-call(s32[2]{0:T(128)} %pad_add_fusion.2._, bf16[1280,1024]{1,0:T(8,128)(2,1)} %get-tuple-element.274.gdb_ref, bf16[1,1280,1024]{2,1,0:T(8,128)(2,1)} %get-tuple-element.191.sib_ref.hidden_ref, ...), custom_call_target="tpu_custom_call" | custom-call | flops 167772160 | bytes 376896 | tf_op jit(solution)/shard_map/feed_back/pallas_call | solution.py:428
  746.9 21.1 %feed_back.13 = (bf16[1024,1024]{1,0:T(8,128)(2,1)}, bf16[1024,1024]{1,0:T(8,128)(2,1)}, f32[1,1024]{1,0:T(1,128)}, bf16[1280,1024]{1,0:T(8,128)(2,1)}) custom-call(s32[2]{0:T(128)} %pad_add_fusion.2._, bf16[1280,1024]{1,0:T(8,128)(2,1)} %get-tuple-element.274.gdb_ref, bf16[1,1280,1024]{2,1,0:T(8,128)(2,1)} %get-tuple-element.186.far_ref.hidden_ref, ...), custom_call_target="tpu_custom_call" | custom-call | flops 167772160 | bytes 376896 | tf_op jit(solution)/shard_map/feed_back/pallas_call | solution.py:428
  775.0 20.9 %feed_back.14 = (bf16[1024,1024]{1,0:T(8,128)(2,1)}, bf16[1024,1024]{1,0:T(8,128)(2,1)}, f32[1,1024]{1,0:T(1,128)}, bf16[1280,1024]{1,0:T(8,128)(2,1)}) custom-call(s32[2]{0:T(128)} %pad_add_fusion.2._, bf16[1280,1024]{1,0:T(8,128)(2,1)} %get-tuple-element.274.gdb_ref, bf16[2,1280,1024]{2,1,0:T(8,128)(2,1)} %get-tuple-element.182.own_ref.hidden_ref, ...), custom_call_target="tpu_custom_call" | custom-call | flops 167772160 | bytes 696384 | tf_op jit(solution)/shard_map/feed_back/pallas_call | solution.py:428
  804.7 21.1 %feed_back.15 = (bf16[1024,1024]{1,0:T(8,128)(2,1)}, bf16[1024,1024]{1,0:T(8,128)(2,1)}, f32[1,1024]{1,0:T(1,128)}, bf16[1280,1024]{1,0:T(8,128)(2,1)}) custom-call(s32[2]{0:T(128)} %pad_add_fusion.2._, bf16[1280,1024]{1,0:T(8,128)(2,1)} %get-tuple-element.274.gdb_ref, bf16[2,1280,1024]{2,1,0:T(8,128)(2,1)} %get-tuple-element.182.own_ref.hidden_ref, ...), custom_call_target="tpu_custom_call" | custom-call | flops 167772160 | bytes 696384 | tf_op jit(solution)/shard_map/feed_back/pallas_call | solution.py:428
  825.8 21.0 %join_back.3 = (f32[1280,1024]{1,0:T(8,128)}, bf16[1280,512]{1,0:T(8,128)(2,1)}, bf16[1280,512]{1,0:T(8,128)(2,1)}, bf16[512,1024]{1,0:T(8,128)(2,1)}, bf16[512,1024]{1,0:T(8,128)(2,1)}, /*index=5*/f32[3,1024]{1,0:T(4,128)}) custom-call(s32[2]{0:T(128)} %pad_add_fusion.2._, bf16[1280,1024]{1,0:T(8,128)(2,1)} %get-tuple-element.262.one_ref, ...), custom_call_target="tpu_custom_call" | custom-call | flops 83886080 | bytes 688448 | tf_op jit(solution)/shard_map/join_back/pallas_call | solution.py:428
  853.2 14.3 %attend_back.6 = (bf16[2,1280,768]{2,1,0:T(8,128)(2,1)}, f32[8,256,128]{2,1,0:T(8,128)}) custom-call(s32[2]{0:T(128)} %pad_add_fusion.2._, bf16[2,1280,768]{2,1,0:T(8,128)(2,1)} %project_more.2.proj_ref, bf16[1280,512]{1,0:T(8,128)(2,1)} %get-tuple-element.281.grad_ref, bf16[16,256,128]{2,1,0:T(8,128)(2,1)} %maximum_maximum_fusion.1.ublk_ref, ...), custom_call_target="tpu_custom_call" | custom-call | flops 62914560 | bytes 177152 | tf_op jit(solution)/shard_map/attend_back/pallas_call | solution.py:428
  882.6 14.2 %attend_back.7 = (bf16[2,1280,768]{2,1,0:T(8,128)(2,1)}, f32[8,256,128]{2,1,0:T(8,128)}) custom-call(s32[2]{0:T(128)} %pad_add_fusion.2._, bf16[2,1280,768]{2,1,0:T(8,128)(2,1)} %get-tuple-element.175.proj_ref, bf16[1280,512]{1,0:T(8,128)(2,1)} %get-tuple-element.284.grad_ref, bf16[16,256,128]{2,1,0:T(8,128)(2,1)} %maximum_maximum_fusion.1.ublk_ref, ...), custom_call_target="tpu_custom_call" | custom-call | flops 62914560 | bytes 177152 | tf_op jit(solution)/shard_map/attend_back/pallas_call | solution.py:428
  907.1 43.5 %all-reduce.8.cloned.1.call-done = (bf16[1024,1024]{1,0:T(8,128)(2,1)}, bf16[1024,1024]{1,0:T(8,128)(2,1)}) async-done(((bf16[1024,1024]{1,0:T(8,128)(2,1)}, bf16[1024,1024]{1,0:T(8,128)(2,1)}), (bf16[1024,1024]{1,0:T(8,128)(2,1)}, bf16[1024,1024]{1,0:T(8,128)(2,1)})) %all-reduce.8.cloned.1.call-update) | async-done | bytes 4194320 | tf_op jit(solution)/shard_map/psum | solution.py:1550
  979.3 17.1 %project_back.3 = (f32[1280,1024]{1,0:T(8,128)}, f32[2,1024]{1,0:T(2,128)}) custom-call(s32[2]{0:T(128)} %pad_add_fusion.2._, bf16[2,1280,768]{2,1,0:T(8,128)(2,1)} %get-tuple-element.285.grad_ref.own_ref, bf16[2,1280,768]{2,1,0:T(8,128)(2,1)} %get-tuple-element.282.grad_ref.far_ref, bf16[2,3,1024,512]{3,2,1,0:T(8,128)(2,1)} %bitcast.311, ...), custom_call_target="tpu_custom_call" | custom-call | flops 125829120 | bytes 614592 | tf_op jit(solution)/shard_map/project_back/pallas_call | solution.py:428
  1029.6 31.7 %collective-permute-done.59 = bf16[2048,256]{1,0:T(8,128)(2,1)S(1)} collective-permute-done((bf16[2048,256]{1,0:T(8,128)(2,1)S(1)}, bf16[2048,256]{1,0:T(8,128)(2,1)S(1)}, u32[]{:S(2)}, u32[]{:S(2)}) %collective-permute-start.59) | collective-permute-done | bytes 1048608 | tf_op jit(solution)/shard_map/ppermute | solution.py:1265
  1078.0 20.2 %collective-permute-done.61 = bf16[512,256]{1,0:T(8,128)(2,1)S(1)} collective-permute-done((bf16[512,256]{1,0:T(8,128)(2,1)S(1)}, bf16[512,256]{1,0:T(8,128)(2,1)S(1)}, u32[]{:S(2)}, u32[]{:S(2)}) %collective-permute-start.61) | collective-permute-done | bytes 262176 | tf_op jit(solution)/shard_map/ppermute | solution.py:1428
  1098.3 17.3 %collective-permute-start.63 = (bf16[512,256]{1,0:T(8,128)(2,1)S(1)}, bf16[512,256]{1,0:T(8,128)(2,1)S(1)}, u32[]{:S(2)}, u32[]{:S(2)}) collective-permute-start(bf16[512,256]{1,0:T(8,128)(2,1)S(1)} %add_convert_fusion.17), channel_id=1, source_target_pairs={{0,8},{8,16},{16,24},{24,0},{1,9},{9,17},{17,25},{25,1},{2,10},{10... | collective-permute-start | bytes 786440 | tf_op jit(solution)/shard_map/ppermute | solution.py:1428
  1127.0 19.7 %collective-permute-done.64 = bf16[512,256]{1,0:T(8,128)(2,1)S(1)} collective-permute-done((bf16[512,256]{1,0:T(8,128)(2,1)S(1)}, bf16[512,256]{1,0:T(8,128)(2,1)S(1)}, u32[]{:S(2)}, u32[]{:S(2)}) %collective-permute-start.64) | collective-permute-done | bytes 262176 | tf_op jit(solution)/shard_map/ppermute | solution.py:1428
  1150.6 30.3 %collective-permute-done.66 = bf16[2048,256]{1,0:T(8,128)(2,1)} collective-permute-done((bf16[2048,256]{1,0:T(8,128)(2,1)}, bf16[2048,256]{1,0:T(8,128)(2,1)}, u32[]{:S(2)}, u32[]{:S(2)}) %collective-permute-start.66) | collective-permute-done | bytes 1048608 | tf_op jit(solution)/shard_map/ppermute | solution.py:1265
  1183.0 123.1 %all-reduce.6.cloned.1.call-done = (bf16[4096,256]{1,0:T(8,128)(2,1)}, bf16[1024,1024]{1,0:T(8,128)(2,1)}, bf16[1024,1024]{1,0:T(8,128)(2,1)}) async-done(((bf16[4096,256]{1,0:T(8,128)(2,1)}, bf16[1024,1024]{1,0:T(8,128)(2,1)}, bf16[1024,1024]{1,0:T(8,128)(2,1)}), (bf16[4096,256]{1,0:T(8,128)(2,1)}, bf16[1024,1024]{1,0:T(8,128)(2,1)}, bf16[1024,1024]{1,0:T(8,128)(2,1)})) %all-reduce.6.cloned.1.call-update) | async-done | bytes 6291472 | tf_op jit(solution)/shard_map/psum | solution.py:1536
  1307.6 13.1 modulation_back.1
  (631 shorter events, 592.8 us)
Async XLA Ops:
  7.2 943.4 %all-reduce.8.cloned.1.call-start = ((), (), s32[]{:S(2)}) async-start(), calls=%async_computation.1 | async-start | bytes 8388608 | tf_op jit(solution)/shard_map/psum | solution.py:1550
  59.6 47.3 %collective-permute-start.15 = (bf16[512,1024]{1,0:T(8,128)(2,1)S(1)}, bf16[512,1024]{1,0:T(8,128)(2,1)}, u32[]{:S(2)}, u32[]{:S(2)}) collective-permute-start(bf16[512,1024]{1,0:T(8,128)(2,1)S(1)} %dynamic-slice_bitcast_fusion.3), channel_id=1, source_target_pairs={{0,1},{1,0},{2,3},{3,2},{4,5},{5,4},{6,7},{7,6},{8,9},{9,8},{10,11... | collective-permute-start | bytes 3145736 | tf_op jit(solution)/shard_map/ppermute | solution.py:1236
  62.9 50.2 %collective-permute-start.9 = (bf16[1024,512]{1,0:T(8,128)(2,1)}, bf16[1024,512]{1,0:T(8,128)(2,1)S(1)}, u32[]{:S(2)}, u32[]{:S(2)}) collective-permute-start(bf16[1024,512]{1,0:T(8,128)(2,1)} %dynamic-slice_bitcast_fusion.6), channel_id=1, source_target_pairs={{0,1},{1,0},{2,3},{3,2},{4,5},{5,4},{6,7},{7,6},{8,9},{9,8},{10,11... | collective-permute-start | bytes 3145736 | tf_op jit(solution)/shard_map/ppermute | solution.py:1236
  113.1 41.8 %collective-permute-start.10 = (bf16[1024,512]{1,0:T(8,128)(2,1)S(1)}, bf16[1024,512]{1,0:T(8,128)(2,1)S(1)}, u32[]{:S(2)}, u32[]{:S(2)}) collective-permute-start(bf16[1024,512]{1,0:T(8,128)(2,1)S(1)} %collective-permute-done.9), channel_id=1, source_target_pairs={{0,4},{4,0},{1,5},{5,1},{2,6},{6,2},{3,7},{7,3},{8,12},{12,8},{9,1... | collective-permute-start | bytes 3145736 | tf_op jit(solution)/shard_map/ppermute | solution.py:1265
  157.7 40.5 %collective-permute-start.11 = (bf16[1024,1024]{1,0:T(8,128)(2,1)}, bf16[1024,1024]{1,0:T(8,128)(2,1)S(1)}, u32[]{:S(2)}, u32[]{:S(2)}) collective-permute-start(bf16[1024,1024]{1,0:T(8,128)(2,1)} %get-tuple-element.412), channel_id=1, source_target_pairs={{0,2},{2,0},{1,3},{3,1},{4,6},{6,4},{5,7},{7,5},{8,10},{10,8},{9,1... | collective-permute-start | bytes 6291464 | tf_op jit(solution)/shard_map/ppermute | solution.py:1239
  160.4 68.8 %collective-permute-start.17 = (bf16[1024,1024]{1,0:T(8,128)(2,1)}, bf16[1024,1024]{1,0:T(8,128)(2,1)}, u32[]{:S(2)}, u32[]{:S(2)}) collective-permute-start(bf16[1024,1024]{1,0:T(8,128)(2,1)} %get-tuple-element.401.w2_ref), channel_id=1, source_target_pairs={{0,2},{2,0},{1,3},{3,1},{4,6},{6,4},{5,7},{7,5},{8,10},{10,8},{9,1... | collective-permute-start | bytes 6291464 | tf_op jit(solution)/shard_map/ppermute | solution.py:1239
  164.0 65.2 %collective-permute-start.13 = (bf16[1024,512]{1,0:T(8,128)(2,1)}, bf16[1024,512]{1,0:T(8,128)(2,1)}, u32[]{:S(2)}, u32[]{:S(2)}) collective-permute-start(bf16[1024,512]{1,0:T(8,128)(2,1)} %dynamic-slice_bitcast_fusion.5), channel_id=1, source_target_pairs={{0,1},{1,0},{2,3},{3,2},{4,5},{5,4},{6,7},{7,6},{8,9},{9,8},{10,11... | collective-permute-start | bytes 3145736 | tf_op jit(solution)/shard_map/ppermute | solution.py:1236
  167.3 62.0 %collective-permute-start.14 = (bf16[512,1024]{1,0:T(8,128)(2,1)}, bf16[512,1024]{1,0:T(8,128)(2,1)}, u32[]{:S(2)}, u32[]{:S(2)}) collective-permute-start(bf16[512,1024]{1,0:T(8,128)(2,1)} %dynamic-slice_bitcast_fusion.4), channel_id=1, source_target_pairs={{0,1},{1,0},{2,3},{3,2},{4,5},{5,4},{6,7},{7,6},{8,9},{9,8},{10,11... | collective-permute-start | bytes 3145736 | tf_op jit(solution)/shard_map/ppermute | solution.py:1236
  169.2 60.1 %collective-permute-start.12 = (bf16[3,1024,128]{2,1,0:T(8,128)(2,1)}, bf16[3,1024,128]{2,1,0:T(8,128)(2,1)}, u32[]{:S(2)}, u32[]{:S(2)}) collective-permute-start(bf16[3,1024,128]{2,1,0:T(8,128)(2,1)} %dynamic-slice_bitcast_fusion.7), channel_id=1, source_target_pairs={{0,1},{1,0},{2,3},{3,2},{4,5},{5,4},{6,7},{7,6},{8,9},{9,8},{10,11... | collective-permute-start | bytes 2359304 | tf_op jit(solution)/shard_map/ppermute | solution.py:1236
  255.6 46.3 %collective-permute-start.22 = (bf16[1024,512]{1,0:T(8,128)(2,1)}, bf16[1024,512]{1,0:T(8,128)(2,1)S(1)}, u32[]{:S(2)}, u32[]{:S(2)}) collective-permute-start(bf16[1024,512]{1,0:T(8,128)(2,1)} %collective-permute-done.13), channel_id=1, source_target_pairs={{0,4},{4,0},{1,5},{5,1},{2,6},{6,2},{3,7},{7,3},{8,12},{12,8},{9,1... | collective-permute-start | bytes 3145736 | tf_op jit(solution)/shard_map/ppermute | solution.py:1265
  257.9 59.0 %collective-permute-start.24 = (bf16[512,1024]{1,0:T(8,128)(2,1)}, bf16[512,1024]{1,0:T(8,128)(2,1)}, u32[]{:S(2)}, u32[]{:S(2)}) collective-permute-start(bf16[512,1024]{1,0:T(8,128)(2,1)} %collective-permute-done.14), channel_id=1, source_target_pairs={{0,4},{4,0},{1,5},{5,1},{2,6},{6,2},{3,7},{7,3},{8,12},{12,8},{9,1... | collective-permute-start | bytes 3145736 | tf_op jit(solution)/shard_map/ppermute | solution.py:1265
  290.1 45.8 %collective-permute-start.20 = (bf16[3,1024,256]{2,1,0:T(8,128)(2,1)}, bf16[3,1024,256]{2,1,0:T(8,128)(2,1)S(1)}, u32[]{:S(2)}, u32[]{:S(2)}) collective-permute-start(bf16[3,1024,256]{2,1,0:T(8,128)(2,1)} %get-tuple-element.420), channel_id=1, source_target_pairs={{0,2},{2,0},{1,3},{3,1},{4,6},{6,4},{5,7},{7,5},{8,10},{10,8},{9,1... | collective-permute-start | bytes 4718600 | tf_op jit(solution)/shard_map/ppermute | solution.py:1239
  305.8 91.5 %collective-permute-start.23 = (bf16[1024,1024]{1,0:T(8,128)(2,1)}, bf16[1024,1024]{1,0:T(8,128)(2,1)S(1)}, u32[]{:S(2)}, u32[]{:S(2)}) collective-permute-start(bf16[1024,1024]{1,0:T(8,128)(2,1)} %get-tuple-element.406), channel_id=1, source_target_pairs={{0,2},{2,0},{1,3},{3,1},{4,6},{6,4},{5,7},{7,5},{8,10},{10,8},{9,1... | collective-permute-start | bytes 6291464 | tf_op jit(solution)/shard_map/ppermute | solution.py:1239
  321.2 89.6 %collective-permute-start.25 = (bf16[1024,1024]{1,0:T(8,128)(2,1)}, bf16[1024,1024]{1,0:T(8,128)(2,1)}, u32[]{:S(2)}, u32[]{:S(2)}) collective-permute-start(bf16[1024,1024]{1,0:T(8,128)(2,1)} %get-tuple-element.403.w2_ref), channel_id=1, source_target_pairs={{0,2},{2,0},{1,3},{3,1},{4,6},{6,4},{5,7},{7,5},{8,10},{10,8},{9,1... | collective-permute-start | bytes 6291464 | tf_op jit(solution)/shard_map/ppermute | solution.py:1239
  358.3 49.6 %collective-permute-start.26 = (bf16[2,256,1024]{2,1,0:T(8,128)(2,1)S(1)}, bf16[2,256,1024]{2,1,0:T(8,128)(2,1)S(1)}, u32[]{:S(2)}, u32[]{:S(2)}) collective-permute-start(bf16[2,256,1024]{2,1,0:T(8,128)(2,1)S(1)} %pad_maximum_fusion.17), channel_id=1, source_target_pairs={{0,1},{1,0},{2,3},{3,2},{4,5},{5,4},{6,7},{7,6},{8,9},{9,8},{10,11... | collective-permute-start | bytes 3145736 | tf_op jit(solution)/shard_map/ppermute | solution.py:1236
  488.0 68.2 %collective-permute-start.31 = (bf16[1024,1024]{1,0:T(8,128)(2,1)S(1)}, bf16[1024,1024]{1,0:T(8,128)(2,1)}, u32[]{:S(2)}, u32[]{:S(2)}) collective-permute-start(bf16[1024,1024]{1,0:T(8,128)(2,1)S(1)} %add_convert_fusion.7), channel_id=1, source_target_pairs={{0,1},{1,0},{2,3},{3,2},{4,5},{5,4},{6,7},{7,6},{8,9},{9,8},{10,11... | collective-permute-start | bytes 6291464 | tf_op jit(solution)/shard_map/ppermute | solution.py:1236
  514.3 41.9 %collective-permute-start.30 = (bf16[1024,1024]{1,0:T(8,128)(2,1)}, bf16[1024,1024]{1,0:T(8,128)(2,1)}, u32[]{:S(2)}, u32[]{:S(2)}) collective-permute-start(bf16[1024,1024]{1,0:T(8,128)(2,1)} %get-tuple-element.232), channel_id=1, source_target_pairs={{0,2},{2,0},{1,3},{3,1},{4,6},{6,4},{5,7},{7,5},{8,10},{10,8},{9,1... | collective-permute-start | bytes 6291464 | tf_op jit(solution)/shard_map/ppermute | solution.py:1239
  592.4 48.5 %collective-permute-start.35 = (bf16[1024,1024]{1,0:T(8,128)(2,1)S(1)}, bf16[1024,1024]{1,0:T(8,128)(2,1)}, u32[]{:S(2)}, u32[]{:S(2)}) collective-permute-start(bf16[1024,1024]{1,0:T(8,128)(2,1)S(1)} %add_convert_fusion.6), channel_id=1, source_target_pairs={{0,1},{1,0},{2,3},{3,2},{4,5},{5,4},{6,7},{7,6},{8,9},{9,8},{10,11... | collective-permute-start | bytes 6291464 | tf_op jit(solution)/shard_map/ppermute | solution.py:1236
  617.3 68.1 %collective-permute-start.36 = (bf16[3,1024,256]{2,1,0:T(8,128)(2,1)}, bf16[3,1024,256]{2,1,0:T(8,128)(2,1)S(1)}, u32[]{:S(2)}, u32[]{:S(2)}) collective-permute-start(bf16[3,1024,256]{2,1,0:T(8,128)(2,1)} %add_convert_fusion.11), channel_id=1, source_target_pairs={{0,1},{1,0},{2,3},{3,2},{4,5},{5,4},{6,7},{7,6},{8,9},{9,8},{10,11... | collective-permute-start | bytes 4718600 | tf_op jit(solution)/shard_map/ppermute | solution.py:1236
  772.1 74.8 %collective-permute-start.44 = (bf16[1024,1024]{1,0:T(8,128)(2,1)}, bf16[1024,1024]{1,0:T(8,128)(2,1)}, u32[]{:S(2)}, u32[]{:S(2)}) collective-permute-start(bf16[1024,1024]{1,0:T(8,128)(2,1)} %add_convert_fusion.3), channel_id=1, source_target_pairs={{0,1},{1,0},{2,3},{3,2},{4,5},{5,4},{6,7},{7,6},{8,9},{9,8},{10,11... | collective-permute-start | bytes 6291464 | tf_op jit(solution)/shard_map/ppermute | solution.py:1236
  795.9 52.3 %collective-permute-start.43 = (bf16[1024,1024]{1,0:T(8,128)(2,1)}, bf16[1024,1024]{1,0:T(8,128)(2,1)}, u32[]{:S(2)}, u32[]{:S(2)}) collective-permute-start(bf16[1024,1024]{1,0:T(8,128)(2,1)} %get-tuple-element.273), channel_id=1, source_target_pairs={{0,2},{2,0},{1,3},{3,1},{4,6},{6,4},{5,7},{7,5},{8,10},{10,8},{9,1... | collective-permute-start | bytes 6291464 | tf_op jit(solution)/shard_map/ppermute | solution.py:1239
  796.0 510.1 %all-reduce.6.cloned.1.call-start = ((), (), s32[]{:S(2)}) async-start(), calls=%async_computation | async-start | bytes 12582912 | tf_op jit(solution)/shard_map/psum | solution.py:1536
  804.0 97.5 %collective-permute-start.47 = (bf16[1024,1024]{1,0:T(8,128)(2,1)}, bf16[1024,1024]{1,0:T(8,128)(2,1)}, u32[]{:S(2)}, u32[]{:S(2)}) collective-permute-start(bf16[1024,1024]{1,0:T(8,128)(2,1)} %get-tuple-element.291), channel_id=1, source_target_pairs={{0,2},{2,0},{1,3},{3,1},{4,6},{6,4},{5,7},{7,5},{8,10},{10,8},{9,1... | collective-permute-start | bytes 6291464 | tf_op jit(solution)/shard_map/ppermute | solution.py:1239
  846.9 54.7 %collective-permute-start.48 = (bf16[1024,1024]{1,0:T(8,128)(2,1)}, bf16[1024,1024]{1,0:T(8,128)(2,1)}, u32[]{:S(2)}, u32[]{:S(2)}) collective-permute-start(bf16[1024,1024]{1,0:T(8,128)(2,1)} %add_convert_fusion.2), channel_id=1, source_target_pairs={{0,1},{1,0},{2,3},{3,2},{4,5},{5,4},{6,7},{7,6},{8,9},{9,8},{10,11... | collective-permute-start | bytes 6291464 | tf_op jit(solution)/shard_map/ppermute | solution.py:1236
  900.6 95.8 %collective-permute-start.50 = (bf16[3,1024,256]{2,1,0:T(8,128)(2,1)}, bf16[3,1024,256]{2,1,0:T(8,128)(2,1)}, u32[]{:S(2)}, u32[]{:S(2)}) collective-permute-start(bf16[3,1024,256]{2,1,0:T(8,128)(2,1)} %add_convert_fusion.9), channel_id=1, source_target_pairs={{0,1},{1,0},{2,3},{3,2},{4,5},{5,4},{6,7},{7,6},{8,9},{9,8},{10,11... | collective-permute-start | bytes 4718600 | tf_op jit(solution)/shard_map/ppermute | solution.py:1236
  960.7 35.7 %collective-permute-start.49 = (bf16[3,1024,256]{2,1,0:T(8,128)(2,1)}, bf16[3,1024,256]{2,1,0:T(8,128)(2,1)}, u32[]{:S(2)}, u32[]{:S(2)}) collective-permute-start(bf16[3,1024,256]{2,1,0:T(8,128)(2,1)} %get-tuple-element.298), channel_id=1, source_target_pairs={{0,2},{2,0},{1,3},{3,1},{4,6},{6,4},{5,7},{7,5},{8,10},{10,8},{9,1... | collective-permute-start | bytes 4718600 | tf_op jit(solution)/shard_map/ppermute | solution.py:1239
  1024.5 36.8 %collective-permute-start.59 = (bf16[2048,256]{1,0:T(8,128)(2,1)S(1)}, bf16[2048,256]{1,0:T(8,128)(2,1)S(1)}, u32[]{:S(2)}, u32[]{:S(2)}) collective-permute-start(bf16[2048,256]{1,0:T(8,128)(2,1)S(1)} %copy-done.45), channel_id=1, source_target_pairs={{0,4},{4,0},{1,5},{5,1},{2,6},{6,2},{3,7},{7,3},{8,12},{12,8},{9,1... | collective-permute-start | bytes 3145736 | tf_op jit(solution)/shard_map/ppermute | solution.py:1265
  1026.3 39.7 %collective-permute-start.53 = (f32[8,16,1024]{2,1,0:T(8,128)S(1)}, f32[8,16,1024]{2,1,0:T(8,128)S(1)}, u32[]{:S(2)}, u32[]{:S(2)}) collective-permute-start(f32[8,16,1024]{2,1,0:T(8,128)S(1)} %bitcast.374), channel_id=1, source_target_pairs={{0,1},{1,0},{2,3},{3,2},{4,5},{5,4},{6,7},{7,6},{8,9},{9,8},{10,11... | collective-permute-start | bytes 1572872 | tf_op jit(solution)/shard_map/ppermute | solution.py:1236
  1028.1 119.9 %collective-permute-start.58 = (f32[8,12072]{1,0:T(8,128)S(1)}, f32[8,12072]{1,0:T(8,128)S(1)}, u32[]{:S(2)}, u32[]{:S(2)}) collective-permute-start(f32[8,12072]{1,0:T(8,128)S(1)} %pad_maximum_fusion.21), channel_id=1, source_target_pairs={{0,16},{4,20},{8,24},{12,28},{16,0},{20,4},{24,8},{28,12},{1,17},{... | collective-permute-start | bytes 1158920 | tf_op jit(solution)/shard_map/ppermute | solution.py:1256
  1062.4 35.8 %collective-permute-start.61 = (bf16[512,256]{1,0:T(8,128)(2,1)S(1)}, bf16[512,256]{1,0:T(8,128)(2,1)S(1)}, u32[]{:S(2)}, u32[]{:S(2)}) collective-permute-start(bf16[512,256]{1,0:T(8,128)(2,1)S(1)} %get-tuple-element.428), channel_id=1, source_target_pairs={{0,16},{8,24},{16,0},{24,8},{1,17},{9,25},{17,1},{25,9},{2,18},{10... | collective-permute-start | bytes 786440 | tf_op jit(solution)/shard_map/ppermute | solution.py:1428
  1150.5 173.3 %collective-permute-start.67 = (bf16[2048,256]{1,0:T(8,128)(2,1)}, bf16[2048,256]{1,0:T(8,128)(2,1)}, u32[]{:S(2)}, u32[]{:S(2)}) collective-permute-start(bf16[2048,256]{1,0:T(8,128)(2,1)} %bitcast.143), channel_id=1, source_target_pairs={{0,2},{2,0},{1,3},{3,1},{4,6},{6,4},{5,7},{7,5},{8,10},{10,8},{9,1... | collective-permute-start | bytes 3145736 | tf_op jit(solution)/shard_map/ppermute | solution.py:1239
  1180.8 142.9 %collective-permute-start.68 = (bf16[2048,256]{1,0:T(8,128)(2,1)}, bf16[2048,256]{1,0:T(8,128)(2,1)}, u32[]{:S(2)}, u32[]{:S(2)}) collective-permute-start(bf16[2048,256]{1,0:T(8,128)(2,1)} %collective-permute-done.66), channel_id=1, source_target_pairs={{0,2},{2,0},{1,3},{3,1},{4,6},{6,4},{5,7},{7,5},{8,10},{10,8},{9,1... | collective-permute-start | bytes 3145736 | tf_op jit(solution)/shard_map/ppermute | solution.py:1239
  (153 other events, 2045.2 us)
Sparse Core Ops, SparseCore 0:
  796.1 154.4 all-reduce.7
  1020.5 285.5 all-reduce.5
